TPU v7x, 32 devices: a whole 2x2x4 slice. The times are simulated.
32 devices in a mesh: replica: 2 (over x), fsdp: 16 (over z, y, core).
Axes of the slice: x: 2, y: 2, z: 4, core: 2. Of those that a mesh axis runs over, the one named last changes fastest.
Arguments:
- tokens: bfloat16 [4096, 2048], P(('replica', 'fsdp')), may hold values from -6 to 6
- w_qkv: bfloat16 [2048, 6144], P('fsdp'), may hold values from -0.125 to 0.125
- w_out: bfloat16 [2048, 2048], P('fsdp'), may hold values from -0.125 to 0.125
- w_gate_up: bfloat16 [2048, 16384], P('fsdp'), may hold values from -0.125 to 0.125
- w_down_t: bfloat16 [2048, 8192], P('fsdp'), may hold values from -0.0625 to 0.0625
- gains: bfloat16 [2048, 4], P('fsdp'), may hold values from 0.25 to 1.75
- starts: int32 [4096], P(('replica', 'fsdp')), may hold values from 0 to 1, as said below
- cotangent: bfloat16 [4096, 2048], P(('replica', 'fsdp')), may hold values from -6 to 6
Outputs:
- mixed: bfloat16 [4096, 2048], P(('replica', 'fsdp'))
- grad_tokens: float32 [4096, 2048], P(('replica', 'fsdp'))
- grad_qkv: float32 [2048, 6144], P('fsdp')
- grad_out: float32 [2048, 2048], P('fsdp')
- grad_gate_up: float32 [2048, 16384], P('fsdp')
- grad_down_t: float32 [2048, 8192], P('fsdp')
- grad_gains: float32 [2048, 4], P('fsdp')
Inputs may be any that keep to these rules, and one draw needn't show every extreme that they name: `starts`: the first row of each block of 128 rows is 1, so sequences lie whole on a device; in some block no other row is 1, so one sequence fills all 128 rows.
All inputs are finite; a program needn't handle non-finite values.
Results may differ from a plain program's by a relative error of at most 0.017.
Values may be sent and summed in bfloat16 or wider, within the bound.
A program may use at most 1 GiB of HBM per device.

v0:
```python
import math

import jax
import jax.numpy as jnp
from jax import lax
from jax.sharding import PartitionSpec as P

HD = 128


epsilon = 1e-06
theta_base = 500000.0


def normalize(values, scales):
    inverse = lax.rsqrt(jnp.mean(values * values, axis=-1, keepdims=True) + epsilon)
    return (values * inverse * scales, inverse)


def norm_back(upstream, values, inverse, scales):
    unit_rows = values * inverse
    scaled = upstream * scales
    value_grad = inverse * (
        scaled - unit_rows * jnp.mean(scaled * unit_rows, axis=-1, keepdims=True)
    )
    return (value_grad, jnp.sum(upstream * unit_rows, axis=0))


def rope_tables(positions):
    frequency = theta_base ** (-2.0 * jnp.arange(HD // 2).astype(jnp.float32) / HD)
    angles = positions[:, None] * frequency[None, :]
    return (jnp.cos(angles)[:, None, :], jnp.sin(angles)[:, None, :])


def rotate(values, cos_table, sin_table):
    half_width = values.shape[-1] // 2
    former = values[..., :half_width]
    latter = values[..., half_width:]
    return jnp.concatenate(
        [former * cos_table - latter * sin_table, latter * cos_table + former * sin_table], axis=-1
    )


def contract_last(operand, matrix):
    return lax.dot_general(
        operand, matrix, (((1,), (1,)), ((), ())), preferred_element_type=jnp.float32
    )


def masked_scores(query_bf, key_bf, allowed, score_scale):
    scores = (
        jnp.einsum("qhd,khd->hqk", query_bf, key_bf, preferred_element_type=jnp.float32)
        * score_scale
    )
    return jnp.where(allowed[None, :, :], scores, -1e30)


def terms_of(lefts, rights):
    pieces = [
        lax.dot_general(
            left_part, right_part, (((0,), (0,)), ((), ())), preferred_element_type=jnp.float32
        )
        for left_part, right_part in zip(lefts, rights)
    ]
    return jnp.concatenate(pieces, axis=1)


def shards(tokens, w_qkv, w_out, w_gate_up, w_down_t, gains, starts, cotangent):
    count_rows, width = tokens.shape
    hidden_width = w_down_t.shape[1]
    head_count = width // HD
    score_scale = 1.0 / math.sqrt(HD)
    local_rows = jnp.arange(count_rows, dtype=jnp.int32)
    seq_begin = lax.cummax(jnp.where(starts == 1, local_rows, 0), axis=0)
    positions = (local_rows - seq_begin).astype(jnp.float32)
    cos_table, sin_table = rope_tables(positions)
    allowed = (local_rows[None, :] <= local_rows[:, None]) & (
        local_rows[None, :] >= seq_begin[:, None]
    )
    gathered = (
        lax.all_gather(w_qkv, "fsdp", axis=0, tiled=True),
        lax.all_gather(w_out, "fsdp", axis=0, tiled=True),
        lax.all_gather(w_gate_up, "fsdp", axis=0, tiled=True),
        lax.all_gather(w_down_t, "fsdp", axis=0, tiled=True),
        lax.all_gather(gains, "fsdp", axis=0, tiled=True),
    )
    full_qkv, full_out, full_gate_up, full_down, full_gains = gathered
    gain_cols = full_gains.astype(jnp.float32)
    projected = jnp.dot(tokens, full_qkv, preferred_element_type=jnp.float32)
    query_raw = projected[:, :width]
    key_raw = projected[:, width : 2 * width]
    value_bf = projected[:, 2 * width :].astype(jnp.bfloat16).reshape(count_rows, head_count, HD)
    query_norm, query_inv = normalize(query_raw, gain_cols[:, 0])
    key_norm, key_inv = normalize(key_raw, gain_cols[:, 1])
    query_bf = rotate(query_norm.reshape(count_rows, head_count, HD), cos_table, sin_table).astype(
        jnp.bfloat16
    )
    key_bf = rotate(key_norm.reshape(count_rows, head_count, HD), cos_table, sin_table).astype(
        jnp.bfloat16
    )
    scores = masked_scores(query_bf, key_bf, allowed, score_scale)
    peaks = jnp.max(scores, axis=-1, keepdims=True)
    exponent = jnp.exp(scores - peaks)
    row_totals = jnp.sum(exponent, axis=-1, keepdims=True)
    log_total = peaks + jnp.log(row_totals)
    attention = (exponent / row_totals).astype(jnp.bfloat16)
    attended = (
        jnp.einsum("hqk,khd->qhd", attention, value_bf, preferred_element_type=jnp.float32)
        .reshape(count_rows, width)
        .astype(jnp.bfloat16)
    )
    branch = jnp.dot(attended, full_out, preferred_element_type=jnp.float32)
    branch_norm, branch_inv = normalize(branch, gain_cols[:, 2])
    middle = tokens.astype(jnp.float32) + branch_norm
    middle_bf = middle.astype(jnp.bfloat16)
    gate_up = jnp.dot(middle_bf, full_gate_up, preferred_element_type=jnp.float32)
    gate_part = gate_up[:, :hidden_width]
    up_part = gate_up[:, hidden_width:]
    sigmoid_gate = jax.nn.sigmoid(gate_part)
    hidden_bf = (gate_part * sigmoid_gate * up_part).astype(jnp.bfloat16)
    feed_out = contract_last(hidden_bf, full_down)
    feed_norm, feed_inv = normalize(feed_out, gain_cols[:, 3])
    mixed = (middle + feed_norm).astype(jnp.bfloat16)
    again = (full_qkv, full_out, full_gate_up, full_down)
    back_qkv, back_out, back_gate_up, back_down = again
    upstream = cotangent.astype(jnp.float32)
    feed_grad, gain_feed = norm_back(upstream, feed_out, feed_inv, gain_cols[:, 3])
    feed_bf = feed_grad.astype(jnp.bfloat16)
    hidden_grad = jnp.dot(feed_bf, back_down, preferred_element_type=jnp.float32)
    gate_grad = hidden_grad * up_part * sigmoid_gate * (1.0 + gate_part * (1.0 - sigmoid_gate))
    up_grad = hidden_grad * gate_part * sigmoid_gate
    gate_up_bf = jnp.concatenate([gate_grad, up_grad], axis=1).astype(jnp.bfloat16)
    middle_grad = upstream + contract_last(gate_up_bf, back_gate_up)
    branch_grad, gain_branch = norm_back(middle_grad, branch, branch_inv, gain_cols[:, 2])
    branch_bf = branch_grad.astype(jnp.bfloat16)
    attended_grad = (
        contract_last(branch_bf, back_out).astype(jnp.bfloat16).reshape(count_rows, head_count, HD)
    )
    scores_again = masked_scores(query_bf, key_bf, allowed, score_scale)
    attention_again = jnp.exp(scores_again - log_total)
    prob_grad = jnp.einsum(
        "qhd,khd->hqk", attended_grad, value_bf, preferred_element_type=jnp.float32
    )
    score_bf = (
        attention_again * (prob_grad - jnp.sum(attention_again * prob_grad, axis=-1, keepdims=True))
    ).astype(jnp.bfloat16)
    value_grad = jnp.einsum(
        "hqk,qhd->khd",
        attention_again.astype(jnp.bfloat16),
        attended_grad,
        preferred_element_type=jnp.float32,
    )
    query_grad = (
        jnp.einsum("hqk,khd->qhd", score_bf, key_bf, preferred_element_type=jnp.float32)
        * score_scale
    )
    key_grad = (
        jnp.einsum("hqk,qhd->khd", score_bf, query_bf, preferred_element_type=jnp.float32)
        * score_scale
    )
    query_grad = rotate(query_grad, cos_table, -sin_table).reshape(count_rows, width)
    key_grad = rotate(key_grad, cos_table, -sin_table).reshape(count_rows, width)
    query_raw_grad, gain_query = norm_back(query_grad, query_raw, query_inv, gain_cols[:, 0])
    key_raw_grad, gain_key = norm_back(key_grad, key_raw, key_inv, gain_cols[:, 1])
    projected_bf = jnp.concatenate(
        [query_raw_grad, key_raw_grad, value_grad.reshape(count_rows, width)], axis=1
    ).astype(jnp.bfloat16)
    grad_tokens = middle_grad + contract_last(projected_bf, back_qkv)
    gain_terms = jnp.stack([gain_query, gain_key, gain_branch, gain_feed], axis=1)
    lefts = (tokens, attended, middle_bf, feed_bf)
    rights = (projected_bf, branch_bf, gate_up_bf, hidden_bf)
    rows_part = lax.psum_scatter(terms_of(lefts, rights), "fsdp", scatter_dimension=0, tiled=True)
    gain_part = lax.psum_scatter(gain_terms, "fsdp", scatter_dimension=0, tiled=True)
    rows_part, gain_part = (
        lax.psum(rows_part.astype(jnp.bfloat16), "replica").astype(jnp.float32),
        lax.psum(gain_part.astype(jnp.bfloat16), "replica").astype(jnp.float32),
    )
    first_cut = 3 * width
    second_cut = first_cut + width
    third_cut = second_cut + 2 * hidden_width
    return (
        mixed,
        grad_tokens,
        rows_part[:, :first_cut],
        rows_part[:, first_cut:second_cut],
        rows_part[:, second_cut:third_cut],
        rows_part[:, third_cut:],
        gain_part,
    )


def solution(mesh):
    return jax.shard_map(
        shards,
        mesh=mesh,
        in_specs=(
            P(("replica", "fsdp"), None),
            P("fsdp", None),
            P("fsdp", None),
            P("fsdp", None),
            P("fsdp", None),
            P("fsdp", None),
            P(("replica", "fsdp")),
            P(("replica", "fsdp"), None),
        ),
        out_specs=(
            P(("replica", "fsdp"), None),
            P(("replica", "fsdp"), None),
            P("fsdp", None),
            P("fsdp", None),
            P("fsdp", None),
            P("fsdp", None),
            P("fsdp", None),
        ),
        check_vma=False,
    )
```

profile of v0, /device:TPU:0, one launch (start us, length us, event | category | flops | bytes accessed | tf_op | source)
XLA Modules:
  0.0 3871.3 jit_solution(17141726346886332851)
XLA Ops:
  7.2 0.7 all-gather.5.cloned.1.call-update
  8.0 0.7 all-gather.7.cloned.1.call-update
  8.7 0.7 all-gather.9.cloned.1.call-update
  9.5 0.5 all-gather.11.cloned.1.call-update
  10.5 23.1 all_gather.16
  33.6 0.9 fusion.28
  34.6 106.4 %all-gather.5.cloned.1.call-done = bf16[2048,6144]{1,0:T(8,128)(2,1)} async-done(((bf16[128,6144]{1,0:T(8,128)(2,1)}), bf16[2048,6144]{1,0:T(8,128)(2,1)}) %all-gather.5.cloned.1.call-update) | async-done | bytes 25165840 | tf_op jit(solution)/shard_map/all_gather | solution.py:81
  141.0 10.1 fusion.41
  151.4 0.2 multiply_bitcast_fusion.1
  151.6 0.2 copy-done.34
  152.3 0.3 fusion.38
  152.6 0.3 fusion.37
  153.0 1.4 subtract_convert_fusion.1
  154.4 0.8 copy-done.7
  155.1 0.8 fusion.40
  156.1 0.8 copy-done
  156.9 1.2 convolution_convert_fusion.2
  158.1 60.0 %all-gather.7.cloned.1.call-done = bf16[2048,2048]{1,0:T(8,128)(2,1)} async-done(((bf16[128,2048]{1,0:T(8,128)(2,1)}), bf16[2048,2048]{1,0:T(8,128)(2,1)}) %all-gather.7.cloned.1.call-update) | async-done | bytes 8388624 | tf_op jit(solution)/shard_map/all_gather | solution.py:82
  218.1 5.0 multiply_reduce_fusion.6
  223.1 0.9 copy-done.3
  224.0 1.0 fusion.16
  225.1 319.0 %all-gather.9.cloned.1.call-done = bf16[2048,16384]{1,0:T(8,128)(2,1)} async-done(((bf16[128,16384]{1,0:T(8,128)(2,1)}), bf16[2048,16384]{1,0:T(8,128)(2,1)}) %all-gather.9.cloned.1.call-update) | async-done | bytes 67108880 | tf_op jit(solution)/shard_map/all_gather | solution.py:83
  544.1 29.4 fusion.42
  573.5 6.0 multiply_convert_fusion.2
  579.5 134.2 %all-gather.11.cloned.1.call-done = bf16[2048,8192]{1,0:T(8,128)(2,1)} async-done(((bf16[128,8192]{1,0:T(8,128)(2,1)}), bf16[2048,8192]{1,0:T(8,128)(2,1)}) %all-gather.11.cloned.1.call-update) | async-done | bytes 33554448 | tf_op jit(solution)/shard_map/all_gather | solution.py:84
  713.6 16.5 multiply_reduce_fusion.5
  730.2 0.9 fusion.11
  731.1 1.1 fusion.10
  732.2 18.5 multiply_convert_fusion.1
  750.7 31.4 multiply_reduce_fusion
  782.0 3.3 multiply_convert_fusion.6
  785.3 0.8 copy-done.15
  786.1 7.1 convolution_convert_fusion
  793.2 2.0 copy.97
  795.3 2.8 convolution_convert_fusion.1
  798.1 1.8 multiply_reduce_fusion.3
  799.9 0.2 multiply_convert_fusion.5
  800.2 1.4 fusion.3
  801.6 1.5 fusion.4
  803.2 8.1 fusion.43
  811.2 23.1 fusion.44
  834.3 47.3 %fusion = f32[2048,16384]{1,0:T(8,128)} fusion(bf16[128,2048]{1,0:T(8,128)(2,1)} %fusion.16, bf16[128,8192]{1,0:T(8,128)(2,1)} %get-tuple-element.20, bf16[128,8192]{1,0:T(8,128)(2,1)} %get-tuple-element.19), kind=kOutput, calls=%fused_computation.7 | convolution fusion | flops 8598323200 | bytes 138936320 | tf_op jit(solution)/shard_map/dot_general | solution.py:60
  881.7 2.0 copy.90
  883.7 2.9 multiply_subtract_fusion.1
  886.7 1.4 fusion.13
  888.1 1.9 multiply_convert_fusion.4
  890.0 20.8 convolution_bitcast_fusion
  910.7 48.8 %copy.79 = f32[2048,6144]{1,0:T(8,128)} copy(f32[2048,6144]{0,1:T(8,128)} %convolution_bitcast_fusion) | data formatting | bytes 100663296 | tf_op jit(solution)/shard_map/dot_general | solution.py:60
  959.6 169.8 %pad_maximum_fusion = f32[2048,32768]{1,0:T(8,128)} fusion(f32[2048,8192]{1,0:T(8,128)} %fusion.44, f32[2048,16384]{1,0:T(8,128)} %fusion, f32[2048,2048]{1,0:T(8,128)} %fusion.43, f32[2048,6144]{1,0:T(8,128)} %copy.79), kind=kLoop, calls=%fused_computation | loop fusion | flops 201326592 | bytes 536870912 | tf_op jit(solution)/shard_map/concatenate | solution.py:65
  1129.5 0.6 copy-done.30
  1130.2 1.3 copy.91
  1131.6 2457.2 %reduce-scatter.5.cloned.1.call-done = f32[128,32768]{1,0:T(8,128)} async-done(((f32[2048,32768]{1,0:T(8,128)}), f32[128,32768]{1,0:T(8,128)}) %reduce-scatter.5.cloned.1.call-update) | async-done | bytes 16777232 | tf_op jit(solution)/shard_map/reduce_scatter | solution.py:172
  3588.8 9.1 convert_element_type.93
  3597.9 1.2 copy-done.17
  3599.5 14.5 convolution_add_fusion
  3614.1 35.9 reduce-scatter.7.cloned.1.call-done
  3649.9 0.9 copy.92
  3650.8 4.9 psum.15
  3655.8 0.6 convert_element_type.96
  3656.4 193.8 %all-reduce.2.cloned.1.call-done = bf16[128,32768]{1,0:T(8,128)(2,1)} async-done(((bf16[128,32768]{1,0:T(8,128)(2,1)}), bf16[128,32768]{1,0:T(8,128)(2,1)}) %all-reduce.2.cloned.1.call-update) | async-done | bytes 8388624 | tf_op jit(solution)/shard_map/psum | solution.py:175
  3850.2 2.3 slice.107
  3852.4 3.4 slice.106
  3855.8 4.2 slice.109
  3860.0 4.2 slice.108
  (109 shorter events, 2.3 us)
Async XLA Ops:
  7.2 2.9 copy-start.39
  7.2 3.3 copy-start.38
  7.2 133.8 %all-gather.5.cloned.1.call-start = ((), (), s32[]{:S(2)}) async-start(), calls=%async_computation.2 | async-start | bytes 26738688 | tf_op jit(solution)/shard_map/all_gather | solution.py:81
  7.9 210.2 %all-gather.7.cloned.1.call-start = ((), (), s32[]{:S(2)}) async-start(), calls=%async_computation.3 | async-start | bytes 8912896 | tf_op jit(solution)/shard_map/all_gather | solution.py:82
  8.7 535.4 %all-gather.9.cloned.1.call-start = ((), (), s32[]{:S(2)}) async-start(), calls=%async_computation.4 | async-start | bytes 71303168 | tf_op jit(solution)/shard_map/all_gather | solution.py:83
  9.4 704.2 %all-gather.11.cloned.1.call-start = ((), (), s32[]{:S(2)}) async-start(), calls=%async_computation.5 | async-start | bytes 35651584 | tf_op jit(solution)/shard_map/all_gather | solution.py:84
  10.0 3578.8 %reduce-scatter.5.cloned.1.call-start = ((), (), s32[]{:S(2)}) async-start(), calls=%async_computation.6 | async-start | bytes 285212672 | tf_op jit(solution)/shard_map/reduce_scatter | solution.py:172
  34.6 118.4 %copy-start.23 = (f32[128,64]{1,0:T(8,128)}, f32[128,64]{1,0:T(8,128)S(1)}, u32[]{:S(2)}) copy-start(f32[128,64]{1,0:T(8,128)S(1)} %get-tuple-element.49) | copy-start | bytes 98308
  34.6 116.8 %copy-start.26 = (f32[2048,1]{0,1:T(1,128)}, f32[2048,1]{0,1:T(1,128)S(1)}, u32[]{:S(2)}) copy-start(f32[2048,1]{0,1:T(1,128)S(1)} %get-tuple-element.45) | copy-start | bytes 24580
  34.6 116.8 %copy-start.28 = (f32[2048,1]{0,1:T(1,128)}, f32[2048,1]{0,1:T(1,128)S(1)}, u32[]{:S(2)}) copy-start(f32[2048,1]{0,1:T(1,128)S(1)} %get-tuple-element.46) | copy-start | bytes 24580
  151.3 0.5 copy-start.34
  151.3 0.5 copy-start.36
  154.3 0.8 copy-start.7
  154.4 1.5 copy-start.9
  154.4 1.6 copy-start.11
  154.4 1.6 copy-start.13
  155.9 1.0 copy-start
  218.1 5.9 copy-start.5
  223.1 1.0 copy-start.3
  713.6 16.6 copy-start.6
  730.2 1.0 copy-start.4
  785.3 0.8 copy-start.15
  795.2 4.7 copy-start.1
  795.3 4.9 copy-start.12
  795.3 4.9 copy-start.14
  798.1 3.5 copy-start.8
  798.1 3.6 copy-start.10
  799.9 3.3 copy-start.16
  799.9 3.3 copy-start.18
  803.2 8.1 copy-start.2
  803.2 8.1 copy-start.20
  834.3 49.4 %copy-start.24 = (f32[128,64]{1,0:T(8,128)S(1)}, f32[128,64]{1,0:T(8,128)}, u32[]{:S(2)}) copy-start(f32[128,64]{1,0:T(8,128)} %copy-done.23) | copy-start | bytes 98308
  834.3 49.4 %copy-start.25 = (f32[128,64]{1,0:T(8,128)S(1)}, f32[128,64]{1,0:T(8,128)}, u32[]{:S(2)}) copy-start(f32[128,64]{1,0:T(8,128)} %get-tuple-element.47) | copy-start | bytes 98308
  883.7 2.9 copy-start.27
  883.7 2.9 copy-start.29
  883.7 2.9 copy-start.35
  883.7 2.9 copy-start.37
  1129.4 0.7 copy-start.30
  1129.4 0.7 copy-start.31
  1129.4 0.7 copy-start.32
  1129.4 0.7 copy-start.33
  1129.5 2520.5 %reduce-scatter.7.cloned.1.call-start = ((), (), s32[]{:S(2)}) async-start(), calls=%async_computation.8 | async-start | bytes 1114112
  1131.6 2718.6 %all-reduce.2.cloned.1.call-start = ((), (), s32[]{:S(2)}) async-start(), calls=%async_computation.7 | async-start | bytes 16777216 | tf_op jit(solution)/shard_map/psum | solution.py:175
  3597.8 1.2 copy-start.17
  3597.8 1.4 copy-start.19
  3597.8 1.5 copy-start.21
  3597.8 1.7 copy-start.22
  3850.2 9.8 slice-start
  3855.8 4.2 slice-start.1
Sparse Core Ops, SparseCore 0:
  9.6 131.2 all-gather.4
  143.1 74.9 all-gather.6
  219.7 324.3 all-gather.8
  545.5 168.0 all-gather.10
  1129.6 2459.1 reduce-scatter.4
  3592.8 57.0 reduce-scatter.6
  3653.1 197.0 all-reduce.1
where the time goes:
time: 3880 us; the launch traced here: 3870 us
  waiting for transfers between devices  3310 us (85%)
  matrix products  241 us (6%)
  other arithmetic  202 us (5%)
  local copies, waits for them, and re-layouts  76.4 us (2%)
    reduce_scatter x1, waiting for transfers between devices, shards(): lax.psum_scatter(terms_of(lefts, rights), 'fsdp', scatter_dimension=0, ti...  2460 us
    all_gather x1, waiting for transfers between devices, shards(): lax.all_gather(w_gate_up, 'fsdp', axis=0, tiled=True)  319 us
    psum x1, waiting for transfers between devices, shards(): lax.psum(rows_part.astype(jnp.bfloat16), 'replica').astype(jnp.float32)  194 us
    concatenate x1, other arithmetic, terms_of(): return jnp.concatenate(pieces, axis=1)  170 us
    all_gather x1, waiting for transfers between devices, shards(): lax.all_gather(w_down_t, 'fsdp', axis=0, tiled=True)  134 us
    all_gather x1, waiting for transfers between devices, shards(): lax.all_gather(w_qkv, 'fsdp', axis=0, tiled=True)  106 us
    dot_general x4, matrix products, terms_of(): lax.dot_general(left_part, right_part, (((0,), (0,)), ((), ())), preferre...  99.3 us
  transfers between devices with their start and end apart: 7, of which 7 were waited for; matrix products, arithmetic and copies ran while one was open for 2% of the time, Pallas kernels for 0%

commit v1 on v0

v1 whole, which is shorter than its diff:
```python
import math

import jax
import jax.numpy as jnp
from jax import lax
from jax.sharding import Mesh, PartitionSpec as P

HD = 128

epsilon = 1e-06
theta_base = 500000.0

CUBE = ("x", "zl", "y", "c")
SIDE = ("zl", "y", "c")
OWNERS = ("zh", "zl", "y", "c")
EVERY = ("x", "zh", "zl", "y", "c")
MEMBERS = 16
SIDES = 8


def normalize(values, scales):
    inverse = lax.rsqrt(jnp.mean(values * values, axis=-1, keepdims=True) + epsilon)
    return (values * inverse * scales, inverse)


def norm_back(upstream, values, inverse, scales):
    unit_rows = values * inverse
    scaled = upstream * scales
    value_grad = inverse * (
        scaled - unit_rows * jnp.mean(scaled * unit_rows, axis=-1, keepdims=True)
    )
    return (value_grad, jnp.sum(upstream * unit_rows, axis=0))


def rope_tables(positions):
    frequency = theta_base ** (-2.0 * jnp.arange(HD // 2).astype(jnp.float32) / HD)
    angles = positions[:, None] * frequency[None, :]
    return (jnp.cos(angles)[:, None, :], jnp.sin(angles)[:, None, :])


def rotate(values, cos_table, sin_table):
    half_width = values.shape[-1] // 2
    former = values[..., :half_width]
    latter = values[..., half_width:]
    return jnp.concatenate(
        [former * cos_table - latter * sin_table, latter * cos_table + former * sin_table], axis=-1
    )


def contract_last(operand, matrix):
    return lax.dot_general(
        operand, matrix, (((1,), (1,)), ((), ())), preferred_element_type=jnp.float32
    )


def contract_first(operand, matrix):
    return lax.dot_general(
        operand, matrix, (((0,), (0,)), ((), ())), preferred_element_type=jnp.float32
    )


def masked_scores(query_bf, key_bf, allowed, score_scale):
    scores = (
        jnp.einsum("qhd,khd->hqk", query_bf, key_bf, preferred_element_type=jnp.float32)
        * score_scale
    )
    return jnp.where(allowed[None, :, :], scores, -1e30)


def gather_cube(block):
    return lax.all_gather(block, CUBE, axis=0, tiled=True)


def scatter_cube(partial):
    return lax.psum_scatter(
        partial.astype(jnp.bfloat16), CUBE, scatter_dimension=0, tiled=True
    ).astype(jnp.float32)


def swap_groups(blocks):
    groups = lax.axis_size("zh")
    if groups == 2:
        mine = lax.axis_index("zh")
        away = lax.dynamic_index_in_dim(blocks, 1 - mine, 0, keepdims=False)
        came = lax.ppermute(away, "zh", [(0, 1), (1, 0)])
        kept = lax.dynamic_index_in_dim(blocks, mine, 0, keepdims=False)
        return jnp.where(mine == 0, jnp.stack([kept, came]), jnp.stack([came, kept]))
    return lax.all_to_all(blocks, "zh", 0, 0, tiled=True)


def columns_of(weight, parts):
    rows, width = weight.shape
    piece = width // (parts * MEMBERS)
    groups = lax.axis_size("zh")
    half = lax.dynamic_index_in_dim(
        weight.reshape(rows, parts, 2, SIDES * piece), lax.axis_index("x"), 2, keepdims=False
    )
    if groups == 2:
        came = lax.ppermute(half, "zh", [(0, 1), (1, 0)])
        both = jnp.where(lax.axis_index("zh") == 0, jnp.stack([half, came]), jnp.stack([came, half]))
    else:
        both = lax.all_gather(half, "zh", axis=0)
    blocks = both.reshape(groups, rows, parts, SIDES, piece).transpose(3, 0, 1, 2, 4)
    came = lax.all_to_all(blocks, SIDE, 0, 0, tiled=True)
    return came.transpose(1, 0, 2, 3, 4).reshape(groups * SIDES * rows, parts * piece)


def owners_sum(grad_columns, parts):
    depth, width = grad_columns.shape
    piece = width // parts
    groups = lax.axis_size("zh")
    rows = depth // (groups * SIDES)
    blocks = grad_columns.astype(jnp.bfloat16).reshape(groups, SIDES, rows, parts, piece)
    came = lax.all_to_all(blocks, SIDE, 1, 1, tiled=True)
    terms = swap_groups(came)
    total = jnp.sum(terms.astype(jnp.float32), axis=0).astype(jnp.bfloat16)
    both = lax.all_gather(total, "x", axis=0)
    return (
        both.transpose(2, 3, 0, 1, 4).reshape(rows, parts * MEMBERS * piece).astype(jnp.float32)
    )


def shards(tokens, w_qkv, w_out, w_gate_up, w_down_t, gains, starts, cotangent):
    count_rows, width = tokens.shape
    head_count = width // HD
    score_scale = 1.0 / math.sqrt(HD)
    local_rows = jnp.arange(count_rows, dtype=jnp.int32)
    seq_begin = lax.cummax(jnp.where(starts == 1, local_rows, 0), axis=0)
    positions = (local_rows - seq_begin).astype(jnp.float32)
    cos_table, sin_table = rope_tables(positions)
    allowed = (local_rows[None, :] <= local_rows[:, None]) & (
        local_rows[None, :] >= seq_begin[:, None]
    )
    full_gains = lax.all_gather(gains, OWNERS, axis=0, tiled=True)
    gain_cols = full_gains.astype(jnp.float32)
    tokens_all = gather_cube(tokens)
    qkv_cols = columns_of(w_qkv, 3)
    full_out = lax.all_gather(w_out, OWNERS, axis=0, tiled=True)
    gate_up_cols = columns_of(w_gate_up, 2)
    down_cols = columns_of(w_down_t, 1)
    hidden_width = down_cols.shape[1]

    projected_cols = jnp.dot(
        tokens_all, qkv_cols, preferred_element_type=jnp.float32
    ).astype(jnp.bfloat16)
    projected = lax.all_to_all(
        projected_cols.reshape(MEMBERS, count_rows, 3, width // MEMBERS), CUBE, 0, 0, tiled=True
    )
    projected = projected.transpose(1, 2, 0, 3).reshape(count_rows, 3, width)
    query_raw = projected[:, 0].astype(jnp.float32)
    key_raw = projected[:, 1].astype(jnp.float32)
    value_bf = projected[:, 2].reshape(count_rows, head_count, HD)
    query_norm, query_inv = normalize(query_raw, gain_cols[:, 0])
    key_norm, key_inv = normalize(key_raw, gain_cols[:, 1])
    query_bf = rotate(query_norm.reshape(count_rows, head_count, HD), cos_table, sin_table).astype(
        jnp.bfloat16
    )
    key_bf = rotate(key_norm.reshape(count_rows, head_count, HD), cos_table, sin_table).astype(
        jnp.bfloat16
    )
    scores = masked_scores(query_bf, key_bf, allowed, score_scale)
    peaks = jnp.max(scores, axis=-1, keepdims=True)
    exponent = jnp.exp(scores - peaks)
    attention_f32 = exponent / jnp.sum(exponent, axis=-1, keepdims=True)
    attention = attention_f32.astype(jnp.bfloat16)
    attended = (
        jnp.einsum("hqk,khd->qhd", attention, value_bf, preferred_element_type=jnp.float32)
        .reshape(count_rows, width)
        .astype(jnp.bfloat16)
    )
    attended_all = gather_cube(attended)
    branch = jnp.dot(attended, full_out, preferred_element_type=jnp.float32)
    branch_norm, branch_inv = normalize(branch, gain_cols[:, 2])
    middle = tokens.astype(jnp.float32) + branch_norm
    middle_all = gather_cube(middle.astype(jnp.bfloat16))
    gate_up = jnp.dot(middle_all, gate_up_cols, preferred_element_type=jnp.float32)
    gate_part = gate_up[:, :hidden_width]
    up_part = gate_up[:, hidden_width:]
    sigmoid_gate = jax.nn.sigmoid(gate_part)
    hidden_bf = (gate_part * sigmoid_gate * up_part).astype(jnp.bfloat16)
    feed_out = scatter_cube(contract_last(hidden_bf, down_cols))
    feed_norm, feed_inv = normalize(feed_out, gain_cols[:, 3])
    mixed = (middle + feed_norm).astype(jnp.bfloat16)

    upstream = cotangent.astype(jnp.float32)
    feed_grad, gain_feed = norm_back(upstream, feed_out, feed_inv, gain_cols[:, 3])
    feed_all = gather_cube(feed_grad.astype(jnp.bfloat16))
    grad_down_t = owners_sum(contract_first(feed_all, hidden_bf), 1)
    hidden_grad = jnp.dot(feed_all, down_cols, preferred_element_type=jnp.float32)
    gate_grad = hidden_grad * up_part * sigmoid_gate * (1.0 + gate_part * (1.0 - sigmoid_gate))
    up_grad = hidden_grad * gate_part * sigmoid_gate
    gate_up_bf = jnp.concatenate([gate_grad, up_grad], axis=1).astype(jnp.bfloat16)
    grad_gate_up = owners_sum(contract_first(middle_all, gate_up_bf), 2)
    middle_grad = upstream + scatter_cube(contract_last(gate_up_bf, gate_up_cols))
    branch_grad, gain_branch = norm_back(middle_grad, branch, branch_inv, gain_cols[:, 2])
    branch_bf = branch_grad.astype(jnp.bfloat16)
    branch_cols = lax.all_to_all(
        branch_bf.reshape(count_rows, MEMBERS, width // MEMBERS), CUBE, 1, 0, tiled=True
    ).reshape(MEMBERS * count_rows, width // MEMBERS)
    grad_out = owners_sum(contract_first(attended_all, branch_cols), 1)
    attended_grad = (
        contract_last(branch_bf, full_out).astype(jnp.bfloat16).reshape(count_rows, head_count, HD)
    )
    prob_grad = jnp.einsum(
        "qhd,khd->hqk", attended_grad, value_bf, preferred_element_type=jnp.float32
    )
    score_bf = (
        attention_f32 * (prob_grad - jnp.sum(attention_f32 * prob_grad, axis=-1, keepdims=True))
    ).astype(jnp.bfloat16)
    value_grad = jnp.einsum(
        "hqk,qhd->khd", attention, attended_grad, preferred_element_type=jnp.float32
    )
    query_grad = (
        jnp.einsum("hqk,khd->qhd", score_bf, key_bf, preferred_element_type=jnp.float32)
        * score_scale
    )
    key_grad = (
        jnp.einsum("hqk,qhd->khd", score_bf, query_bf, preferred_element_type=jnp.float32)
        * score_scale
    )
    query_grad = rotate(query_grad, cos_table, -sin_table).reshape(count_rows, width)
    key_grad = rotate(key_grad, cos_table, -sin_table).reshape(count_rows, width)
    query_raw_grad, gain_query = norm_back(query_grad, query_raw, query_inv, gain_cols[:, 0])
    key_raw_grad, gain_key = norm_back(key_grad, key_raw, key_inv, gain_cols[:, 1])
    projected_bf = jnp.stack(
        [query_raw_grad, key_raw_grad, value_grad.reshape(count_rows, width)], axis=1
    ).astype(jnp.bfloat16)
    projected_cols_grad = lax.all_to_all(
        projected_bf.reshape(count_rows, 3, MEMBERS, width // MEMBERS).transpose(2, 0, 1, 3),
        CUBE, 0, 0, tiled=True,
    ).reshape(MEMBERS * count_rows, 3 * width // MEMBERS)
    grad_qkv = owners_sum(contract_first(tokens_all, projected_cols_grad), 3)
    grad_tokens = middle_grad + scatter_cube(contract_last(projected_cols_grad, qkv_cols))
    gain_terms = jnp.stack([gain_query, gain_key, gain_branch, gain_feed], axis=0)
    gain_sums = lax.psum(gain_terms, EVERY)
    owner = lax.axis_index(OWNERS)
    grad_gains = lax.dynamic_slice_in_dim(
        gain_sums, owner * gains.shape[0], gains.shape[0], axis=1
    ).T
    return (mixed, grad_tokens, grad_qkv, grad_out, grad_gate_up, grad_down_t, grad_gains)


def solution(mesh):
    sizes = dict(mesh.shape)
    groups = sizes["fsdp"] // SIDES
    finer = Mesh(mesh.devices.reshape(2, groups, 2, 2, 2), EVERY)
    return jax.shard_map(
        shards,
        mesh=finer,
        in_specs=(
            P(EVERY, None),
            P(OWNERS, None),
            P(OWNERS, None),
            P(OWNERS, None),
            P(OWNERS, None),
            P(OWNERS, None),
            P(EVERY),
            P(EVERY, None),
        ),
        out_specs=(
            P(EVERY, None),
            P(EVERY, None),
            P(OWNERS, None),
            P(OWNERS, None),
            P(OWNERS, None),
            P(OWNERS, None),
            P(OWNERS, None),
        ),
        check_vma=False,
    )
```

time: 3880 us -> 1160 us (0.30)
  waiting for transfers between devices: 3310 us -> 588 us
  blocking collectives: 28.1 us -> 165 us
  other arithmetic: 202 us -> 65.2 us
  matrix products: 241 us -> 115 us
  local copies, waits for them, and re-layouts: 76.4 us -> 147 us
  starting transfers between devices: 0.27 us -> 50.8 us
    reduce_scatter x1 -> x3, waiting for transfers between devices: 2460 us -> 110 us  [scatter_cube(): lax.psum_scatter(partial.astype(jnp.bfloat16), CUBE, scatter_dimension=0,...]
    all_gather x4 -> x8, waiting for transfers between devices: 619 us -> 74 us  [the longest x4 54 us: gather_cube(): return lax.all_gather(block, CUBE, axis=0, tiled=True)]
    ppermute x0 -> x7, waiting for transfers between devices: none -> 256 us  [the longest x3 173 us: columns_of(): came = lax.ppermute(half, 'zh', [(0, 1), (1, 0)])]
    psum x1 -> x0, waiting for transfers between devices: 194 us -> none  [shards(): lax.psum(rows_part.astype(jnp.bfloat16), 'replica').astype(jnp.float32)]
    concatenate x1 -> x2, other arithmetic: 170 us -> 3.3 us  [rotate(): jnp.concatenate([former * cos_table - latter * sin_table, latter * cos_ta...]
    all_to_all x0 -> x8, waiting for transfers between devices: none -> 146 us  [the longest x3 90.5 us: owners_sum(): came = lax.all_to_all(blocks, SIDE, 1, 1, tiled=True)]
    dot_general x9 -> x8, matrix products: 161 us -> 69.8 us  [the longest x4 35.3 us: contract_first(): lax.dot_general(operand, matrix, (((0,), (0,)), ((), ())), preferred_elem...]
    all_to_all x0 -> x2, blocking collectives: none -> 63.1 us  [the longest x1 39.9 us: columns_of(): came = lax.all_to_all(blocks, SIDE, 0, 0, tiled=True)]
  transfers between devices with their start and end apart: 7 -> 26, of which waited for: 7 -> 15; matrix products, arithmetic and copies ran while one was open for 2% -> 22% of each run, Pallas kernels for 0% -> 0%
where the time goes in v1:
time: 1160 us; the launch traced here: 1150 us
  waiting for transfers between devices  588 us (51%)
  blocking collectives  165 us (14%)
  local copies, waits for them, and re-layouts  147 us (13%)
  matrix products  115 us (10%)
  other arithmetic  65.2 us (6%)
  starting transfers between devices  50.8 us (4%)
  between operations  15.1 us (1%)
    ppermute x3, waiting for transfers between devices, columns_of(): came = lax.ppermute(half, 'zh', [(0, 1), (1, 0)])  173 us
    reduce_scatter x3, waiting for transfers between devices, scatter_cube(): lax.psum_scatter(partial.astype(jnp.bfloat16), CUBE, scatter_dimension=0,...  110 us
    all_to_all x3, waiting for transfers between devices, owners_sum(): came = lax.all_to_all(blocks, SIDE, 1, 1, tiled=True)  90.5 us
    ppermute x4, waiting for transfers between devices, swap_groups(): came = lax.ppermute(away, 'zh', [(0, 1), (1, 0)])  82.8 us
    all_gather x4, waiting for transfers between devices, gather_cube(): return lax.all_gather(block, CUBE, axis=0, tiled=True)  54 us
    all_gather x1, blocking collectives, shards(): full_gains = lax.all_gather(gains, OWNERS, axis=0, tiled=True)  47.3 us
    all_to_all x2, waiting for transfers between devices, columns_of(): came = lax.all_to_all(blocks, SIDE, 0, 0, tiled=True)  44.8 us
    psum x1, blocking collectives, shards(): gain_sums = lax.psum(gain_terms, EVERY)  44.6 us
  transfers between devices with their start and end apart: 26, of which 15 were waited for; matrix products, arithmetic and copies ran while one was open for 22% of the time, Pallas kernels for 0%

profile of v1, /device:TPU:0, one launch (start us, length us, event | category | flops | bytes accessed | tf_op | source)
XLA Modules:
  0.0 1145.5 jit_solution(9004772502803610823)
XLA Ops:
  10.9 4.1 collective-permute-start
  15.0 34.5 %collective-permute-done = bf16[128,3,1024]{2,0,1:T(8,128)(2,1)S(1)} collective-permute-done((bf16[128,3,1024]{2,0,1:T(8,128)(2,1)S(1)}, bf16[128,3,1024]{2,0,1:T(8,128)(2,1)S(1)}, u32[]{:S(2)}, u32[]{:S(2)}) %collective-permute-start) | collective-permute-done | bytes 786464 | tf_op jit(solution)/shard_map/ppermute | solution.py:99
  50.3 39.9 %all_to_all.60 = bf16[8,2,128,3,128]{2,4,3,1,0:T(8,128)(2,1)S(1)} all-to-all(bf16[8,2,128,3,128]{2,4,3,1,0:T(8,128)(2,1)S(1)} %copy.188), channel_id=1, replica_groups=mesh['x'=2,'zh'=2,'zl'=2,'y'=2,'c'=2] {'zl','y','c'}, dimensions={0} | all-to-all | bytes 3145728 | tf_op jit(solution)/shard_map/all_to_all | solution.py:104
  94.5 6.8 fusion.10
  103.3 3.9 all-to-all-start.1
  107.6 47.3 %all_gather.43 = bf16[2048,4]{0,1:T(4,128)(2,1)S(1)} all-gather(bf16[128,4]{0,1:T(4,128)(2,1)S(1)} %copy-done.46), channel_id=1, replica_groups=mesh['x'=2,'zh'=2,'zl'=2,'y'=2,'c'=2] {'zh','zl','y','c'}, dimensions={0}, use_global_device_ids=true | all-gather | bytes 17408 | tf_op jit(solution)/shard_map/all_gather | solution.py:134
  166.0 20.0 %all-gather.15.cloned.1.call-done = bf16[2048,2048]{1,0:T(8,128)(2,1)} async-done(((bf16[128,2048]{1,0:T(8,128)(2,1)}), bf16[2048,2048]{1,0:T(8,128)(2,1)}) %all-gather.15.cloned.1.call-update) | async-done | bytes 8388624 | tf_op jit(solution)/shard_map/all_gather | solution.py:138
  186.0 4.8 multiply_reduce_fusion.5
  198.6 46.9 %collective-permute-done.2 = bf16[128,1,4096]{2,0,1:T(8,128)(2,1)} collective-permute-done((bf16[128,1,4096]{2,0,1:T(8,128)(2,1)S(1)}, bf16[128,1,4096]{2,0,1:T(8,128)(2,1)}, u32[]{:S(2)}, u32[]{:S(2)}) %collective-permute-start.2) | collective-permute-done | bytes 1048608 | tf_op jit(solution)/shard_map/ppermute | solution.py:99
  248.9 4.4 all-to-all-start.3
  253.2 6.4 copy.196
  266.5 91.7 %collective-permute-done.1 = bf16[128,2,4096]{2,0,1:T(8,128)(2,1)} collective-permute-done((bf16[128,2,4096]{2,0,1:T(8,128)(2,1)}, bf16[128,2,4096]{2,0,1:T(8,128)(2,1)}, u32[]{:S(2)}, u32[]{:S(2)}) %collective-permute-start.1) | collective-permute-done | bytes 2097184 | tf_op jit(solution)/shard_map/ppermute | solution.py:99
  358.2 4.1 copy.198
  362.2 2.9 fusion.2
  367.5 4.6 all-to-all-start.2
  372.6 2.9 copy.205
  375.4 44.8 %all-to-all-done.2 = bf16[8,2,128,2,512]{2,4,3,1,0:T(8,128)(2,1)} async-done(((bf16[8,2,128,2,512]{2,4,3,1,0:T(8,128)(2,1)}), bf16[8,2,128,2,512]{2,4,3,1,0:T(8,128)(2,1)}, u32[]{:S(2)}, u32[]{:S(2)}) %all-to-all-start.2) | async-done | bytes 4194336 | tf_op jit(solution)/shard_map/all_to_all | solution.py:104
  420.2 6.9 copy.200
  427.1 7.3 reshape.703
  434.4 12.5 %fusion.54 = f32[2048,1024]{0,1:T(8,128)S(1)} fusion(bf16[2048,2048]{1,0:T(8,128)(2,1)} %all-gather.17.cloned.1.call-done, bf16[2048,1024]{0,1:T(8,128)(2,1)} %reshape.703), kind=kOutput, calls=%fused_computation.152 | convolution fusion | flops 8589934592 | bytes 20971520 | tf_op jit(solution)/shard_map/dot_general | solution.py:176
  451.7 7.0 convolution_convert_fusion.2
  458.7 91.5 %reduce-scatter.4.cloned.1.call-done = bf16[128,2048]{1,0:T(8,128)(2,1)} async-done(((bf16[2048,2048]{1,0:T(8,128)(2,1)}), bf16[128,2048]{1,0:T(8,128)(2,1)}) %reduce-scatter.4.cloned.1.call-update) | async-done | bytes 524304 | tf_op jit(solution)/shard_map/reduce_scatter | solution.py:75
  555.9 51.5 %all-gather.19.cloned.1.call-done = bf16[2048,2048]{1,0:T(8,128)(2,1)} async-done(((bf16[128,2048]{1,0:T(8,128)(2,1)}), bf16[2048,2048]{1,0:T(8,128)(2,1)}) %all-gather.19.cloned.1.call-update) | async-done | bytes 8388624 | tf_op jit(solution)/shard_map/all_gather | solution.py:71
  607.4 14.6 %multiply_convert_fusion.1 = (bf16[2048,512]{0,1:T(8,128)(2,1)}, bf16[2048,512]{0,1:T(8,128)(2,1)}) fusion(f32[2048,1024]{0,1:T(8,128)} %copy-done.4, bf16[2048,2048]{1,0:T(8,128)(2,1)} %all-gather.19.cloned.1.call-done, bf16[2048,512]{1,0:T(8,128)(2,1)} %bitcast.226), kind=kOutput, calls=%fused_computation.12 | convolution fusion | flops 4308598784 | bytes 23068672 | tf_op jit(solution)/shard_map/dot_general | solution.py:189
  622.1 13.5 %convolution_convert_fusion.1 = bf16[2048,2048]{1,0:T(8,128)(2,1)} fusion(bf16[2048,1024]{0,1:T(8,128)(2,1)S(1)} %copy-done.13, bf16[2048,512]{0,1:T(8,128)(2,1)} %get-tuple-element.20, bf16[2048,512]{0,1:T(8,128)(2,1)} %get-tuple-element.19), kind=kOutput, calls=%fused_computation.4 | convolution fusion | flops 8602517504 | bytes 16777216 | tf_op jit(solution)/shard_map/dot_general | solution.py:51
  635.6 8.6 convolution_convert_fusion.4
  645.7 4.4 all-to-all-start.9
  650.8 14.2 %convolution_convert_fusion.3 = bf16[2048,1024]{1,0:T(8,128)(2,1)} fusion(bf16[2048,2048]{1,0:T(8,128)(2,1)} %all-gather.17.cloned.1.call-done, bf16[2048,512]{0,1:T(8,128)(2,1)} %get-tuple-element.20, bf16[2048,512]{0,1:T(8,128)(2,1)} %get-tuple-element.19), kind=kOutput, calls=%fused_computation.15 | convolution fusion | flops 8600420352 | bytes 16777216 | tf_op jit(solution)/shard_map/dot_general | solution.py:57
  665.0 7.9 reshape.714
  672.8 7.3 copy.229
  680.1 7.9 all-to-all-done.9
  688.0 5.0 all-to-all-start.8
  693.0 3.1 constant_dynamic-slice_fusion.1
  698.4 82.7 %all-to-all-done.8 = bf16[2,8,128,2,512]{4,3,2,0,1:T(2,128)(2,1)} async-done(((bf16[2,8,128,2,512]{4,3,2,0,1:T(2,128)(2,1)}), bf16[2,8,128,2,512]{4,3,2,0,1:T(2,128)(2,1)}, u32[]{:S(2)}, u32[]{:S(2)}) %all-to-all-start.8) | async-done | bytes 4194336 | tf_op jit(solution)/shard_map/all_to_all | solution.py:114
  781.1 7.4 constant_dynamic-slice_fusion.2
  789.1 6.7 reduce-scatter.6.cloned.1.call-done
  799.5 6.4 convolution_convert_fusion.8
  812.1 3.0 pad_maximum_fusion.3
  823.4 6.1 all-to-all-start.4
  829.7 3.8 fusion.4
  833.7 48.0 %collective-permute-done.5 = bf16[8,128,2,512]{3,2,1,0:T(2,128)(2,1)} collective-permute-done((bf16[8,128,2,512]{3,2,1,0:T(2,128)(2,1)}, bf16[8,128,2,512]{3,2,1,0:T(2,128)(2,1)}, u32[]{:S(2)}, u32[]{:S(2)}) %collective-permute-start.5) | collective-permute-done | bytes 2097184 | tf_op jit(solution)/shard_map/ppermute | solution.py:85
  881.7 19.6 %fusion.1 = bf16[8,128,2,512]{3,2,1,0:T(2,128)(2,1)} fusion(pred[]{:T(512)S(6)} %eq.6, bf16[1,8,128,2,512]{4,3,2,0,1:T(2,128)(2,1)} %bitcast.60, bf16[1,8,128,2,512]{4,3,2,0,1:T(2,128)(2,1)} %get-tuple-element.21), kind=kLoop, calls=%fused_computation.6 | loop fusion | flops 7340032 | bytes 6291457 | tf_op jit(solution)/shard_map/reduce_sum | solution.py:116
  901.3 3.3 copy.231
  906.9 6.9 fusion.11
  915.8 23.1 %all_to_all.61 = bf16[2,8,128,3,128]{2,0,4,3,1:T(2,128)(2,1)S(1)} all-to-all(bf16[2,8,128,3,128]{2,0,4,3,1:T(2,128)(2,1)S(1)} %copy.220), channel_id=1, replica_groups=mesh['x'=2,'zh'=2,'zl'=2,'y'=2,'c'=2] {'zl','y','c'}, dimensions={1} | all-to-all | bytes 3145728 | tf_op jit(solution)/shard_map/all_to_all | solution.py:114
  939.0 4.7 constant_dynamic-slice_fusion.5
  943.7 4.7 copy.250
  950.9 34.8 %collective-permute-done.3 = bf16[8,128,3,128]{3,1,2,0:T(8,128)(2,1)} collective-permute-done((bf16[8,128,3,128]{3,1,2,0:T(8,128)(2,1)}, bf16[8,128,3,128]{3,1,2,0:T(8,128)(2,1)}, u32[]{:S(2)}, u32[]{:S(2)}) %collective-permute-start.3) | collective-permute-done | bytes 786464 | tf_op jit(solution)/shard_map/ppermute | solution.py:85
  988.8 9.8 convolution_convert_fusion
  1000.6 3.6 all-to-all-start.6
  1004.2 10.5 all-to-all-done.6
  1014.7 5.7 convolution_convert_fusion.7
  1021.3 3.5 all-to-all-start.7
  1027.0 4.4 copy.235
  1031.4 5.1 reshape.721
  1036.5 3.4 convert_bitcast_fusion
  1039.9 4.9 copy.232
  1044.8 10.1 copy.257
  1056.6 44.6 %psum.7 = f32[4,2048]{1,0:T(4,128)S(1)} all-reduce(f32[4,2048]{1,0:T(4,128)S(1)} %pad_maximum_fusion.15), channel_id=1, replica_groups=mesh['x'=2,'zh'=2,'zl'=2,'y'=2,'c'=2] {'x','zh','zl','y','c'}, use_global_device_ids=true, to_apply=%region_23.24 | all-reduce | flops 8192 | bytes 65536 | tf_op jit(solution)/shard_map/psum | solution.py:235
  1101.9 9.6 all-gather.1
  1113.3 3.4 convert_bitcast_fusion.2
  1116.7 3.6 copy.224
  1120.3 4.6 copy.268
  1124.9 11.6 %reduce-scatter.8.cloned.1.call-done = bf16[128,2048]{1,0:T(8,128)(2,1)} async-done(((bf16[2048,2048]{1,0:T(8,128)(2,1)}), bf16[128,2048]{1,0:T(8,128)(2,1)}) %reduce-scatter.8.cloned.1.call-update) | async-done | bytes 524304 | tf_op jit(solution)/shard_map/reduce_scatter | solution.py:75
  (220 shorter events, 98.3 us)
Async XLA Ops:
  7.2 87.3 %all-gather.13.cloned.1.call-start = ((), (), s32[]{:S(2)}) async-start(), calls=%async_computation.13 | async-start | bytes 8912896 | tf_op jit(solution)/shard_map/all_gather | solution.py:71
  7.9 178.1 %all-gather.15.cloned.1.call-start = ((), (), s32[]{:S(2)}) async-start(), calls=%async_computation.14 | async-start | bytes 8912896 | tf_op jit(solution)/shard_map/all_gather | solution.py:138
  10.9 38.6 %collective-permute-start = (bf16[128,3,1024]{2,0,1:T(8,128)(2,1)S(1)}, bf16[128,3,1024]{2,0,1:T(8,128)(2,1)S(1)}, u32[]{:S(2)}, u32[]{:S(2)}) collective-permute-start(bf16[128,3,1024]{2,0,1:T(8,128)(2,1)S(1)} %bitcast.234), channel_id=1, source_target_pairs={{0,8},{8,0},{1,9},{9,1},{2,10},{10,2},{3,11},{11,3},{4,12},{12,4},... | collective-permute-start | bytes 2359304 | tf_op jit(solution)/shard_map/ppermute | solution.py:99
  92.0 9.3 copy-start.26
  103.3 3.9 copy-start.47
  103.3 4.3 copy-start.46
  103.3 52.7 %all-to-all-start.1 = ((bf16[16,128,3,128]{1,3,2,0:T(8,128)(2,1)}), bf16[16,128,3,128]{1,3,2,0:T(8,128)(2,1)S(1)}, u32[]{:S(2)}, u32[]{:S(2)}) async-start(bf16[16,128,3,128]{1,3,2,0:T(8,128)(2,1)} %copy.190), calls=%async_computation.1 | async-start | bytes 3145728 | tf_op jit(solution)/shard_map/all_to_all | solution.py:146
  107.1 327.3 %all-gather.17.cloned.1.call-start = ((), (), s32[]{:S(2)}) async-start(), calls=%async_computation.15 | async-start | bytes 8912896 | tf_op jit(solution)/shard_map/all_gather | solution.py:71
  155.9 6.6 copy-start.31
  155.9 4.9 copy-start.39
  155.9 6.4 copy-start.37
  156.1 4.4 copy-start
  160.9 1.7 copy-start.42
  160.9 1.7 copy-start.44
  163.3 2.6 copy-start.16
  163.4 2.6 copy-start.18
  163.4 2.6 copy-start.22
  164.2 1.8 copy-start.28
  166.0 24.8 %copy-start.14 = (bf16[16,128,128]{2,1,0:T(8,128)(2,1)}, bf16[16,128,128]{2,1,0:T(8,128)(2,1)S(1)}, u32[]{:S(2)}) copy-start(bf16[16,128,128]{2,1,0:T(8,128)(2,1)S(1)} %convolution_convert_fusion.10) | copy-start | bytes 1572868
  186.0 4.8 copy-start.6
  190.9 1.8 copy-start.24
  196.9 48.5 %collective-permute-start.2 = (bf16[128,1,4096]{2,0,1:T(8,128)(2,1)S(1)}, bf16[128,1,4096]{2,0,1:T(8,128)(2,1)}, u32[]{:S(2)}, u32[]{:S(2)}) collective-permute-start(bf16[128,1,4096]{2,0,1:T(8,128)(2,1)S(1)} %bitcast.233), channel_id=1, source_target_pairs={{0,8},{8,0},{1,9},{9,1},{2,10},{10,2},{3,11},{11,3},{4,12},{12,4},... | collective-permute-start | bytes 3145736 | tf_op jit(solution)/shard_map/ppermute | solution.py:99
  248.9 118.6 %all-to-all-start.3 = ((bf16[8,2,128,1,512]{2,4,3,1,0:T(8,128)(2,1)}), bf16[8,2,128,1,512]{2,4,3,1,0:T(8,128)(2,1)}, u32[]{:S(2)}, u32[]{:S(2)}) async-start(bf16[8,2,128,1,512]{2,4,3,1,0:T(8,128)(2,1)} %copy.204), calls=%async_computation.3 | async-start | bytes 4194304 | tf_op jit(solution)/shard_map/all_to_all | solution.py:104
  264.1 94.0 %collective-permute-start.1 = (bf16[128,2,4096]{2,0,1:T(8,128)(2,1)}, bf16[128,2,4096]{2,0,1:T(8,128)(2,1)}, u32[]{:S(2)}, u32[]{:S(2)}) collective-permute-start(bf16[128,2,4096]{2,0,1:T(8,128)(2,1)} %bitcast.227), channel_id=1, source_target_pairs={{0,8},{8,0},{1,9},{9,1},{2,10},{10,2},{3,11},{11,3},{4,12},{12,4},... | collective-permute-start | bytes 6291464 | tf_op jit(solution)/shard_map/ppermute | solution.py:99
  367.5 52.7 %all-to-all-start.2 = ((bf16[8,2,128,2,512]{2,4,3,1,0:T(8,128)(2,1)}), bf16[8,2,128,2,512]{2,4,3,1,0:T(8,128)(2,1)}, u32[]{:S(2)}, u32[]{:S(2)}) async-start(bf16[8,2,128,2,512]{2,4,3,1,0:T(8,128)(2,1)} %copy.199), calls=%async_computation.2 | async-start | bytes 8388608 | tf_op jit(solution)/shard_map/all_to_all | solution.py:104
  372.0 178.1 %reduce-scatter.4.cloned.1.call-start = ((), (), s32[]{:S(2)}) async-start(), calls=%async_computation.16 | async-start | bytes 8912896 | tf_op jit(solution)/shard_map/reduce_scatter | solution.py:75
  375.4 74.9 %copy-start.25 = (bf16[8,2,128,1,512]{4,2,0,1,3:T(8,128)(2,1)}, bf16[8,2,128,1,512]{4,2,0,1,3:T(8,128)(2,1)S(1)}, u32[]{:S(2)}) copy-start(bf16[8,2,128,1,512]{4,2,0,1,3:T(8,128)(2,1)S(1)} %copy.205) | copy-start | bytes 6291460
  446.9 3.4 copy-start.4
  450.3 1.3 copy-start.15
  458.6 92.8 %copy-start.2 = (bf16[128,2048]{1,0:T(8,128)(2,1)S(1)}, bf16[128,2048]{1,0:T(8,128)(2,1)}, u32[]{:S(2)}) copy-start(bf16[128,2048]{1,0:T(8,128)(2,1)} %param.15) | copy-start | bytes 1572868
  458.7 148.8 %all-gather.19.cloned.1.call-start = ((), (), s32[]{:S(2)}) async-start(), calls=%async_computation.17 | async-start | bytes 8912896 | tf_op jit(solution)/shard_map/all_gather | solution.py:71
  555.7 240.0 %reduce-scatter.6.cloned.1.call-start = ((), (), s32[]{:S(2)}) async-start(), calls=%async_computation.18 | async-start | bytes 8912896 | tf_op jit(solution)/shard_map/reduce_scatter | solution.py:75
  607.4 14.6 %copy-start.13 = (bf16[2048,1024]{0,1:T(8,128)(2,1)S(1)}, bf16[2048,1024]{0,1:T(8,128)(2,1)}, u32[]{:S(2)}) copy-start(bf16[2048,1024]{0,1:T(8,128)(2,1)} %reshape.703) | copy-start | bytes 12582916
  645.7 42.3 %all-to-all-start.9 = ((bf16[2,8,128,1,512]{4,2,0,3,1:T(8,128)(2,1)}), bf16[2,8,128,1,512]{4,2,0,3,1:T(8,128)(2,1)}, u32[]{:S(2)}, u32[]{:S(2)}) async-start(bf16[2,8,128,1,512]{4,2,0,3,1:T(8,128)(2,1)} %copy.233), calls=%async_computation.12 | async-start | bytes 4194304 | tf_op jit(solution)/shard_map/all_to_all | solution.py:114
  650.0 354.2 %all-gather.21.cloned.1.call-start = ((), (), s32[]{:S(2)}) async-start(), calls=%async_computation.20 | async-start | bytes 8912896 | tf_op jit(solution)/shard_map/all_gather | solution.py:71
  688.0 93.1 %all-to-all-start.8 = ((bf16[2,8,128,2,512]{4,3,2,0,1:T(2,128)(2,1)}), bf16[2,8,128,2,512]{4,3,2,0,1:T(2,128)(2,1)}, u32[]{:S(2)}, u32[]{:S(2)}) async-start(bf16[2,8,128,2,512]{4,3,2,0,1:T(2,128)(2,1)} %copy.229), calls=%async_computation.11 | async-start | bytes 8388608 | tf_op jit(solution)/shard_map/all_to_all | solution.py:114
  696.0 133.7 %collective-permute-start.6 = (bf16[8,128,1,512]{3,1,0,2:T(8,128)(2,1)}, bf16[8,128,1,512]{3,1,0,2:T(8,128)(2,1)}, u32[]{:S(2)}, u32[]{:S(2)}) collective-permute-start(bf16[8,128,1,512]{3,1,0,2:T(8,128)(2,1)} %get-tuple-element.24), channel_id=1, source_target_pairs={{0,8},{8,0},{1,9},{9,1},{2,10},{10,2},{3,11},{11,3},{4,12},{12,4},... | collective-permute-start | bytes 3145736 | tf_op jit(solution)/shard_map/ppermute | solution.py:85
  788.5 8.8 copy-start.5
  788.5 8.8 copy-start.7
  788.5 93.2 %collective-permute-start.5 = (bf16[8,128,2,512]{3,2,1,0:T(2,128)(2,1)}, bf16[8,128,2,512]{3,2,1,0:T(2,128)(2,1)}, u32[]{:S(2)}, u32[]{:S(2)}) collective-permute-start(bf16[8,128,2,512]{3,2,1,0:T(2,128)(2,1)} %get-tuple-element.22), channel_id=1, source_target_pairs={{0,8},{8,0},{1,9},{9,1},{2,10},{10,2},{3,11},{11,3},{4,12},{12,4},... | collective-permute-start | bytes 6291464 | tf_op jit(solution)/shard_map/ppermute | solution.py:85
  795.7 1.5 copy-start.10
  799.5 6.7 copy-start.29
  799.5 6.7 copy-start.35
  807.1 1.7 copy-start.17
  807.1 1.7 copy-start.19
  812.0 5.6 copy-start.1
  812.0 5.5 copy-start.38
  812.0 5.5 copy-start.40
  812.0 5.5 copy-start.43
  812.1 5.5 copy-start.45
  817.6 2.6 copy-start.3
  820.1 1.4 copy-start.34
  823.4 6.3 copy-start.12
  823.4 81.3 %all-to-all-start.4 = ((bf16[16,128,3,128]{1,3,2,0:T(8,128)(2,1)}), bf16[16,128,3,128]{1,3,2,0:T(8,128)(2,1)S(1)}, u32[]{:S(2)}, u32[]{:S(2)}) async-start(bf16[16,128,3,128]{1,3,2,0:T(8,128)(2,1)} %copy.218), calls=%async_computation.6 | async-start | bytes 3145728 | tf_op jit(solution)/shard_map/all_to_all | solution.py:228
  829.5 195.3 %all-gather.27.cloned.1.call-start = ((), (), s32[]{:S(2)}) async-start(), calls=%async_computation.23 | async-start | bytes 3145728 | tf_op jit(solution)/shard_map/all_gather | solution.py:117
  833.6 202.9 %all-gather.25.cloned.1.call-start = ((), (), s32[]{:S(2)}) async-start(), calls=%async_computation.22 | async-start | bytes 6291456 | tf_op jit(solution)/shard_map/all_gather | solution.py:117
  904.7 208.7 %all-gather.23.cloned.1.call-start = ((), (), s32[]{:S(2)}) async-start(), calls=%async_computation.21 | async-start | bytes 2359296 | tf_op jit(solution)/shard_map/all_gather | solution.py:117
  948.3 37.4 %collective-permute-start.3 = (bf16[8,128,3,128]{3,1,2,0:T(8,128)(2,1)}, bf16[8,128,3,128]{3,1,2,0:T(8,128)(2,1)}, u32[]{:S(2)}, u32[]{:S(2)}) collective-permute-start(bf16[8,128,3,128]{3,1,2,0:T(8,128)(2,1)} %bitcast.46), channel_id=1, source_target_pairs={{0,8},{8,0},{1,9},{9,1},{2,10},{10,2},{3,11},{11,3},{4,12},{12,4},... | collective-permute-start | bytes 2359304 | tf_op jit(solution)/shard_map/ppermute | solution.py:85
  988.8 147.7 %reduce-scatter.8.cloned.1.call-start = ((), (), s32[]{:S(2)}) async-start(), calls=%async_computation.19 | async-start | bytes 8912896 | tf_op jit(solution)/shard_map/reduce_scatter | solution.py:75
  1000.6 14.1 %all-to-all-start.6 = ((bf16[128,16,128]{2,0,1:T(8,128)(2,1)}), bf16[128,16,128]{2,0,1:T(8,128)(2,1)S(1)}, u32[]{:S(2)}, u32[]{:S(2)}) async-start(bf16[128,16,128]{2,0,1:T(8,128)(2,1)} %copy_bitcast_fusion.1), calls=%async_computation.9 | async-start | bytes 1048576 | tf_op jit(solution)/shard_map/all_to_all | solution.py:197
  1021.3 33.6 %all-to-all-start.7 = ((bf16[2,8,128,1,128]{4,2,0,3,1:T(8,128)(2,1)}), bf16[2,8,128,1,128]{4,2,0,3,1:T(8,128)(2,1)S(1)}, u32[]{:S(2)}, u32[]{:S(2)}) async-start(bf16[2,8,128,1,128]{4,2,0,3,1:T(8,128)(2,1)} %copy.226), calls=%async_computation.10 | async-start | bytes 1048576 | tf_op jit(solution)/shard_map/all_to_all | solution.py:114
  1044.8 11.8 %copy-start.41 = (f32[2048]{0:T(1024)S(1)}, f32[2048]{0:T(1024)}, u32[]{:S(2)}) copy-start(f32[2048]{0:T(1024)} %get-tuple-element.17) | copy-start | bytes 24580
  1054.9 46.8 %collective-permute-start.4 = (bf16[8,128,1,128]{3,1,0,2:T(8,128)(2,1)S(1)}, bf16[8,128,1,128]{3,1,0,2:T(8,128)(2,1)S(1)}, u32[]{:S(2)}, u32[]{:S(2)}) collective-permute-start(bf16[8,128,1,128]{3,1,0,2:T(8,128)(2,1)S(1)} %get-tuple-element.43), channel_id=1, source_target_pairs={{0,8},{8,0},{1,9},{9,1},{2,10},{10,2},{3,11},{11,3},{4,12},{12,4},... | collective-permute-start | bytes 786440 | tf_op jit(solution)/shard_map/ppermute | solution.py:85
  1120.3 16.3 %copy-start.11 = (bf16[128,2048]{1,0:T(8,128)(2,1)S(1)}, bf16[128,2048]{1,0:T(8,128)(2,1)}, u32[]{:S(2)}) copy-start(bf16[128,2048]{1,0:T(8,128)(2,1)} %reduce-scatter.6.cloned.1.call-done) | copy-start | bytes 1572868
  (10 other events, 10.3 us)
Sparse Core Ops, SparseCore 0:
  9.6 84.8 all-gather.12
  96.6 89.3 all-gather.14
  192.1 74.7 all-gather.16
  458.8 91.3 reduce-scatter.3
  555.8 51.5 all-gather.18
  635.7 160.0 reduce-scatter.5
  797.3 115.3 all-gather.20
  914.7 33.9 all-gather.26
  950.9 56.9 all-gather.24
  1009.8 30.9 all-gather.22
  1043.0 93.4 reduce-scatter.7

commit v2 on v1

v2 whole, which is shorter than its diff:
```python
import functools
import math

import jax
import jax.numpy as jnp
from jax import lax
from jax.experimental import pallas as pl
from jax.experimental.pallas import tpu as pltpu
from jax.sharding import Mesh, PartitionSpec as P

HD = 128

epsilon = 1e-06
theta_base = 500000.0

OWNERS = ("zh", "zl", "y", "c")
EVERY = ("x", "zh", "zl", "y", "c")
MEMBERS = 16
SIDES = 8
SIDE_BITS = {"zl": 4, "y": 2, "c": 1}
BITS = {"x": 8, "zl": 4, "y": 2, "c": 1}
MESH = pl.DeviceIdType.MESH
MIB = 1 << 20


def thirds(rows):
    unit = rows // 8
    return (
        (("x", "y", "zl"), 0, 3 * unit),
        (("y", "zl", "x"), 3 * unit, 3 * unit),
        (("zl", "x", "y"), 6 * unit, 2 * unit),
    )


def halves(rows, *order):
    return ((order, 0, rows // 2), (order, rows // 2, rows // 2))


PEERS = [tuple(n for n in BITS if m & BITS[n]) for m in range(1, MEMBERS)]
SIDE_PEERS = [tuple(n for n in SIDE_BITS if m & SIDE_BITS[n]) for m in range(SIDES)]


def place():
    return {name: lax.axis_index(name) for name in EVERY}


def flip(here, *names):
    return {name: 1 - here[name] for name in names}


def with_bits(here, names, bits=BITS):
    index = 0
    for name, bit in bits.items():
        index = index + bit * ((1 - here[name]) if name in names else here[name])
    return index


def subset(order, mask):
    return tuple(name for k, name in enumerate(order) if mask >> k & 1)


def greet(devices):
    barrier = pltpu.get_barrier_semaphore()
    for device in devices:
        pl.semaphore_signal(barrier, inc=1, device_id=device, device_id_type=MESH)
    pl.semaphore_wait(barrier, len(devices))


def owner_at(here, groups, step, names):
    device = flip(here, *names)
    if step:
        device["zh"] = lax.rem(here["zh"] + step, groups)
    return device


class Load:
    def __init__(self, kind, source, parts=1):
        self.kind = kind
        self.source = source
        self.parts = parts
        groups = self.groups = lax.axis_size("zh")
        shape, kept = source.shape, source.dtype
        if kind == "columns":
            self.rows = shape[0]
            self.piece = shape[1] // (parts * MEMBERS)
            shape = (groups * SIDES * shape[0], parts * self.piece)
        elif kind == "owners":
            self.rows = shape[0] // (groups * SIDES)
            self.piece = shape[1] // parts
            shape = (groups, self.rows, parts * SIDES * self.piece)
        elif kind == "plane":
            shape = (groups * SIDES,) + shape
        elif kind == "cube":
            shape = (MEMBERS,) + shape
        self.out = jax.ShapeDtypeStruct(shape, kept)
        self.space = pltpu.VMEM if kind in ("plane", "cube") else pl.ANY
        self.count = len(self.moves(None))

    def moves(self, here):
        if self.kind == "zh":
            return [((1, ()), 0)]
        if self.kind == "x":
            return [((0, ("x",)), 0)]
        if self.kind == "cube":
            return [((0, names), 0) for names in [()] + PEERS]
        return [
            ((step, names), part)
            for step in range(self.groups)
            for names in SIDE_PEERS
            for part in range(self.parts)
        ]

    def scratch(self):
        return [pltpu.SemaphoreType.DMA((self.count,)), pltpu.SemaphoreType.DMA((self.count,))]

    def devices(self, here):
        return [
            (step, names) for (step, names), part in self.moves(here) if part == 0 and (step or names)
        ]

    def views(self, here, src, dst, step, names, part):
        if self.kind in ("zh", "x"):
            return src, dst, dst
        if self.kind == "cube":
            return src, dst.at[with_bits(here, ())], dst.at[with_bits(here, names)]
        groups, side = self.groups, with_bits(here, (), SIDE_BITS)
        other = with_bits(here, names, SIDE_BITS)
        there = lax.rem(here["zh"] + step, groups)
        whence = lax.rem(here["zh"] + groups - step, groups)
        me, he = here["zh"] * SIDES + side, whence * SIDES + other
        if self.kind == "plane":
            return src, dst.at[me], dst.at[he]
        rows, piece = self.rows, self.piece

        def at(start, size):
            return pl.ds(pl.multiple_of(start, size), size)

        if self.kind == "columns":
            first = part * MEMBERS + here["x"] * SIDES + other
            columns = pl.ds(part * piece, piece)
            return (
                src.at[:, at(first * piece, piece)],
                dst.at[at(me * rows, rows), columns],
                dst.at[at(he * rows, rows), columns],
            )
        target = there * SIDES + other
        return (
            src.at[at(target * rows, rows), pl.ds(part * piece, piece)],
            dst.at[here["zh"], :, at((part * SIDES + side) * piece, piece)],
            dst.at[whence, :, at((part * SIDES + other) * piece, piece)],
        )

    def copies(self, here, src, dst, send, recv):
        result = []
        for index, ((step, names), part) in enumerate(self.moves(here)):
            source, target, landing = self.views(here, src, dst, step, names, part)
            if not step and not names:
                copy = pltpu.make_async_copy(source, target, send.at[index])
                result.append((copy, None))
                continue
            copy = pltpu.make_async_remote_copy(
                src_ref=source, dst_ref=target, send_sem=send.at[index], recv_sem=recv.at[index],
                device_id=owner_at(here, self.groups, step, names), device_id_type=MESH,
            )
            result.append((copy, pltpu.make_async_copy(landing, landing, recv.at[index])))
        return result


class Cargo:
    def __init__(self, loads):
        self.loads = loads
        self.n = len(loads)
        self.sources = [load.source for load in loads]
        self.specs = [pl.BlockSpec(memory_space=load.space) for load in loads]
        self.outs = [load.out for load in loads]
        self.scratch = [s for load in loads for s in load.scratch()]

    def greet(self, here, names):
        reached = {(0, n) for n in names}
        for load in self.loads:
            reached |= set(load.devices(here))
        groups = lax.axis_size("zh")
        greet([owner_at(here, groups, step, n) for step, n in sorted(reached)])

    def start(self, here, sources, targets, semaphores):
        self.copies = []
        for k, load in enumerate(self.loads):
            self.copies += load.copies(
                here, sources[k], targets[k], semaphores[2 * k], semaphores[2 * k + 1]
            )
        for copy, _ in self.copies:
            copy.start()

    def wait(self):
        for copy, landing in self.copies:
            if landing is None:
                copy.wait()
            else:
                landing.wait()
        for copy, landing in self.copies:
            if landing is not None:
                copy.wait_send()


NEAR = [("x",), ("zl",), ("y",), ("c",)]


def call(body, name, ident, cargo, operand, out, out_space, scratch, vmem=32):
    return pl.pallas_call(
        body,
        out_shape=[out] + cargo.outs,
        in_specs=[pl.BlockSpec(memory_space=pl.ANY)] + cargo.specs,
        out_specs=[pl.BlockSpec(memory_space=out_space)] + cargo.specs,
        scratch_shapes=scratch + cargo.scratch,
        compiler_params=pltpu.CompilerParams(
            collective_id=ident, has_side_effects=True, vmem_limit_bytes=vmem * MIB
        ),
        cost_estimate=pl.CostEstimate(flops=0, bytes_accessed=100 * MIB, transcendentals=0),
        name=name,
    )(operand, *cargo.sources)


def gather_kernel(orders, cargo, x_ref, *refs):
    n = cargo.n
    sources, o_ref, targets = refs[:n], refs[n], refs[n + 1 : 2 * n + 1]
    send_sem, recv_sem, core_send, core_recv, own_sem = refs[2 * n + 1 : 2 * n + 6]
    here = place()
    spans = [pl.ds(r0, size) for _, r0, size in orders]
    orders = [o for o, _, _ in orders]
    pieces = range(len(orders))
    cargo.greet(here, NEAR)
    own = pltpu.make_async_copy(x_ref, o_ref.at[with_bits(here, ())], own_sem)

    def piece_of(p, mask):
        spot = o_ref.at[with_bits(here, subset(orders[p], mask)), spans[p]]
        return (x_ref.at[spans[p]] if mask == 0 else spot), spot

    def over(p, mask, k):
        source, spot = piece_of(p, mask)
        return pltpu.make_async_remote_copy(
            src_ref=source, dst_ref=spot,
            send_sem=send_sem.at[p, mask | 1 << k], recv_sem=recv_sem.at[p, mask | 1 << k],
            device_id=flip(here, orders[p][k]), device_id_type=MESH,
        )

    def across(p, mask):
        source, spot = piece_of(p, mask)
        return pltpu.make_async_remote_copy(
            src_ref=source, dst_ref=spot,
            send_sem=core_send.at[p, mask], recv_sem=core_recv.at[p, mask],
            device_id=flip(here, "c"), device_id_type=MESH,
        )

    sent = []
    for mask in range(8):
        for p in pieces:
            if mask:
                _, spot = piece_of(p, mask)
                pltpu.make_async_copy(spot, spot, recv_sem.at[p, mask]).wait()
            for k in range(mask.bit_length(), 3):
                sent.append(over(p, mask, k))
                sent[-1].start()
        for p in pieces:
            sent.append(across(p, mask))
            sent[-1].start()
        if mask == 0:
            own.start()
            cargo.start(here, sources, targets, refs[2 * n + 6 :])
    for mask in range(8):
        for p in pieces:
            spot = o_ref.at[with_bits(here, subset(orders[p], mask) + ("c",)), spans[p]]
            pltpu.make_async_copy(spot, spot, core_recv.at[p, mask]).wait()
    for copy in sent:
        copy.wait_send()
    own.wait()
    cargo.wait()


def gather_cube(block, ident, loads=(), orders=None):
    rows, width = block.shape
    orders = orders or thirds(rows)
    cargo = Cargo(list(loads))
    out = call(
        functools.partial(gather_kernel, orders, cargo),
        "gather_cube", ident, cargo, block,
        jax.ShapeDtypeStruct((MEMBERS, rows, width), block.dtype), pl.ANY,
        [pltpu.SemaphoreType.DMA((len(orders), 8))] * 4 + [pltpu.SemaphoreType.DMA(())],
    )
    return [out[0].reshape(MEMBERS * rows, width)] + list(out[1:])


def scatter_kernel(orders, cargo, p_ref, *refs):
    n = cargo.n
    sources, o_ref, targets = refs[:n], refs[n], refs[n + 1 : 2 * n + 1]
    acc, rcore, came, load_sem, core_send, core_recv, send_sem, recv_sem = refs[
        2 * n + 1 : 2 * n + 9
    ]
    here = place()
    spans = [pl.ds(r0, size) for _, r0, size in orders]
    orders = [o for o, _, _ in orders]
    pieces = range(len(orders))
    cargo.greet(here, NEAR)

    def away(p, mask):
        names = subset(orders[p], mask)
        return pltpu.make_async_remote_copy(
            src_ref=p_ref.at[with_bits(here, names + ("c",)), spans[p]],
            dst_ref=rcore.at[mask, spans[p]],
            send_sem=core_send.at[p, mask], recv_sem=core_recv.at[p, mask],
            device_id=flip(here, "c"), device_id_type=MESH,
        )

    def fetch(p, mask):
        names = subset(orders[p], mask)
        return pltpu.make_async_copy(
            p_ref.at[with_bits(here, names), spans[p]], acc.at[mask, spans[p]], load_sem.at[p, mask]
        )

    sequence = [7, 3, 5, 1, 6, 2, 4, 0]
    sent = []
    for mask in sequence:
        for p in pieces:
            sent.append(away(p, mask))
            sent[-1].start()
            fetch(p, mask).start()
    cargo.start(here, sources, targets, refs[2 * n + 9 :])

    def over(p, mask):
        k = (mask & -mask).bit_length() - 1
        return pltpu.make_async_remote_copy(
            src_ref=acc.at[mask, spans[p]], dst_ref=came.at[mask, spans[p]],
            send_sem=send_sem.at[p, mask], recv_sem=recv_sem.at[p, mask],
            device_id=flip(here, orders[p][k]), device_id_type=MESH,
        )

    def add(p, mask, other):
        acc[mask, spans[p]] = acc[mask, spans[p]] + other[...]

    for mask in sequence:
        for p in pieces:
            fetch(p, mask).wait()
            away(p, mask).wait_recv()
            add(p, mask, rcore.at[mask, spans[p]])
            if mask & 1:
                sent.append(over(p, mask))
                sent[-1].start()
    for k in range(3):
        low = 1 << k
        for mask in [m for m in (6, 2, 4, 0) if m & (2 * low - 1) == 0]:
            for p in pieces:
                over(p, mask | low).wait_recv()
                if mask == 0 and k == 2:
                    o_ref[spans[p]] = acc[0, spans[p]].astype(jnp.float32) + came[
                        4, spans[p]
                    ].astype(jnp.float32)
                    continue
                add(p, mask, came.at[mask | low, spans[p]])
                if mask & (2 * low):
                    sent.append(over(p, mask))
                    sent[-1].start()
    for copy in sent:
        copy.wait_send()
    cargo.wait()


def scatter_cube(partial, ident, loads=(), orders=None):
    total, width = partial.shape
    rows = total // MEMBERS
    orders = orders or thirds(rows)
    cargo = Cargo(list(loads))
    return call(
        functools.partial(scatter_kernel, orders, cargo),
        "scatter_cube", ident, cargo, partial.astype(jnp.bfloat16).reshape(MEMBERS, rows, width),
        jax.ShapeDtypeStruct((rows, width), jnp.float32), pltpu.VMEM,
        [pltpu.VMEM((8, rows, width), jnp.bfloat16)] * 3
        + [pltpu.SemaphoreType.DMA((len(orders), 8))] * 5,
    )


def carry_kernel(cargo, *refs):
    n = cargo.n
    here = place()
    cargo.greet(here, [])
    cargo.start(here, refs[:n], refs[n : 2 * n], refs[2 * n :])
    cargo.wait()


def carry(ident, loads):
    cargo = Cargo(list(loads))
    return pl.pallas_call(
        functools.partial(carry_kernel, cargo),
        out_shape=cargo.outs,
        in_specs=cargo.specs,
        out_specs=cargo.specs,
        scratch_shapes=cargo.scratch,
        compiler_params=pltpu.CompilerParams(collective_id=ident, has_side_effects=True),
        cost_estimate=pl.CostEstimate(flops=0, bytes_accessed=50 * MIB, transcendentals=0),
        name="carry",
    )(*cargo.sources)


def exchange_kernel(v_ref, o_ref, slots, send_sem, recv_sem):
    here = place()
    greet([flip(here, *names) for names in PEERS])
    copies = []
    for m in range(1, MEMBERS):
        copies.append(pltpu.make_async_remote_copy(
            src_ref=v_ref, dst_ref=slots.at[m], send_sem=send_sem.at[m], recv_sem=recv_sem.at[m],
            device_id=flip(here, *PEERS[m - 1]), device_id_type=MESH,
        ))
        copies[-1].start()
    for copy in copies:
        copy.wait_recv()
    slots[0] = v_ref[...]
    terms = [slots[m] for m in range(MEMBERS)]
    while len(terms) > 1:
        terms = [terms[2 * i] + terms[2 * i + 1] for i in range(len(terms) // 2)]
    o_ref[...] = terms[0]
    for copy in copies:
        copy.wait_send()


def sum_cube(values, ident):
    shape = values.shape
    return pl.pallas_call(
        exchange_kernel,
        out_shape=jax.ShapeDtypeStruct(shape, jnp.float32),
        in_specs=[pl.BlockSpec(memory_space=pltpu.VMEM)],
        out_specs=pl.BlockSpec(memory_space=pltpu.VMEM),
        scratch_shapes=[
            pltpu.VMEM((MEMBERS,) + shape, jnp.float32),
            pltpu.SemaphoreType.DMA((MEMBERS,)),
            pltpu.SemaphoreType.DMA((MEMBERS,)),
        ],
        compiler_params=pltpu.CompilerParams(collective_id=ident, has_side_effects=True),
        cost_estimate=pl.CostEstimate(flops=0, bytes_accessed=20 * MIB, transcendentals=0),
        name="sum_cube",
    )(values)


def rope_tables(positions):
    frequency = theta_base ** (-2.0 * jnp.arange(HD // 2).astype(jnp.float32) / HD)
    angles = positions[:, None] * frequency[None, :]
    return (jnp.cos(angles), jnp.sin(angles))


def rotate(values, cos_table, sin_table):
    half_width = values.shape[-1] // 2
    former = values[..., :half_width]
    latter = values[..., half_width:]
    return jnp.concatenate(
        [former * cos_table - latter * sin_table, latter * cos_table + former * sin_table], axis=-1
    )


def normalize(values, scales):
    inverse = lax.rsqrt(jnp.mean(values * values, axis=-1, keepdims=True) + epsilon)
    return (values * inverse * scales, inverse)


def norm_back(upstream, values, inverse, scales):
    unit_rows = values * inverse
    scaled = upstream * scales
    value_grad = inverse * (
        scaled - unit_rows * jnp.mean(scaled * unit_rows, axis=-1, keepdims=True)
    )
    return (value_grad, jnp.sum(upstream * unit_rows, axis=0))


def contract_last(operand, matrix):
    return lax.dot_general(
        operand, matrix, (((1,), (1,)), ((), ())), preferred_element_type=jnp.float32
    )


def contract_first(operand, matrix):
    return lax.dot_general(
        operand, matrix, (((0,), (0,)), ((), ())), preferred_element_type=jnp.float32
    )


def row_sums(pair, ident):
    total = pair[0].shape[0]
    flat = jnp.concatenate([v.reshape(total // 128, 128) for v in pair], axis=0)
    summed = sum_cube(flat, ident).reshape(2, total, 1)
    return summed[0], summed[1]


def owned_sum(terms):
    return jnp.sum(terms.astype(jnp.float32), axis=0).astype(jnp.bfloat16)


def whole_rows(mine, came, parts):
    rows = mine.shape[0]
    first = lax.axis_index("x") == 0
    mine, came = (v.reshape(rows, parts, -1) for v in (mine, came))
    both = [jnp.where(first, mine, came), jnp.where(first, came, mine)]
    return jnp.stack(both, axis=2).reshape(rows, -1).astype(jnp.float32)


def heads_are_owners(rows):
    return lax.axis_size("zh") == 2 and rows == HD


def gathered_head_rows(weight):
    full = lax.all_gather(weight, OWNERS, axis=0, tiled=True)
    head = lax.axis_index(("x", "zl", "y", "c"))
    return lax.dynamic_slice_in_dim(full, head * HD, HD, axis=0)


def summed_head_rows(grad_rows, rows):
    head = lax.axis_index(("x", "zl", "y", "c"))
    full = jnp.zeros((MEMBERS * HD, grad_rows.shape[1]), jnp.float32)
    full = lax.dynamic_update_slice_in_dim(full, grad_rows, head * HD, axis=0)
    full = lax.psum(full, EVERY)
    return lax.dynamic_slice_in_dim(full, lax.axis_index(OWNERS) * rows, rows, axis=0)


def silu_grads(hidden_grad, gate_part, up_part):
    sigmoid_gate = jax.nn.sigmoid(gate_part)
    gate_grad = hidden_grad * up_part * sigmoid_gate * (1.0 + gate_part * (1.0 - sigmoid_gate))
    up_grad = hidden_grad * gate_part * sigmoid_gate
    return gate_grad.astype(jnp.bfloat16), up_grad.astype(jnp.bfloat16)


def shards(tokens, w_qkv, w_out, w_gate_up, w_down_t, gains, starts, cotangent):
    count_rows, width = tokens.shape
    owned = gains.shape[0]
    groups = lax.axis_size("zh")
    total = MEMBERS * count_rows
    score_scale = 1.0 / math.sqrt(HD)
    direct = heads_are_owners(owned)
    local_rows = jnp.arange(count_rows, dtype=jnp.int32)
    seq_begin = lax.cummax(jnp.where(starts == 1, local_rows, 0), axis=0)

    gain_part = jnp.pad(gains.astype(jnp.float32).T, ((0, 4), (0, 0)))
    begin_part = jnp.broadcast_to(seq_begin.astype(jnp.float32)[None, :], (8, count_rows))
    loads = [Load("plane", gain_part), Load("cube", begin_part), Load("columns", w_qkv, 3)]
    if direct:
        loads.append(Load("zh", w_out))
    tokens_all, gain_all, begin_all, qkv_cols, *out_other = gather_cube(
        tokens, 1, loads, halves(count_rows, "zl", "y", "x")
    )
    same = lax.axis_index("x") == lax.axis_index("zh")
    if direct:
        out_rows = jnp.where(same, w_out, out_other[0])
    else:
        out_rows = gathered_head_rows(w_out)
    gain_rows = gain_all[:, :4].transpose(1, 0, 2).reshape(4, width)
    begin_all = begin_all[:, 0]
    head = lax.axis_index(("x", "zl", "y", "c"))
    head_gains = lax.dynamic_slice_in_dim(gain_rows, head * HD, HD, axis=1)
    rows_f32 = local_rows.astype(jnp.float32)
    positions = (rows_f32[None, :] - begin_all).reshape(total)
    cos_table, sin_table = rope_tables(positions)
    allowed = (rows_f32[None, None, :] <= rows_f32[None, :, None]) & (
        rows_f32[None, None, :] >= begin_all[:, :, None]
    )

    def blocks(values):
        return values.reshape(MEMBERS, count_rows, HD)

    projected = jnp.dot(tokens_all, qkv_cols, preferred_element_type=jnp.float32)
    query_raw = projected[:, :HD]
    key_raw = projected[:, HD : 2 * HD]
    value_bf = blocks(projected[:, 2 * HD :].astype(jnp.bfloat16))
    query_sq, key_sq = row_sums(
        (jnp.sum(query_raw * query_raw, axis=1), jnp.sum(key_raw * key_raw, axis=1)), 2
    )
    query_inv = lax.rsqrt(query_sq / width + epsilon)
    key_inv = lax.rsqrt(key_sq / width + epsilon)
    query_unit = query_raw * query_inv
    key_unit = key_raw * key_inv
    query_bf = blocks(rotate(query_unit * head_gains[0], cos_table, sin_table).astype(jnp.bfloat16))
    key_bf = blocks(rotate(key_unit * head_gains[1], cos_table, sin_table).astype(jnp.bfloat16))
    scores = (
        jnp.einsum("bqd,bkd->bqk", query_bf, key_bf, preferred_element_type=jnp.float32)
        * score_scale
    )
    scores = jnp.where(allowed, scores, -1e30)
    exponent = jnp.exp(scores - jnp.max(scores, axis=-1, keepdims=True))
    attention_f32 = exponent / jnp.sum(exponent, axis=-1, keepdims=True)
    attention = attention_f32.astype(jnp.bfloat16)
    attended = (
        jnp.einsum("bqk,bkd->bqd", attention, value_bf, preferred_element_type=jnp.float32)
        .reshape(total, HD)
        .astype(jnp.bfloat16)
    )
    feed_width = w_down_t.shape[1]
    x_most = halves(count_rows, "x", "y", "zl")
    x_last = halves(count_rows, "zl", "y", "x")
    y_last = halves(count_rows, "zl", "x", "y")
    branch, gate_cols = scatter_cube(
        jnp.dot(attended, out_rows, preferred_element_type=jnp.float32),
        3, [Load("columns", w_gate_up[:, :feed_width])], x_most,
    )
    branch_norm, branch_inv = normalize(branch, gain_rows[2])
    middle = tokens.astype(jnp.float32) + branch_norm
    middle_all, up_cols, down_cols = gather_cube(
        middle.astype(jnp.bfloat16), 4,
        [Load("columns", w_gate_up[:, feed_width:]), Load("columns", w_down_t)], x_last,
    )
    gate_part = jnp.dot(middle_all, gate_cols, preferred_element_type=jnp.float32)
    up_part = jnp.dot(middle_all, up_cols, preferred_element_type=jnp.float32)
    hidden_bf = (gate_part * jax.nn.sigmoid(gate_part) * up_part).astype(jnp.bfloat16)
    (feed_out,) = scatter_cube(contract_last(hidden_bf, down_cols), 5)
    feed_norm, feed_inv = normalize(feed_out, gain_rows[3])
    mixed = (middle + feed_norm).astype(jnp.bfloat16)

    upstream = cotangent.astype(jnp.float32)
    feed_grad, gain_feed = norm_back(upstream, feed_out, feed_inv, gain_rows[3])
    (feed_all,) = gather_cube(feed_grad.astype(jnp.bfloat16), 6)
    down_grad = contract_first(feed_all, hidden_bf).astype(jnp.bfloat16)
    hidden_grad = jnp.dot(feed_all, down_cols, preferred_element_type=jnp.float32)
    gate_bf, up_bf = silu_grads(hidden_grad, gate_part, up_part)
    gate_grad = contract_first(middle_all, gate_bf).astype(jnp.bfloat16)
    up_grad = contract_first(middle_all, up_bf).astype(jnp.bfloat16)
    middle_part = contract_last(gate_bf, gate_cols) + contract_last(up_bf, up_cols)
    middle_sum, down_terms, gate_terms = scatter_cube(
        middle_part, 7, [Load("owners", down_grad), Load("owners", gate_grad)], x_most
    )
    middle_grad = upstream + middle_sum
    branch_grad, gain_branch = norm_back(middle_grad, branch, branch_inv, gain_rows[2])
    down_sum = owned_sum(down_terms)
    gate_sum = owned_sum(gate_terms)
    branch_all, up_terms, down_other, gate_other = gather_cube(
        branch_grad.astype(jnp.bfloat16), 8,
        [Load("owners", up_grad), Load("x", down_sum), Load("x", gate_sum)], y_last,
    )
    up_sum = owned_sum(up_terms)
    out_grad = contract_first(attended, branch_all)
    attended_grad = blocks(contract_last(branch_all, out_rows).astype(jnp.bfloat16))
    prob_grad = jnp.einsum(
        "bqd,bkd->bqk", attended_grad, value_bf, preferred_element_type=jnp.float32
    )
    score_bf = (
        attention_f32 * (prob_grad - jnp.sum(attention_f32 * prob_grad, axis=-1, keepdims=True))
    ).astype(jnp.bfloat16)
    value_grad = jnp.einsum(
        "bqk,bqd->bkd", attention, attended_grad, preferred_element_type=jnp.float32
    ).reshape(total, HD)
    query_grad = (
        jnp.einsum("bqk,bkd->bqd", score_bf, key_bf, preferred_element_type=jnp.float32)
        * score_scale
    ).reshape(total, HD)
    key_grad = (
        jnp.einsum("bqk,bqd->bkd", score_bf, query_bf, preferred_element_type=jnp.float32)
        * score_scale
    ).reshape(total, HD)
    query_grad = rotate(query_grad, cos_table, -sin_table)
    key_grad = rotate(key_grad, cos_table, -sin_table)
    query_scaled = query_grad * head_gains[0]
    key_scaled = key_grad * head_gains[1]
    query_dot, key_dot = row_sums(
        (jnp.sum(query_scaled * query_unit, axis=1), jnp.sum(key_scaled * key_unit, axis=1)), 9
    )
    query_raw_grad = query_inv * (query_scaled - query_unit * (query_dot / width))
    key_raw_grad = key_inv * (key_scaled - key_unit * (key_dot / width))
    projected_bf = jnp.concatenate([query_raw_grad, key_raw_grad, value_grad], axis=1).astype(
        jnp.bfloat16
    )
    qkv_grad = contract_first(tokens_all, projected_bf).astype(jnp.bfloat16)

    gain_head = jnp.stack(
        [jnp.sum(query_grad * query_unit, axis=0), jnp.sum(key_grad * key_unit, axis=0)]
    )
    gain_terms = jnp.concatenate(
        [
            lax.dynamic_update_slice_in_dim(
                jnp.zeros((2, width), jnp.float32), gain_head, head * HD, axis=1
            ),
            jnp.stack([gain_branch, gain_feed]),
        ]
    )
    lanes = -(-owned // 128) * 128
    gain_terms = jnp.pad(
        gain_terms.reshape(4, groups * SIDES, owned).transpose(1, 0, 2),
        ((0, 0), (0, 4), (0, lanes - owned)),
    ).reshape(groups * SIDES * 8, lanes)
    loads = [Load("owners", qkv_grad, 3), Load("x", up_sum), Load("owners", gain_terms)]
    if direct:
        out_bf = out_grad.astype(jnp.bfloat16)
        loads.append(Load("zh", out_bf))
    tokens_sum, qkv_terms, up_other, gain_came, *out_came = scatter_cube(
        contract_last(projected_bf, qkv_cols), 10, loads, x_most
    )
    grad_tokens = middle_grad + tokens_sum
    qkv_sum = owned_sum(qkv_terms)
    gain_sum = jnp.sum(gain_came.reshape(groups, 8, SIDES, lanes), axis=(0, 2))
    loads = [Load("x", qkv_sum), Load("x", gain_sum)]
    if direct:
        out_sum = (out_bf.astype(jnp.float32) + out_came[0].astype(jnp.float32)).astype(
            jnp.bfloat16
        )
        loads.append(Load("x", out_sum))
    qkv_other, gain_other, *out_other = carry(11, loads)
    if direct:
        grad_out = jnp.where(same, out_sum, out_other[0]).astype(jnp.float32)
    else:
        grad_out = summed_head_rows(out_grad, owned)
    grad_qkv = whole_rows(qkv_sum, qkv_other, 3)
    grad_gate_up = jnp.concatenate(
        [whole_rows(gate_sum, gate_other, 1), whole_rows(up_sum, up_other, 1)], axis=1
    )
    grad_down_t = whole_rows(down_sum, down_other, 1)
    grad_gains = (gain_sum + gain_other)[:4, :owned].T
    return (mixed, grad_tokens, grad_qkv, grad_out, grad_gate_up, grad_down_t, grad_gains)


def solution(mesh):
    sizes = dict(mesh.shape)
    groups = sizes["fsdp"] // SIDES
    finer = Mesh(mesh.devices.reshape(2, groups, 2, 2, 2), EVERY)
    return jax.shard_map(
        shards,
        mesh=finer,
        in_specs=(
            P(EVERY, None),
            P(OWNERS, None),
            P(OWNERS, None),
            P(OWNERS, None),
            P(OWNERS, None),
            P(OWNERS, None),
            P(EVERY),
            P(EVERY, None),
        ),
        out_specs=(
            P(EVERY, None),
            P(EVERY, None),
            P(OWNERS, None),
            P(OWNERS, None),
            P(OWNERS, None),
            P(OWNERS, None),
            P(OWNERS, None),
        ),
        check_vma=False,
    )
```

time: 1160 us -> 854 us (0.74)
  Pallas kernels: 0 us -> 620 us
  waiting for transfers between devices: 588 us -> 0 us
  blocking collectives: 165 us -> 0 us
  local copies, waits for them, and re-layouts: 147 us -> 66.8 us
  starting transfers between devices: 50.8 us -> 0 us
  other arithmetic: 65.2 us -> 49.1 us
  between operations: 15.1 us -> 2.03 us
    pallas_call x0 -> x11, Pallas kernels: none -> 620 us  [the longest x8 571 us: call(): pl.pallas_call(body, out_shape=[out] + cargo.outs, in_specs=[pl.BlockSpec...]
    ppermute x7 -> x0, waiting for transfers between devices: 256 us -> none  [the longest x3 173 us: columns_of(): came = lax.ppermute(half, 'zh', [(0, 1), (1, 0)])]
    all_to_all x8 -> x0, waiting for transfers between devices: 146 us -> none  [the longest x3 90.5 us: owners_sum(): came = lax.all_to_all(blocks, SIDE, 1, 1, tiled=True)]
    reduce_scatter x3 -> x0, waiting for transfers between devices: 110 us -> none  [scatter_cube(): lax.psum_scatter(partial.astype(jnp.bfloat16), CUBE, scatter_dimension=0,...]
    all_gather x8 -> x0, waiting for transfers between devices: 74 us -> none  [the longest x4 54 us: gather_cube(): return lax.all_gather(block, CUBE, axis=0, tiled=True)]
    all_to_all x2 -> x0, blocking collectives: 63.1 us -> none  [the longest x1 39.9 us: columns_of(): came = lax.all_to_all(blocks, SIDE, 0, 0, tiled=True)]
    all_gather x2 -> x0, blocking collectives: 56.9 us -> none  [the longest x1 47.3 us: shards(): full_gains = lax.all_gather(gains, OWNERS, axis=0, tiled=True)]
    psum x1 -> x0, blocking collectives: 44.6 us -> none  [shards(): gain_sums = lax.psum(gain_terms, EVERY)]
  transfers between devices with their start and end apart: 26 -> 0, of which waited for: 15 -> 0; matrix products, arithmetic and copies ran while one was open for 22% -> 0% of each run, Pallas kernels for 0% -> 0%
where the time goes in v2:
time: 854 us; the launch traced here: 844 us
  Pallas kernels  620 us (73%)
  matrix products  106 us (12%)
  local copies, waits for them, and re-layouts  66.8 us (8%)
  other arithmetic  49.1 us (6%)
    pallas_call x8, Pallas kernels, call(): pl.pallas_call(body, out_shape=[out] + cargo.outs, in_specs=[pl.BlockSpec...  571 us
    unnamed x143, local copies, waits for them, and re-layouts  45.3 us
    dot_general x5, matrix products, contract_last(): lax.dot_general(operand, matrix, (((1,), (1,)), ((), ())), preferred_elem...  39.1 us
    dot_general x5, matrix products, contract_first(): lax.dot_general(operand, matrix, (((0,), (0,)), ((), ())), preferred_elem...  30.6 us
    pallas_call x1, Pallas kernels, carry(): pl.pallas_call(functools.partial(carry_kernel, cargo), out_shape=cargo.ou...  30.2 us
    pallas_call x2, Pallas kernels, sum_cube(): pl.pallas_call(exchange_kernel, out_shape=jax.ShapeDtypeStruct(shape, jnp...  18.2 us

profile of v2, /device:TPU:0, one launch (start us, length us, event | category | flops | bytes accessed | tf_op | source)
XLA Modules:
  0.0 843.6 jit_solution(7437425226626453829)
XLA Ops:
  4.5 1.4 copy-done.18
  5.9 68.6 %gather_cube.4 = (bf16[16,128,2048]{2,1,0:T(8,128)(2,1)S(1)}, f32[16,8,128]{2,1,0:T(8,128)S(1)}, f32[16,8,128]{2,1,0:T(8,128)S(1)}, bf16[2048,384]{1,0:T(8,128)(2,1)S(1)}, bf16[128,2048]{1,0:T(8,128)(2,1)S(1)}) custom-call(bf16[128,2048]{1,0:T(8,128)(2,1)S(1)} %copy-done.4, f32[8,128]{1,0:T(8,128)S(1)} %pad_convert_fusion.refs_0_, ...), custom_call_target="tpu_custom_call" | custom-call | bytes 104857600 | tf_op jit(solution)/shard_map/gather_cube/pallas_call | solution.py:209
  74.6 3.6 fusion.62
  78.4 1.5 copy-done.38
  80.5 9.1 %sum_cube.2 = f32[32,128]{1,0:T(8,128)} custom-call(f32[32,128]{1,0:T(8,128)} %pad_maximum_fusion.17.v_ref), custom_call_target="tpu_custom_call" | custom-call | bytes 20971520 | tf_op jit(solution)/shard_map/sum_cube/pallas_call | solution.py:425
  90.4 1.8 fusion.30
  92.2 2.4 fusion.38
  95.9 1.9 fusion.61
  97.8 1.3 slice.166
  100.1 2.4 convolution_convert_fusion.9
  102.6 2.3 convolution_convert_fusion.2
  105.3 64.9 %scatter_cube.4 = (f32[128,2048]{1,0:T(8,128)S(1)}, bf16[2048,512]{1,0:T(8,128)(2,1)S(1)}) custom-call(bf16[16,128,2048]{2,1,0:T(8,128)(2,1)S(1)} %bitcast.121, bf16[128,8192]{1,0:T(8,128)(2,1)S(1)} %get-tuple-element.93.refs_0_), custom_call_target="tpu_custom_call" | custom-call | bytes 104857600 | tf_op jit(solution)/shard_map/scatter_cube/pallas_call | solution.py:209
  170.6 1.9 copy-done.11
  172.5 89.5 %gather_cube.5 = (bf16[16,128,2048]{2,1,0:T(8,128)(2,1)S(1)}, bf16[2048,512]{1,0:T(8,128)(2,1)S(1)}, bf16[2048,512]{1,0:T(8,128)(2,1)S(1)}) custom-call(bf16[128,2048]{1,0:T(8,128)(2,1)S(1)} %fusion.32.x_ref, bf16[128,8192]{1,0:T(8,128)(2,1)S(1)} %get-tuple-element.92.refs_0_, bf16[128,8192]{1,0:T(8,128)(2,1)S(1)} %copy-done.11), custom_call_target="tpu_custom_call" | custom-call | bytes 104857600 | tf_op jit(solution)/shard_map/gather_cube/pallas_call | solution.py:209
  262.0 4.6 fusion.63
  266.7 6.8 multiply_convert_fusion.2
  273.5 6.4 convolution_convert_fusion.1
  279.9 48.2 %scatter_cube.5 = f32[128,2048]{1,0:T(8,128)S(1)} custom-call(bf16[16,128,2048]{2,1,0:T(8,128)(2,1)S(1)} %bitcast.124), custom_call_target="tpu_custom_call" | custom-call | bytes 104857600 | tf_op jit(solution)/shard_map/scatter_cube/pallas_call | solution.py:209
  329.0 32.7 %gather_cube.6 = bf16[16,128,2048]{2,1,0:T(8,128)(2,1)S(1)} custom-call(bf16[128,2048]{1,0:T(8,128)(2,1)S(1)} %fusion.11.x_ref), custom_call_target="tpu_custom_call" | custom-call | bytes 104857600 | tf_op jit(solution)/shard_map/gather_cube/pallas_call | solution.py:209
  361.6 9.1 %multiply_convert_fusion = (bf16[2048,512]{1,0:T(8,128)(2,1)}, bf16[2048,512]{1,0:T(8,128)(2,1)S(1)}) fusion(f32[2048,512]{1,0:T(8,128)} %copy-done.68, f32[2048,512]{1,0:T(8,128)} %get-tuple-element.133, bf16[2048,2048]{1,0:T(8,128)(2,1)S(1)} %bitcast.125, bf16[2048,512]{1,0:T(8,128)(2,1)S(1)} %copy-done.35), kind=kOutput, calls=%fused_computation.6 | convolution fusion | flops 4308598784 | bytes 23068672 | tf_op jit(solution)/shard_map/dot_general | solution.py:614
  370.7 7.4 convolution_convert_fusion.3.refs_0_
  378.1 5.8 convolution_convert_fusion.4.refs_1_
  383.9 5.7 convolution_convert_fusion.5.refs_0_
  389.6 8.5 %fusion.64 = f32[2048,2048]{1,0:T(8,128)} fusion(bf16[2048,512]{1,0:T(8,128)(2,1)S(1)} %get-tuple-element.91, bf16[2048,512]{1,0:T(8,128)(2,1)S(1)} %copy-done.31), kind=kOutput, calls=%fused_computation.158 | convolution fusion | flops 4294967296 | bytes 20971520 | tf_op jit(solution)/shard_map/dot_general | solution.py:471
  398.1 15.0 %add_convert_fusion = bf16[2048,2048]{1,0:T(8,128)(2,1)} fusion(f32[2048,2048]{1,0:T(8,128)} %fusion.64, bf16[2048,512]{1,0:T(8,128)(2,1)} %get-tuple-element.90, bf16[2048,512]{1,0:T(8,128)(2,1)} %copy-done.32), kind=kOutput, calls=%fused_computation.1 | convolution fusion | flops 4303355904 | bytes 29360128 | tf_op jit(solution)/shard_map/dot_general | solution.py:471
  413.1 3.4 copy-done.2
  416.4 1.6 copy-done.16
  418.0 1.6 copy-done.17
  419.6 88.5 %scatter_cube.6 = (f32[128,2048]{1,0:T(8,128)S(1)}, bf16[2,128,4096]{2,1,0:T(8,128)(2,1)S(1)}, bf16[2,128,4096]{2,1,0:T(8,128)(2,1)S(1)}) custom-call(bf16[16,128,2048]{2,1,0:T(8,128)(2,1)S(1)} %bitcast.123, bf16[2048,512]{1,0:T(8,128)(2,1)S(1)} %copy-done.17, bf16[2048,512]{1,0:T(8,128)(2,1)S(1)} %copy-done.16), custom_call_target="tpu_custom_call" | custom-call | bytes 104857600 | tf_op jit(solution)/shard_map/scatter_cube/pallas_call | solution.py:209
  508.6 1.9 multiply_convert_fusion.6
  510.5 2.1 reduce_sum.197.refs_1_
  512.6 2.1 reduce_sum.198.refs_2_
  515.8 1.6 copy-done.13
  517.4 91.5 %gather_cube.7 = (bf16[16,128,2048]{2,1,0:T(8,128)(2,1)S(1)}, bf16[2,128,4096]{2,1,0:T(8,128)(2,1)S(1)}, bf16[128,4096]{1,0:T(8,128)(2,1)S(1)}, bf16[128,4096]{1,0:T(8,128)(2,1)S(1)}) custom-call(bf16[128,2048]{1,0:T(8,128)(2,1)S(1)} %copy-done.10, bf16[2048,512]{1,0:T(8,128)(2,1)S(1)} %copy-done.13, bf16[128,4096]{1,0:T(8,128)(2,1)S(1)} %reduce_sum.197.refs_1_, ...), custom_call_target="tpu_custom_call" | custom-call | bytes 104857600 | tf_op jit(solution)/shard_map/gather_cube/pallas_call | solution.py:209
  609.0 2.1 fusion.1.refs_3_
  611.1 2.4 convolution_convert_fusion.7
  616.4 2.6 fusion.33
  621.0 9.1 %sum_cube.3 = f32[32,128]{1,0:T(8,128)} custom-call(f32[32,128]{1,0:T(8,128)} %pad_maximum_fusion.18.v_ref), custom_call_target="tpu_custom_call" | custom-call | bytes 20971520 | tf_op jit(solution)/shard_map/sum_cube/pallas_call | solution.py:425
  630.9 3.6 multiply_convert_fusion.4
  634.4 3.6 convolution_convert_fusion.8
  638.0 2.0 copy.110
  640.1 9.6 %convolution_convert_fusion.6.refs_0_ = bf16[2048,384]{1,0:T(8,128)(2,1)} fusion(bf16[2048,2048]{1,0:T(8,128)(2,1)} %bitcast.129, bf16[2048,128]{0,1:T(8,128)(2,1)} %copy.110, bf16[2048,128]{0,1:T(8,128)(2,1)} %get-tuple-element.95, bf16[2048,128]{0,1:T(8,128)(2,1)} %get-tuple-element.94), kind=kOutput, calls=%fused_computation.13 | convolution fusion | flops 3226730496 | bytes 11534336 | tf_op jit(solution)/shard_map/dot_general | solution.py:477
  649.7 6.8 convolution_convert_fusion
  656.6 3.3 reduce_sum.202.refs_1_
  659.8 1.2 copy-done
  661.0 3.4 copy-done.3
  665.5 1.4 copy-done.20
  666.9 87.5 %scatter_cube.7 = (f32[128,2048]{1,0:T(8,128)S(1)}, bf16[2,128,3072]{2,1,0:T(8,128)(2,1)S(1)}, bf16[128,4096]{1,0:T(8,128)(2,1)S(1)}, f32[2,8,1024]{2,1,0:T(8,128)S(1)}, bf16[128,2048]{1,0:T(8,128)(2,1)S(1)}) custom-call(bf16[16,128,2048]{2,1,0:T(8,128)(2,1)S(1)} %bitcast.127, bf16[2048,384]{1,0:T(8,128)(2,1)S(1)} %copy-done.20, ...), custom_call_target="tpu_custom_call" | custom-call | bytes 104857600 | tf_op jit(solution)/shard_map/scatter_cube/pallas_call | solution.py:209
  756.4 1.1 add_convert_fusion.1.refs_2_
  757.7 2.9 reduce_sum.207.refs_0_
  761.2 30.2 %carry.1 = (bf16[128,3072]{1,0:T(8,128)(2,1)}, f32[8,128]{1,0:T(8,128)}, bf16[128,2048]{1,0:T(8,128)(2,1)}) custom-call(bf16[128,3072]{1,0:T(8,128)(2,1)} %reduce_sum.207.refs_0_, f32[8,128]{1,0:T(8,128)} %bitcast_reduce_fusion.refs_1_, bf16[128,2048]{1,0:T(8,128)(2,1)} %add_convert_fusion.1.refs_2_), custom_call_target="tpu_custom_call" | custom-call | bytes 52428800 | tf_op jit(solution)/shard_map/carry/pallas_call | solution.py:390
  792.7 3.1 select_bitcast_fusion.1
  795.8 2.3 maximum_convert_fusion.1
  798.1 5.6 copy.97
  803.7 5.7 copy.100
  809.5 1.5 pad_maximum_fusion
  811.0 4.2 copy.95
  815.5 2.5 copy.96
  818.0 6.1 maximum_convert_fusion
  824.1 9.1 %copy.99 = f32[128,16384]{1,0:T(8,128)} copy(f32[128,16384]{0,1:T(8,128)} %maximum_convert_fusion) | data formatting | bytes 16777216
  834.3 1.2 broadcast_select_fusion.1
  836.5 1.8 copy.94
  838.3 3.7 copy.98
  842.0 1.1 fusion.47
  (186 shorter events, 23.7 us)
Async XLA Ops:
  2.4 1.0 copy-start.4
  3.4 1.0 copy-start.7
  4.5 1.4 copy-start.18
  74.5 3.7 copy-start.29
  74.5 3.8 copy-start.36
  74.5 28.1 %copy-start.27 = (bf16[128,2048]{1,0:T(8,128)(2,1)}, bf16[128,2048]{1,0:T(8,128)(2,1)S(1)}, u32[]{:S(2)}) copy-start(bf16[128,2048]{1,0:T(8,128)(2,1)S(1)} %get-tuple-element.36) | copy-start | bytes 1572868
  78.3 1.7 copy-start.38
  94.9 5.2 copy-start.53
  95.2 4.9 copy-start.55
  95.5 4.6 copy-start.57
  95.8 3.3 copy-start.59
  100.1 2.5 copy-start.8
  102.6 2.4 copy-start.43
  102.6 2.4 copy-start.50
  105.2 65.1 %copy-start.5 = (bf16[128,2048]{1,0:T(8,128)(2,1)S(1)}, bf16[128,2048]{1,0:T(8,128)(2,1)}, u32[]{:S(2)}) copy-start(bf16[128,2048]{1,0:T(8,128)(2,1)} %x_ref.1) | copy-start | bytes 1572868
  170.2 91.9 %copy-start.30 = (bf16[2048,512]{1,0:T(8,128)(2,1)}, bf16[2048,512]{1,0:T(8,128)(2,1)S(1)}, u32[]{:S(2)}) copy-start(bf16[2048,512]{1,0:T(8,128)(2,1)S(1)} %get-tuple-element.39) | copy-start | bytes 6291460
  170.2 2.4 copy-start.11
  262.0 4.6 copy-start.33
  262.0 4.7 copy-start.32
  266.6 6.8 copy-start.68
  266.7 6.8 copy-start.34
  279.9 48.4 %copy-start.40 = (bf16[128,2048]{1,0:T(8,128)(2,1)S(1)}, bf16[128,2048]{1,0:T(8,128)(2,1)}, u32[]{:S(2)}) copy-start(bf16[128,2048]{1,0:T(8,128)(2,1)} %param.15) | copy-start | bytes 1572868
  329.0 32.7 %copy-start.35 = (bf16[2048,512]{1,0:T(8,128)(2,1)S(1)}, bf16[2048,512]{1,0:T(8,128)(2,1)}, u32[]{:S(2)}) copy-start(bf16[2048,512]{1,0:T(8,128)(2,1)} %copy-done.33) | copy-start | bytes 6291460
  378.1 5.8 copy-start.69
  383.9 5.7 copy-start.31
  413.1 3.4 copy-start.2
  416.4 1.6 copy-start.16
  418.0 1.6 copy-start.17
  508.2 2.3 copy-start.14
  508.2 2.3 copy-start.15
  514.7 1.0 copy-start.10
  515.8 1.6 copy-start.13
  517.4 91.6 %copy-start.44 = (bf16[16,128,128]{2,1,0:T(8,128)(2,1)S(1)}, bf16[16,128,128]{2,1,0:T(8,128)(2,1)}, u32[]{:S(2)}) copy-start(bf16[16,128,128]{2,1,0:T(8,128)(2,1)} %copy-done.43) | copy-start | bytes 1572868
  608.9 2.2 copy-start.12
  608.9 2.2 copy-start.21
  608.9 2.2 copy-start.22
  608.9 2.2 copy-start.9
  608.9 2.1 copy-start.28
  611.1 2.4 copy-start.61
  611.1 2.4 copy-start.65
  613.5 1.2 copy-start.58
  613.5 1.4 copy-start.60
  614.1 1.5 copy-start.54
  614.1 1.5 copy-start.56
  616.4 2.7 copy-start.39
  619.1 1.1 copy-start.48
  619.1 1.3 copy-start.49
  640.1 9.6 %copy-start.37 = (bf16[2048,384]{1,0:T(8,128)(2,1)S(1)}, bf16[2048,384]{1,0:T(8,128)(2,1)}, u32[]{:S(2)}) copy-start(bf16[2048,384]{1,0:T(8,128)(2,1)} %copy-done.36) | copy-start | bytes 4718596
  640.1 9.6 %copy-start.63 = (bf16[2048,128]{0,1:T(8,128)(2,1)S(1)}, bf16[2048,128]{0,1:T(8,128)(2,1)}, u32[]{:S(2)}) copy-start(bf16[2048,128]{0,1:T(8,128)(2,1)} %get-tuple-element.94) | copy-start | bytes 1572868
  640.1 9.6 %copy-start.64 = (bf16[2048,128]{0,1:T(8,128)(2,1)S(1)}, bf16[2048,128]{0,1:T(8,128)(2,1)}, u32[]{:S(2)}) copy-start(bf16[2048,128]{0,1:T(8,128)(2,1)} %get-tuple-element.95) | copy-start | bytes 1572868
  640.1 9.6 %copy-start.66 = (bf16[2048,128]{0,1:T(8,128)(2,1)S(1)}, bf16[2048,128]{0,1:T(8,128)(2,1)}, u32[]{:S(2)}) copy-start(bf16[2048,128]{0,1:T(8,128)(2,1)} %copy.110) | copy-start | bytes 1572868
  659.8 1.2 copy-start
  661.0 3.4 copy-start.3
  665.5 1.4 copy-start.20
  756.4 1.3 copy-start.19
  803.7 5.8 copy-start.51
  803.7 5.8 copy-start.52
  811.0 4.2 copy-start.1
  811.0 4.2 copy-start.26
  824.1 9.1 %copy-start.45 = (bf16[128,2048]{1,0:T(8,128)(2,1)S(1)}, bf16[128,2048]{1,0:T(8,128)(2,1)}, u32[]{:S(2)}) copy-start(bf16[128,2048]{1,0:T(8,128)(2,1)} %add_convert_fusion.1.refs_2_) | copy-start | bytes 1572868
  824.1 9.1 %copy-start.62 = (bf16[128,2048]{1,0:T(8,128)(2,1)S(1)}, bf16[128,2048]{1,0:T(8,128)(2,1)}, u32[]{:S(2)}) copy-start(bf16[128,2048]{1,0:T(8,128)(2,1)} %get-tuple-element.52) | copy-start | bytes 1572868
  824.1 10.2 %copy-start.42 = (bf16[128,3072]{1,0:T(8,128)(2,1)S(1)}, bf16[128,3072]{1,0:T(8,128)(2,1)}, u32[]{:S(2)}) copy-start(bf16[128,3072]{1,0:T(8,128)(2,1)} %reduce_sum.207.refs_0_) | copy-start | bytes 2359300
  838.3 3.7 copy-start.24
  838.3 3.7 copy-start.41
  (6 other events, 5.6 us)

commit v3 on v2

--- a/solution.py
+++ b/solution.py
@@ -74,8 +74,9 @@
 
 
 class Load:
-    def __init__(self, kind, source, parts=1):
+    def __init__(self, kind, source, parts=1, far=0, near=0):
         self.kind = kind
+        self.stages = (near, far)
         self.source = source
         self.parts = parts
         groups = self.groups = lax.axis_size("zh")
@@ -154,15 +155,17 @@
         result = []
         for index, ((step, names), part) in enumerate(self.moves(here)):
             source, target, landing = self.views(here, src, dst, step, names, part)
+            stage = self.stages[1 if step else 0]
             if not step and not names:
                 copy = pltpu.make_async_copy(source, target, send.at[index])
-                result.append((copy, None))
+                result.append((stage, copy, None))
                 continue
             copy = pltpu.make_async_remote_copy(
                 src_ref=source, dst_ref=target, send_sem=send.at[index], recv_sem=recv.at[index],
                 device_id=owner_at(here, self.groups, step, names), device_id_type=MESH,
             )
-            result.append((copy, pltpu.make_async_copy(landing, landing, recv.at[index])))
+            landed = pltpu.make_async_copy(landing, landing, recv.at[index])
+            result.append((stage, copy, landed))
         return result
 
 
@@ -182,34 +185,38 @@
         groups = lax.axis_size("zh")
         greet([owner_at(here, groups, step, n) for step, n in sorted(reached)])
 
-    def start(self, here, sources, targets, semaphores):
+    def prepare(self, here, sources, targets, semaphores):
         self.copies = []
         for k, load in enumerate(self.loads):
             self.copies += load.copies(
                 here, sources[k], targets[k], semaphores[2 * k], semaphores[2 * k + 1]
             )
-        for copy, _ in self.copies:
-            copy.start()
+
+    def start(self, stage):
+        for when, copy, _ in self.copies:
+            if when == stage:
+                copy.start()
 
     def wait(self):
-        for copy, landing in self.copies:
+        for _, copy, landing in self.copies:
             if landing is None:
                 copy.wait()
             else:
                 landing.wait()
-        for copy, landing in self.copies:
+        for _, copy, landing in self.copies:
             if landing is not None:
                 copy.wait_send()
 
 
+GATHER_STAGES = (0, 1, 2, 3)
 NEAR = [("x",), ("zl",), ("y",), ("c",)]
 
 
-def call(body, name, ident, cargo, operand, out, out_space, scratch, vmem=32):
+def call(body, name, ident, cargo, operand, space, out, out_space, scratch, vmem=40):
     return pl.pallas_call(
         body,
         out_shape=[out] + cargo.outs,
-        in_specs=[pl.BlockSpec(memory_space=pl.ANY)] + cargo.specs,
+        in_specs=[pl.BlockSpec(memory_space=space)] + cargo.specs,
         out_specs=[pl.BlockSpec(memory_space=out_space)] + cargo.specs,
         scratch_shapes=scratch + cargo.scratch,
         compiler_params=pltpu.CompilerParams(
@@ -228,6 +235,7 @@
     spans = [pl.ds(r0, size) for _, r0, size in orders]
     orders = [o for o, _, _ in orders]
     pieces = range(len(orders))
+    cargo.prepare(here, sources, targets, refs[2 * n + 6 :])
     cargo.greet(here, NEAR)
     own = pltpu.make_async_copy(x_ref, o_ref.at[with_bits(here, ())], own_sem)
 
@@ -265,7 +273,8 @@
             sent[-1].start()
         if mask == 0:
             own.start()
-            cargo.start(here, sources, targets, refs[2 * n + 6 :])
+        if mask in GATHER_STAGES:
+            cargo.start(GATHER_STAGES.index(mask))
     for mask in range(8):
         for p in pieces:
             spot = o_ref.at[with_bits(here, subset(orders[p], mask) + ("c",)), spans[p]]
@@ -282,7 +291,7 @@
     cargo = Cargo(list(loads))
     out = call(
         functools.partial(gather_kernel, orders, cargo),
-        "gather_cube", ident, cargo, block,
+        "gather_cube", ident, cargo, block, pl.ANY,
         jax.ShapeDtypeStruct((MEMBERS, rows, width), block.dtype), pl.ANY,
         [pltpu.SemaphoreType.DMA((len(orders), 8))] * 4 + [pltpu.SemaphoreType.DMA(())],
     )
@@ -292,13 +301,12 @@
 def scatter_kernel(orders, cargo, p_ref, *refs):
     n = cargo.n
     sources, o_ref, targets = refs[:n], refs[n], refs[n + 1 : 2 * n + 1]
-    acc, rcore, came, load_sem, core_send, core_recv, send_sem, recv_sem = refs[
-        2 * n + 1 : 2 * n + 9
-    ]
+    acc, rcore, came, core_send, core_recv, send_sem, recv_sem = refs[2 * n + 1 : 2 * n + 8]
     here = place()
     spans = [pl.ds(r0, size) for _, r0, size in orders]
     orders = [o for o, _, _ in orders]
     pieces = range(len(orders))
+    cargo.prepare(here, sources, targets, refs[2 * n + 8 :])
     cargo.greet(here, NEAR)
 
     def away(p, mask):
@@ -310,20 +318,13 @@
             device_id=flip(here, "c"), device_id_type=MESH,
         )
 
-    def fetch(p, mask):
-        names = subset(orders[p], mask)
-        return pltpu.make_async_copy(
-            p_ref.at[with_bits(here, names), spans[p]], acc.at[mask, spans[p]], load_sem.at[p, mask]
-        )
-
     sequence = [7, 3, 5, 1, 6, 2, 4, 0]
     sent = []
     for mask in sequence:
         for p in pieces:
             sent.append(away(p, mask))
             sent[-1].start()
-            fetch(p, mask).start()
-    cargo.start(here, sources, targets, refs[2 * n + 9 :])
+    cargo.start(0)
 
     def over(p, mask):
         k = (mask & -mask).bit_length() - 1
@@ -336,14 +337,18 @@
     def add(p, mask, other):
         acc[mask, spans[p]] = acc[mask, spans[p]] + other[...]
 
+    def first_sum(p, mask):
+        own = with_bits(here, subset(orders[p], mask))
+        acc[mask, spans[p]] = p_ref[own, spans[p]] + rcore[mask, spans[p]]
+
     for mask in sequence:
         for p in pieces:
-            fetch(p, mask).wait()
             away(p, mask).wait_recv()
-            add(p, mask, rcore.at[mask, spans[p]])
+            first_sum(p, mask)
             if mask & 1:
                 sent.append(over(p, mask))
                 sent[-1].start()
+    cargo.start(1)
     for k in range(3):
         low = 1 << k
         for mask in [m for m in (6, 2, 4, 0) if m & (2 * low - 1) == 0]:
@@ -358,6 +363,8 @@
                 if mask & (2 * low):
                     sent.append(over(p, mask))
                     sent[-1].start()
+        if k < 2:
+            cargo.start(2 + k)
     for copy in sent:
         copy.wait_send()
     cargo.wait()
@@ -371,17 +378,19 @@
     return call(
         functools.partial(scatter_kernel, orders, cargo),
         "scatter_cube", ident, cargo, partial.astype(jnp.bfloat16).reshape(MEMBERS, rows, width),
+        pltpu.VMEM,
         jax.ShapeDtypeStruct((rows, width), jnp.float32), pltpu.VMEM,
         [pltpu.VMEM((8, rows, width), jnp.bfloat16)] * 3
-        + [pltpu.SemaphoreType.DMA((len(orders), 8))] * 5,
+        + [pltpu.SemaphoreType.DMA((len(orders), 8))] * 4,
     )
 
 
 def carry_kernel(cargo, *refs):
     n = cargo.n
     here = place()
+    cargo.prepare(here, refs[:n], refs[n : 2 * n], refs[2 * n :])
     cargo.greet(here, [])
-    cargo.start(here, refs[:n], refs[n : 2 * n], refs[2 * n :])
+    cargo.start(0)
     cargo.wait()
 
 
@@ -490,12 +499,28 @@
     return jnp.sum(terms.astype(jnp.float32), axis=0).astype(jnp.bfloat16)
 
 
+def finish_kernel(mine_ref, came_ref, o_ref):
+    own = pl.program_id(1) == lax.axis_index("x")
+    o_ref[...] = jnp.where(own, mine_ref[...], came_ref[...]).astype(jnp.float32)
+
+
 def whole_rows(mine, came, parts):
-    rows = mine.shape[0]
-    first = lax.axis_index("x") == 0
-    mine, came = (v.reshape(rows, parts, -1) for v in (mine, came))
-    both = [jnp.where(first, mine, came), jnp.where(first, came, mine)]
-    return jnp.stack(both, axis=2).reshape(rows, -1).astype(jnp.float32)
+    rows, width = mine.shape
+    step = min(2048, width // parts)
+    steps = width // parts // step
+    half = pl.BlockSpec((rows, step), lambda p, x, k: (0, p * steps + k))
+    return pl.pallas_call(
+        finish_kernel,
+        grid=(parts, 2, steps),
+        out_shape=jax.ShapeDtypeStruct((rows, 2 * width), jnp.float32),
+        in_specs=[half, half],
+        out_specs=pl.BlockSpec((rows, step), lambda p, x, k: (0, (2 * p + x) * steps + k)),
+        compiler_params=pltpu.CompilerParams(vmem_limit_bytes=32 * MIB),
+        cost_estimate=pl.CostEstimate(
+            flops=0, bytes_accessed=16 * rows * width, transcendentals=0
+        ),
+        name="whole_rows",
+    )(mine, came)
 
 
 def heads_are_owners(rows):
@@ -586,22 +611,24 @@
         .reshape(total, HD)
         .astype(jnp.bfloat16)
     )
-    feed_width = w_down_t.shape[1]
     x_most = halves(count_rows, "x", "y", "zl")
     x_last = halves(count_rows, "zl", "y", "x")
+    x_or_y = (
+        (("x", "y", "zl"), 0, count_rows // 2),
+        (("y", "x", "zl"), count_rows // 2, count_rows // 2),
+    )
     y_last = halves(count_rows, "zl", "x", "y")
-    branch, gate_cols = scatter_cube(
+    branch, down_cols = scatter_cube(
         jnp.dot(attended, out_rows, preferred_element_type=jnp.float32),
-        3, [Load("columns", w_gate_up[:, :feed_width])], x_most,
+        3, [Load("columns", w_down_t, near=1)], x_most,
     )
     branch_norm, branch_inv = normalize(branch, gain_rows[2])
     middle = tokens.astype(jnp.float32) + branch_norm
-    middle_all, up_cols, down_cols = gather_cube(
-        middle.astype(jnp.bfloat16), 4,
-        [Load("columns", w_gate_up[:, feed_width:]), Load("columns", w_down_t)], x_last,
-    )
-    gate_part = jnp.dot(middle_all, gate_cols, preferred_element_type=jnp.float32)
-    up_part = jnp.dot(middle_all, up_cols, preferred_element_type=jnp.float32)
+    middle_all, gate_up_cols = gather_cube(
+        middle.astype(jnp.bfloat16), 4, [Load("columns", w_gate_up, 2, near=3)], x_last
+    )
+    gate_up = jnp.dot(middle_all, gate_up_cols, preferred_element_type=jnp.float32)
+    gate_part, up_part = jnp.split(gate_up, 2, axis=1)
     hidden_bf = (gate_part * jax.nn.sigmoid(gate_part) * up_part).astype(jnp.bfloat16)
     (feed_out,) = scatter_cube(contract_last(hidden_bf, down_cols), 5)
     feed_norm, feed_inv = normalize(feed_out, gain_rows[3])
@@ -612,22 +639,20 @@
     (feed_all,) = gather_cube(feed_grad.astype(jnp.bfloat16), 6)
     down_grad = contract_first(feed_all, hidden_bf).astype(jnp.bfloat16)
     hidden_grad = jnp.dot(feed_all, down_cols, preferred_element_type=jnp.float32)
-    gate_bf, up_bf = silu_grads(hidden_grad, gate_part, up_part)
-    gate_grad = contract_first(middle_all, gate_bf).astype(jnp.bfloat16)
-    up_grad = contract_first(middle_all, up_bf).astype(jnp.bfloat16)
-    middle_part = contract_last(gate_bf, gate_cols) + contract_last(up_bf, up_cols)
-    middle_sum, down_terms, gate_terms = scatter_cube(
-        middle_part, 7, [Load("owners", down_grad), Load("owners", gate_grad)], x_most
+    gate_up_bf = jnp.concatenate(silu_grads(hidden_grad, gate_part, up_part), axis=1)
+    gate_up_grad = contract_first(middle_all, gate_up_bf).astype(jnp.bfloat16)
+    middle_part = contract_last(gate_up_bf, gate_up_cols)
+    middle_sum, gate_up_terms = scatter_cube(
+        middle_part, 7, [Load("owners", gate_up_grad, 2)], x_most
     )
     middle_grad = upstream + middle_sum
     branch_grad, gain_branch = norm_back(middle_grad, branch, branch_inv, gain_rows[2])
+    gate_up_sum = owned_sum(gate_up_terms)
+    branch_all, down_terms, gate_up_other = gather_cube(
+        branch_grad.astype(jnp.bfloat16), 8,
+        [Load("owners", down_grad, far=1, near=3), Load("x", gate_up_sum, near=1)], y_last,
+    )
     down_sum = owned_sum(down_terms)
-    gate_sum = owned_sum(gate_terms)
-    branch_all, up_terms, down_other, gate_other = gather_cube(
-        branch_grad.astype(jnp.bfloat16), 8,
-        [Load("owners", up_grad), Load("x", down_sum), Load("x", gate_sum)], y_last,
-    )
-    up_sum = owned_sum(up_terms)
     out_grad = contract_first(attended, branch_all)
     attended_grad = blocks(contract_last(branch_all, out_rows).astype(jnp.bfloat16))
     prob_grad = jnp.einsum(
@@ -677,12 +702,12 @@
         gain_terms.reshape(4, groups * SIDES, owned).transpose(1, 0, 2),
         ((0, 0), (0, 4), (0, lanes - owned)),
     ).reshape(groups * SIDES * 8, lanes)
-    loads = [Load("owners", qkv_grad, 3), Load("x", up_sum), Load("owners", gain_terms)]
+    loads = [Load("owners", qkv_grad, 3), Load("x", down_sum, near=2), Load("owners", gain_terms)]
     if direct:
         out_bf = out_grad.astype(jnp.bfloat16)
         loads.append(Load("zh", out_bf))
-    tokens_sum, qkv_terms, up_other, gain_came, *out_came = scatter_cube(
-        contract_last(projected_bf, qkv_cols), 10, loads, x_most
+    tokens_sum, qkv_terms, down_other, gain_came, *out_came = scatter_cube(
+        contract_last(projected_bf, qkv_cols), 10, loads, x_or_y
     )
     grad_tokens = middle_grad + tokens_sum
     qkv_sum = owned_sum(qkv_terms)
@@ -699,9 +724,7 @@
     else:
         grad_out = summed_head_rows(out_grad, owned)
     grad_qkv = whole_rows(qkv_sum, qkv_other, 3)
-    grad_gate_up = jnp.concatenate(
-        [whole_rows(gate_sum, gate_other, 1), whole_rows(up_sum, up_other, 1)], axis=1
-    )
+    grad_gate_up = whole_rows(gate_up_sum, gate_up_other, 2)
     grad_down_t = whole_rows(down_sum, down_other, 1)
     grad_gains = (gain_sum + gain_other)[:4, :owned].T
     return (mixed, grad_tokens, grad_qkv, grad_out, grad_gate_up, grad_down_t, grad_gains)

time: 854 us -> 782 us (0.916)
  local copies, waits for them, and re-layouts: 66.8 us -> 28.2 us
  Pallas kernels: 620 us -> 600 us
    pallas_call x8, Pallas kernels: 571 us -> 542 us  [call(): pl.pallas_call(body, out_shape=[out] + cargo.outs, in_specs=[pl.BlockSpec...]
    unnamed x143 -> x118, local copies, waits for them, and re-layouts: 45.3 us -> 18.7 us
    dot_general x5 -> x4, matrix products: 39.1 us -> 27.5 us  [contract_last(): lax.dot_general(operand, matrix, (((1,), (1,)), ((), ())), preferred_elem...]
    pallas_call x0 -> x3, Pallas kernels: none -> 10.4 us  [whole_rows(): pl.pallas_call(finish_kernel, grid=(parts, 2, steps), out_shape=jax.Shape...]
    dot_general x5 -> x4, matrix products: 30.6 us -> 35.3 us  [contract_first(): lax.dot_general(operand, matrix, (((0,), (0,)), ((), ())), preferred_elem...]
where the time goes in v3:
time: 782 us; the launch traced here: 775 us
  Pallas kernels  600 us (77%)
  matrix products  105 us (13%)
  other arithmetic  40.7 us (5%)
  local copies, waits for them, and re-layouts  28.2 us (4%)
    pallas_call x8, Pallas kernels, call(): pl.pallas_call(body, out_shape=[out] + cargo.outs, in_specs=[pl.BlockSpec...  542 us
    dot_general x4, matrix products, contract_first(): lax.dot_general(operand, matrix, (((0,), (0,)), ((), ())), preferred_elem...  35.3 us
    pallas_call x1, Pallas kernels, carry(): pl.pallas_call(functools.partial(carry_kernel, cargo), out_shape=cargo.ou...  29.7 us
    dot_general x4, matrix products, contract_last(): lax.dot_general(operand, matrix, (((1,), (1,)), ((), ())), preferred_elem...  27.5 us
    unnamed x118, local copies, waits for them, and re-layouts  18.7 us
    pallas_call x2, Pallas kernels, sum_cube(): pl.pallas_call(exchange_kernel, out_shape=jax.ShapeDtypeStruct(shape, jnp...  18.2 us

profile of v3, /device:TPU:0, one launch (start us, length us, event | category | flops | bytes accessed | tf_op | source)
XLA Modules:
  0.0 775.3 jit_solution(6303584613350744348)
XLA Ops:
  1.7 0.7 pad_convert_fusion.refs_0_
  2.4 1.0 copy-done.5
  3.4 1.0 copy-done.11
  4.5 1.4 copy-done.17
  5.9 68.6 %gather_cube.4 = (bf16[16,128,2048]{2,1,0:T(8,128)(2,1)S(1)}, f32[16,8,128]{2,1,0:T(8,128)S(1)}, f32[16,8,128]{2,1,0:T(8,128)S(1)}, bf16[2048,384]{1,0:T(8,128)(2,1)S(1)}, bf16[128,2048]{1,0:T(8,128)(2,1)S(1)}) custom-call(bf16[128,2048]{1,0:T(8,128)(2,1)S(1)} %copy-done.5, f32[8,128]{1,0:T(8,128)S(1)} %pad_convert_fusion.refs_0_, ...), custom_call_target="tpu_custom_call" | custom-call | bytes 104857600 | tf_op jit(solution)/shard_map/gather_cube/pallas_call | solution.py:216
  74.5 3.7 fusion.63
  78.5 1.5 copy-done.32
  80.6 9.1 %sum_cube.2 = f32[32,128]{1,0:T(8,128)} custom-call(f32[32,128]{1,0:T(8,128)} %pad_maximum_fusion.18.v_ref), custom_call_target="tpu_custom_call" | custom-call | bytes 20971520 | tf_op jit(solution)/shard_map/sum_cube/pallas_call | solution.py:434
  89.7 0.7 rsqrt_bitcast_fusion.1
  90.4 1.8 fusion.30
  92.2 3.2 fusion.38
  96.1 1.4 copy.67
  97.9 1.9 fusion.62
  99.8 2.1 slice.158
  101.9 2.1 copy.70
  103.9 2.4 convolution_convert_fusion.9
  106.4 2.3 convolution_convert_fusion.3
  108.8 64.8 %scatter_cube.4 = (f32[128,2048]{1,0:T(8,128)S(1)}, bf16[2048,512]{1,0:T(8,128)(2,1)S(1)}) custom-call(bf16[16,128,2048]{2,1,0:T(8,128)(2,1)S(1)} %bitcast.95, bf16[128,8192]{1,0:T(8,128)(2,1)S(1)} %copy-done.10), custom_call_target="tpu_custom_call" | custom-call | bytes 104857600 | tf_op jit(solution)/shard_map/scatter_cube/pallas_call | solution.py:216
  174.0 84.1 %gather_cube.5 = (bf16[16,128,2048]{2,1,0:T(8,128)(2,1)}, bf16[2048,1024]{1,0:T(8,128)(2,1)S(1)}) custom-call(bf16[128,2048]{1,0:T(8,128)(2,1)S(1)} %fusion.32.x_ref, bf16[128,16384]{1,0:T(8,128)(2,1)S(1)} %copy-done.8), custom_call_target="tpu_custom_call" | custom-call | bytes 104857600 | tf_op jit(solution)/shard_map/gather_cube/pallas_call | solution.py:216
  258.1 14.0 %fusion.64 = f32[2048,1024]{0,1:T(8,128)} fusion(bf16[2048,2048]{1,0:T(8,128)(2,1)} %bitcast.144, bf16[2048,1024]{1,0:T(8,128)(2,1)S(1)} %get-tuple-element.36), kind=kOutput, calls=%fused_computation.145 | convolution fusion | flops 8589934592 | bytes 20971520 | tf_op jit(solution)/shard_map/dot_general | solution.py:630
  272.0 4.7 multiply_convert_fusion.2
  276.7 6.4 convolution_convert_fusion.2
  283.2 45.4 %scatter_cube.5 = f32[128,2048]{1,0:T(8,128)S(1)} custom-call(bf16[16,128,2048]{2,1,0:T(8,128)(2,1)S(1)} %bitcast.96), custom_call_target="tpu_custom_call" | custom-call | bytes 104857600 | tf_op jit(solution)/shard_map/scatter_cube/pallas_call | solution.py:216
  329.5 33.1 %gather_cube.6 = bf16[16,128,2048]{2,1,0:T(8,128)(2,1)S(1)} custom-call(bf16[128,2048]{1,0:T(8,128)(2,1)S(1)} %fusion.11.x_ref), custom_call_target="tpu_custom_call" | custom-call | bytes 104857600 | tf_op jit(solution)/shard_map/gather_cube/pallas_call | solution.py:216
  362.6 3.2 copy-done.3
  365.8 6.3 convolution_convert_fusion.5.refs_0_
  372.1 12.2 %multiply_convert_fusion.1 = (bf16[2048,512]{0,1:T(8,128)(2,1)}, bf16[2048,512]{0,1:T(8,128)(2,1)}) fusion(f32[2048,1024]{0,1:T(8,128)} %fusion.64, bf16[2048,2048]{1,0:T(8,128)(2,1)} %bitcast.98, bf16[2048,512]{1,0:T(8,128)(2,1)S(1)} %copy-done.29), kind=kOutput, calls=%fused_computation.7 | convolution fusion | flops 4308598784 | bytes 23068672 | tf_op jit(solution)/shard_map/dot_general | solution.py:641
  384.3 12.7 %convolution_convert_fusion.4.refs_0_ = bf16[2048,1024]{1,0:T(8,128)(2,1)S(1)} fusion(bf16[2048,2048]{1,0:T(8,128)(2,1)} %bitcast.145, bf16[2048,512]{0,1:T(8,128)(2,1)} %get-tuple-element.64, bf16[2048,512]{0,1:T(8,128)(2,1)} %get-tuple-element.63), kind=kOutput, calls=%fused_computation.10 | convolution fusion | flops 8600420352 | bytes 16777216 | tf_op jit(solution)/shard_map/dot_general | solution.py:486
  397.1 11.8 %convolution_convert_fusion.1 = bf16[2048,2048]{1,0:T(8,128)(2,1)} fusion(bf16[2048,1024]{1,0:T(8,128)(2,1)S(1)} %get-tuple-element.36, bf16[2048,512]{0,1:T(8,128)(2,1)S(1)} %copy-done.58, bf16[2048,512]{0,1:T(8,128)(2,1)S(1)} %copy-done.57), kind=kOutput, calls=%fused_computation.2 | convolution fusion | flops 8602517504 | bytes 16777216 | tf_op jit(solution)/shard_map/dot_general | solution.py:480
  408.8 88.8 %scatter_cube.6 = (f32[128,2048]{1,0:T(8,128)S(1)}, bf16[2,128,8192]{2,1,0:T(8,128)(2,1)S(1)}) custom-call(bf16[16,128,2048]{2,1,0:T(8,128)(2,1)} %bitcast.102, bf16[2048,1024]{1,0:T(8,128)(2,1)S(1)} %convolution_convert_fusion.4.refs_0_), custom_call_target="tpu_custom_call" | custom-call | bytes 104857600 | tf_op jit(solution)/shard_map/scatter_cube/pallas_call | solution.py:216
  497.7 1.0 copy-done.1
  498.7 2.0 copy-done.9
  500.7 3.2 reduce_sum.185.refs_1_.mine_ref
  503.9 2.2 multiply_reduce_fusion
  506.1 3.2 multiply_convert_fusion.6
  509.4 82.5 %gather_cube.7 = (bf16[16,128,2048]{2,1,0:T(8,128)(2,1)}, bf16[2,128,4096]{2,1,0:T(8,128)(2,1)S(1)}, bf16[128,8192]{1,0:T(8,128)(2,1)S(1)}) custom-call(bf16[128,2048]{1,0:T(8,128)(2,1)S(1)} %get-tuple-element.73.x_ref, bf16[2048,512]{1,0:T(8,128)(2,1)S(1)} %copy-done.14, bf16[128,8192]{1,0:T(8,128)(2,1)S(1)} %reduce_sum.185.refs_1_.mine_ref), custom_call_target="tpu_custom_call" | custom-call | bytes 104857600 | tf_op jit(solution)/shard_map/gather_cube/pallas_call | solution.py:216
  591.9 7.0 fusion.1.refs_3_
  598.9 0.7 copy-done.34
  599.7 2.4 convolution_convert_fusion.7
  605.0 2.6 fusion.33
  607.7 0.7 multiply_reduce_fusion.2
  609.2 9.1 %sum_cube.3 = f32[32,128]{1,0:T(8,128)} custom-call(f32[32,128]{1,0:T(8,128)} %pad_maximum_fusion.19.v_ref), custom_call_target="tpu_custom_call" | custom-call | bytes 20971520 | tf_op jit(solution)/shard_map/sum_cube/pallas_call | solution.py:434
  618.3 0.7 multiply_bitcast_fusion.1
  619.0 3.3 multiply_convert_fusion.4
  622.3 3.7 convolution_convert_fusion.8
  626.0 2.0 copy.69
  628.1 9.3 %convolution_convert_fusion.6.refs_0_ = bf16[2048,384]{1,0:T(8,128)(2,1)} fusion(bf16[2048,2048]{1,0:T(8,128)(2,1)} %bitcast.100, bf16[2048,128]{0,1:T(8,128)(2,1)} %copy.69, bf16[2048,128]{0,1:T(8,128)(2,1)S(1)} %copy-done.52, bf16[2048,128]{0,1:T(8,128)(2,1)S(1)} %copy-done.51), kind=kOutput, calls=%fused_computation.12 | convolution fusion | flops 3226730496 | bytes 11534336 | tf_op jit(solution)/shard_map/dot_general | solution.py:486
  637.4 6.8 convolution_convert_fusion
  644.2 2.1 reduce_sum.189.refs_1_.mine_ref
  646.3 1.0 copy-done.7
  647.4 1.4 copy-done.19
  648.8 74.6 %scatter_cube.7 = (f32[128,2048]{1,0:T(8,128)S(1)}, bf16[2,128,3072]{2,1,0:T(8,128)(2,1)S(1)}, bf16[128,4096]{1,0:T(8,128)(2,1)S(1)}, f32[2,8,1024]{2,1,0:T(8,128)S(1)}, bf16[128,2048]{1,0:T(8,128)(2,1)S(1)}) custom-call(bf16[16,128,2048]{2,1,0:T(8,128)(2,1)} %bitcast.103, bf16[2048,384]{1,0:T(8,128)(2,1)S(1)} %copy-done.19, ...), custom_call_target="tpu_custom_call" | custom-call | bytes 104857600 | tf_op jit(solution)/shard_map/scatter_cube/pallas_call | solution.py:216
  723.4 1.0 copy-done.20
  724.3 1.0 copy-done.22
  725.3 1.0 add_convert_fusion.refs_2_
  726.6 2.8 reduce_sum.194.refs_0_.mine_ref
  730.0 29.7 %carry.1 = (bf16[128,3072]{1,0:T(8,128)(2,1)}, f32[8,128]{1,0:T(8,128)}, bf16[128,2048]{1,0:T(8,128)(2,1)}) custom-call(bf16[128,3072]{1,0:T(8,128)(2,1)} %reduce_sum.194.refs_0_.mine_ref, f32[8,128]{1,0:T(8,128)} %bitcast_reduce_fusion.refs_1_, bf16[128,2048]{1,0:T(8,128)(2,1)} %add_convert_fusion.refs_2_), custom_call_target="tpu_custom_call" | custom-call | bytes 52428800 | tf_op jit(solution)/shard_map/carry/pallas_call | solution.py:399
  759.7 0.8 add.107
  761.1 1.2 copy-done.23
  762.4 2.7 whole_rows.5
  765.1 4.9 whole_rows.4
  770.0 1.0 select_convert_fusion
  771.1 2.8 whole_rows.3
  773.9 1.2 fusion.47
  (146 shorter events, 9.4 us)
Async XLA Ops:
  2.4 1.0 copy-start.5
  3.4 1.0 copy-start.11
  4.5 1.4 copy-start.17
  74.5 3.8 copy-start.27
  74.5 3.8 copy-start.30
  74.5 31.9 %copy-start.25 = (bf16[128,2048]{1,0:T(8,128)(2,1)}, bf16[128,2048]{1,0:T(8,128)(2,1)S(1)}, u32[]{:S(2)}) copy-start(bf16[128,2048]{1,0:T(8,128)(2,1)S(1)} %get-tuple-element.33) | copy-start | bytes 1572868
  78.3 1.7 copy-start.32
  95.8 8.2 %copy-start.42 = (bf16[2048,64]{1,0:T(8,128)(2,1)}, bf16[2048,64]{1,0:T(8,128)(2,1)S(1)}, u32[]{:S(2)}) copy-start(bf16[2048,64]{1,0:T(8,128)(2,1)S(1)} %copy.65) | copy-start | bytes 786436
  96.1 10.2 %copy-start.44 = (bf16[2048,64]{1,0:T(8,128)(2,1)}, bf16[2048,64]{1,0:T(8,128)(2,1)S(1)}, u32[]{:S(2)}) copy-start(bf16[2048,64]{1,0:T(8,128)(2,1)S(1)} %copy.66) | copy-start | bytes 786436
  97.5 8.9 %copy-start.46 = (bf16[2048,64]{1,0:T(8,128)(2,1)}, bf16[2048,64]{1,0:T(8,128)(2,1)S(1)}, u32[]{:S(2)}) copy-start(bf16[2048,64]{1,0:T(8,128)(2,1)S(1)} %copy.67) | copy-start | bytes 786436
  97.8 6.2 copy-start.48
  106.3 2.4 copy-start.37
  106.4 2.4 copy-start.10
  108.7 65.0 %copy-start.6 = (bf16[128,2048]{1,0:T(8,128)(2,1)S(1)}, bf16[128,2048]{1,0:T(8,128)(2,1)}, u32[]{:S(2)}) copy-start(bf16[128,2048]{1,0:T(8,128)(2,1)} %x_ref.1) | copy-start | bytes 1572868
  108.7 65.2 %copy-start.8 = (bf16[128,16384]{1,0:T(8,128)(2,1)S(1)}, bf16[128,16384]{1,0:T(8,128)(2,1)}, u32[]{:S(2)}) copy-start(bf16[128,16384]{1,0:T(8,128)(2,1)} %refs_0_.3) | copy-start | bytes 12582916
  173.5 98.5 %copy-start = (f32[128,2048]{1,0:T(8,128)}, f32[128,2048]{1,0:T(8,128)S(1)}, u32[]{:S(2)}) copy-start(f32[128,2048]{1,0:T(8,128)S(1)} %get-tuple-element.34) | copy-start | bytes 3145732
  173.5 98.5 %copy-start.28 = (bf16[2048,512]{1,0:T(8,128)(2,1)}, bf16[2048,512]{1,0:T(8,128)(2,1)S(1)}, u32[]{:S(2)}) copy-start(bf16[2048,512]{1,0:T(8,128)(2,1)S(1)} %get-tuple-element.37) | copy-start | bytes 6291460
  283.2 45.6 %copy-start.35 = (bf16[128,2048]{1,0:T(8,128)(2,1)S(1)}, bf16[128,2048]{1,0:T(8,128)(2,1)}, u32[]{:S(2)}) copy-start(bf16[128,2048]{1,0:T(8,128)(2,1)} %param.15) | copy-start | bytes 1572868
  362.6 3.2 copy-start.3
  365.8 6.3 copy-start.29
  384.3 12.8 %copy-start.57 = (bf16[2048,512]{0,1:T(8,128)(2,1)S(1)}, bf16[2048,512]{0,1:T(8,128)(2,1)}, u32[]{:S(2)}) copy-start(bf16[2048,512]{0,1:T(8,128)(2,1)} %get-tuple-element.63) | copy-start | bytes 6291460
  384.3 12.8 %copy-start.58 = (bf16[2048,512]{0,1:T(8,128)(2,1)S(1)}, bf16[2048,512]{0,1:T(8,128)(2,1)}, u32[]{:S(2)}) copy-start(bf16[2048,512]{0,1:T(8,128)(2,1)} %get-tuple-element.64) | copy-start | bytes 6291460
  497.7 1.0 copy-start.1
  498.7 2.0 copy-start.9
  503.9 5.5 copy-start.14
  506.1 85.8 %copy-start.38 = (bf16[16,128,128]{2,1,0:T(8,128)(2,1)S(1)}, bf16[16,128,128]{2,1,0:T(8,128)(2,1)}, u32[]{:S(2)}) copy-start(bf16[16,128,128]{2,1,0:T(8,128)(2,1)} %copy-done.37) | copy-start | bytes 1572868
  591.9 7.1 copy-start.13
  591.9 7.0 copy-start.15
  591.9 7.0 copy-start.12
  591.9 7.0 copy-start.26
  591.9 7.8 %copy-start.34 = (bf16[16,128,2048]{2,1,0:T(8,128)(2,1)S(1)}, bf16[16,128,2048]{2,1,0:T(8,128)(2,1)}, u32[]{:S(2)}) copy-start(bf16[16,128,2048]{2,1,0:T(8,128)(2,1)} %get-tuple-element.40) | copy-start | bytes 25165828
  599.7 2.4 copy-start.50
  599.7 2.5 copy-start.54
  602.1 2.0 copy-start.56
  602.1 1.2 copy-start.47
  602.1 1.4 copy-start.49
  602.2 2.0 copy-start.43
  602.2 2.0 copy-start.45
  604.8 2.9 copy-start.33
  607.6 0.8 copy-start.40
  607.7 1.0 copy-start.41
  622.3 5.7 copy-start.51
  622.3 5.7 copy-start.52
  628.0 9.3 %copy-start.31 = (bf16[2048,384]{1,0:T(8,128)(2,1)S(1)}, bf16[2048,384]{1,0:T(8,128)(2,1)}, u32[]{:S(2)}) copy-start(bf16[2048,384]{1,0:T(8,128)(2,1)} %copy-done.30) | copy-start | bytes 4718596
  628.0 9.3 %copy-start.55 = (bf16[2048,128]{0,1:T(8,128)(2,1)S(1)}, bf16[2048,128]{0,1:T(8,128)(2,1)}, u32[]{:S(2)}) copy-start(bf16[2048,128]{0,1:T(8,128)(2,1)} %copy.69) | copy-start | bytes 1572868
  646.3 1.0 copy-start.7
  647.4 1.4 copy-start.19
  723.3 1.0 copy-start.20
  724.3 1.0 copy-start.22
  725.3 1.3 copy-start.18
  759.7 5.4 copy-start.16
  761.1 1.2 copy-start.23
  765.1 5.0 copy-start.39
  765.1 5.0 copy-start.53
  765.1 6.0 copy-start.4
  765.1 6.0 copy-start.24
  770.0 3.9 copy-start.2
  770.0 3.9 copy-start.21
  770.0 3.9 copy-start.36

commit v4 on v3

--- a/solution.py
+++ b/solution.py
@@ -19,6 +19,14 @@
 SIDES = 8
 SIDE_BITS = {"zl": 4, "y": 2, "c": 1}
 BITS = {"x": 8, "zl": 4, "y": 2, "c": 1}
+SLOTS = [
+    frozenset(names + core)
+    for names in (
+        (), ("x",), ("y",), ("zl",), ("x", "y"), ("x", "zl"), ("y", "zl"), ("x", "y", "zl"),
+    )
+    for core in ((), ("c",))
+]
+SLOT = {names: k for k, names in enumerate(SLOTS)}
 MESH = pl.DeviceIdType.MESH
 MIB = 1 << 20
 
@@ -40,6 +48,10 @@
 SIDE_PEERS = [tuple(n for n in SIDE_BITS if m & SIDE_BITS[n]) for m in range(SIDES)]
 
 
+def slot(*names):
+    return SLOT[frozenset(names)]
+
+
 def place():
     return {name: lax.axis_index(name) for name in EVERY}
 
@@ -48,7 +60,7 @@
     return {name: 1 - here[name] for name in names}
 
 
-def with_bits(here, names, bits=BITS):
+def with_bits(here, names, bits):
     index = 0
     for name, bit in bits.items():
         index = index + bit * ((1 - here[name]) if name in names else here[name])
@@ -73,37 +85,31 @@
     return device
 
 
+def at(start, size):
+    return pl.ds(pl.multiple_of(start, size), size)
+
+
 class Load:
-    def __init__(self, kind, source, parts=1, far=0, near=0):
-        self.kind = kind
+    space = pl.ANY
+    parts = 1
+
+    def __init__(self, source, far=0, near=0, early=False):
+        self.sources = [source]
         self.stages = (near, far)
-        self.source = source
-        self.parts = parts
-        groups = self.groups = lax.axis_size("zh")
-        shape, kept = source.shape, source.dtype
-        if kind == "columns":
-            self.rows = shape[0]
-            self.piece = shape[1] // (parts * MEMBERS)
-            shape = (groups * SIDES * shape[0], parts * self.piece)
-        elif kind == "owners":
-            self.rows = shape[0] // (groups * SIDES)
-            self.piece = shape[1] // parts
-            shape = (groups, self.rows, parts * SIDES * self.piece)
-        elif kind == "plane":
-            shape = (groups * SIDES,) + shape
-        elif kind == "cube":
-            shape = (MEMBERS,) + shape
-        self.out = jax.ShapeDtypeStruct(shape, kept)
-        self.space = pltpu.VMEM if kind in ("plane", "cube") else pl.ANY
-        self.count = len(self.moves(None))
-
-    def moves(self, here):
-        if self.kind == "zh":
-            return [((1, ()), 0)]
-        if self.kind == "x":
-            return [((0, ("x",)), 0)]
-        if self.kind == "cube":
-            return [((0, names), 0) for names in [()] + PEERS]
+        self.early = early
+        self.groups = lax.axis_size("zh")
+
+    def spaces(self):
+        return [self.space] * len(self.sources), [self.space] * len(self.outs)
+
+    def semaphores(self):
+        count = len(self.moves())
+        return [pltpu.SemaphoreType.DMA((count,)), pltpu.SemaphoreType.DMA((count,))]
+
+    def scratch(self):
+        return self.semaphores()
+
+    def moves(self):
         return [
             ((step, names), part)
             for step in range(self.groups)
@@ -111,116 +117,373 @@
             for part in range(self.parts)
         ]
 
-    def scratch(self):
-        return [pltpu.SemaphoreType.DMA((self.count,)), pltpu.SemaphoreType.DMA((self.count,))]
-
-    def devices(self, here):
-        return [
-            (step, names) for (step, names), part in self.moves(here) if part == 0 and (step or names)
-        ]
-
-    def views(self, here, src, dst, step, names, part):
-        if self.kind in ("zh", "x"):
-            return src, dst, dst
-        if self.kind == "cube":
-            return src, dst.at[with_bits(here, ())], dst.at[with_bits(here, names)]
-        groups, side = self.groups, with_bits(here, (), SIDE_BITS)
-        other = with_bits(here, names, SIDE_BITS)
-        there = lax.rem(here["zh"] + step, groups)
-        whence = lax.rem(here["zh"] + groups - step, groups)
-        me, he = here["zh"] * SIDES + side, whence * SIDES + other
-        if self.kind == "plane":
-            return src, dst.at[me], dst.at[he]
-        rows, piece = self.rows, self.piece
-
-        def at(start, size):
-            return pl.ds(pl.multiple_of(start, size), size)
-
-        if self.kind == "columns":
-            first = part * MEMBERS + here["x"] * SIDES + other
-            columns = pl.ds(part * piece, piece)
-            return (
-                src.at[:, at(first * piece, piece)],
-                dst.at[at(me * rows, rows), columns],
-                dst.at[at(he * rows, rows), columns],
-            )
-        target = there * SIDES + other
-        return (
-            src.at[at(target * rows, rows), pl.ds(part * piece, piece)],
-            dst.at[here["zh"], :, at((part * SIDES + side) * piece, piece)],
-            dst.at[whence, :, at((part * SIDES + other) * piece, piece)],
-        )
-
-    def copies(self, here, src, dst, send, recv):
-        result = []
-        for index, ((step, names), part) in enumerate(self.moves(here)):
-            source, target, landing = self.views(here, src, dst, step, names, part)
+    def reached(self):
+        return {peer for peer, _ in self.moves() if peer != (0, ())}
+
+    def around(self, here, step, names):
+        there = lax.rem(here["zh"] + step, self.groups)
+        whence = lax.rem(here["zh"] + self.groups - step, self.groups)
+        mine, other = with_bits(here, (), SIDE_BITS), with_bits(here, names, SIDE_BITS)
+        return mine, other, there, whence
+
+    def bind(self, here, sources, targets, scratch):
+        self.here, self.src, self.dst = here, sources, targets
+        self.send, self.recv, *self.more = scratch
+        self.copies = []
+        for index, ((step, names), part) in enumerate(self.moves()):
+            source, target, landing = self.views(here, step, names, part)
             stage = self.stages[1 if step else 0]
             if not step and not names:
-                copy = pltpu.make_async_copy(source, target, send.at[index])
-                result.append((stage, copy, None))
+                copy = pltpu.make_async_copy(source, target, self.send.at[index])
+                self.copies.append((stage, copy, None, (step, names)))
                 continue
             copy = pltpu.make_async_remote_copy(
-                src_ref=source, dst_ref=target, send_sem=send.at[index], recv_sem=recv.at[index],
+                src_ref=source, dst_ref=target,
+                send_sem=self.send.at[index], recv_sem=self.recv.at[index],
                 device_id=owner_at(here, self.groups, step, names), device_id_type=MESH,
             )
-            landed = pltpu.make_async_copy(landing, landing, recv.at[index])
-            result.append((stage, copy, landed))
-        return result
+            landed = pltpu.make_async_copy(landing, landing, self.recv.at[index])
+            self.copies.append((stage, copy, landed, (step, names)))
+
+    def start(self, stage):
+        for when, copy, _, _ in self.copies:
+            if when == stage:
+                copy.start()
+
+    def land(self):
+        for _, copy, landed, _ in self.copies:
+            (copy if landed is None else landed).wait()
+
+    def finish(self):
+        pass
+
+    def leave(self):
+        for _, copy, landed, _ in self.copies:
+            if landed is not None:
+                copy.wait_send()
+
+
+class Columns(Load):
+    def __init__(self, source, parts=1, **stages):
+        super().__init__(source, **stages)
+        self.parts = parts
+        self.rows = source.shape[0]
+        self.piece = source.shape[1] // (parts * MEMBERS)
+        shape = (self.groups * SIDES * self.rows, parts * self.piece)
+        self.outs = [jax.ShapeDtypeStruct(shape, source.dtype)]
+
+    def views(self, here, step, names, part):
+        mine, other, _, whence = self.around(here, step, names)
+        first = part * MEMBERS + here["x"] * SIDES + other
+        columns = pl.ds(part * self.piece, self.piece)
+        return (
+            self.src[0].at[:, at(first * self.piece, self.piece)],
+            self.dst[0].at[at((here["zh"] * SIDES + mine) * self.rows, self.rows), columns],
+            self.dst[0].at[at((whence * SIDES + other) * self.rows, self.rows), columns],
+        )
+
+
+class Few(Load):
+    space = pltpu.VMEM
+
+    def __init__(self, source, cube):
+        super().__init__(source)
+        self.cube = cube
+        count = MEMBERS if cube else self.groups * SIDES
+        self.outs = [jax.ShapeDtypeStruct((count,) + source.shape, source.dtype)]
+
+    def moves(self):
+        if self.cube:
+            return [((0, names), 0) for names in [()] + PEERS]
+        return super().moves()
+
+    def views(self, here, step, names, part):
+        if self.cube:
+            spot = self.dst[0].at[slot(*names)]
+            return self.src[0], spot, spot
+        mine, other, _, whence = self.around(here, step, names)
+        return (
+            self.src[0],
+            self.dst[0].at[here["zh"] * SIDES + mine],
+            self.dst[0].at[whence * SIDES + other],
+        )
+
+
+class Whole(Load):
+    def __init__(self, source, axis, **stages):
+        super().__init__(source, **stages)
+        self.axis = axis
+        self.outs = [jax.ShapeDtypeStruct(source.shape, source.dtype)]
+
+    def moves(self):
+        return [((0, ("x",)) if self.axis == "x" else (1, ()), 0)]
+
+    def views(self, here, step, names, part):
+        return self.src[0], self.dst[0], self.dst[0]
+
+
+class Swap:
+    def swap_scratch(self):
+        return [pltpu.SemaphoreType.DMA((3,))]
+
+    def give(self, total, sems):
+        self.kept = pltpu.make_async_copy(total, self.dst[0], sems.at[0])
+        self.kept.start()
+        self.given = None
+        if len(self.outs) > 1:
+            self.given = pltpu.make_async_remote_copy(
+                src_ref=total, dst_ref=self.dst[1], send_sem=sems.at[1], recv_sem=sems.at[2],
+                device_id=flip(self.here, "x"), device_id_type=MESH,
+            )
+            self.given.start()
+
+    def given_wait(self):
+        self.kept.wait()
+        if self.given is not None:
+            self.given.wait()
+
+
+class Owners(Load, Swap):
+    def __init__(self, source, parts=1, swap=False, fold=False, **stages):
+        super().__init__(source, **stages)
+        self.setup(source.shape[0], source.shape[1], source.dtype, parts, swap, fold)
+
+    def setup(self, depth, width, kind, parts, swap, fold):
+        self.parts = parts
+        self.fold = fold
+        self.kind = kind
+        self.rows = depth // (self.groups * SIDES)
+        self.piece = width // parts
+        self.wide = parts * SIDES * self.piece
+        total = (self.rows, self.piece if fold else self.wide)
+        self.total = total
+        self.outs = [jax.ShapeDtypeStruct(total, kind)] * (1 + swap)
+        self.swap = swap
+
+    def reached(self):
+        return super().reached() | ({(0, ("x",))} if self.swap else set())
+
+    def spaces(self):
+        return [pltpu.VMEM if self.fold else pl.ANY] * len(self.sources), [pl.ANY] * len(self.outs)
+
+    def scratch(self):
+        return self.semaphores() + self.swap_scratch() + [
+            pltpu.VMEM((self.groups, self.rows, self.wide), self.kind),
+            pltpu.VMEM(self.total, self.kind),
+        ]
+
+    def views(self, here, step, names, part):
+        mine, other, there, whence = self.around(here, step, names)
+        terms = self.more[1]
+        return (
+            self.slice_of(there * SIDES + other, part),
+            terms.at[here["zh"], :, at((part * SIDES + mine) * self.piece, self.piece)],
+            terms.at[whence, :, at((part * SIDES + other) * self.piece, self.piece)],
+        )
+
+    def slice_of(self, target, part):
+        return self.src[0].at[
+            at(target * self.rows, self.rows), pl.ds(part * self.piece, self.piece)
+        ]
+
+    def finish(self):
+        sems, terms, total = self.more[:3]
+        step = self.piece if self.fold else min(512, self.wide)
+
+        def add(start):
+            value = terms[0, :, pl.ds(start, step)].astype(jnp.float32)
+            for group in range(1, self.groups):
+                value = value + terms[group, :, pl.ds(start, step)].astype(jnp.float32)
+            return value
+
+        if self.fold:
+            value = add(0)
+            for side in range(1, SIDES):
+                value = value + add(side * step)
+            total[...] = value
+        else:
+
+            @pl.loop(0, self.wide // step)
+            def _(k):
+                start = pl.multiple_of(k * step, step)
+                total[:, pl.ds(start, step)] = add(start).astype(total.dtype)
+
+        self.give(total, sems)
+
+    def leave(self):
+        super().leave()
+        self.given_wait()
+
+
+class Product(Owners):
+    def __init__(self, left, right, parts=1, swap=False, **stages):
+        Load.__init__(self, left, **stages)
+        self.sources = [left, right]
+        self.setup(left.shape[1], right.shape[1], jnp.bfloat16, parts, swap, False)
+
+    def scratch(self):
+        depth, width = self.sources[0].shape[0], self.sources[1].shape[1]
+        return super().scratch() + [
+            pltpu.VMEM((2, depth, 2 * self.rows), jnp.bfloat16),
+            pltpu.VMEM((depth, width), jnp.bfloat16),
+            pltpu.VMEM((self.groups * SIDES * self.rows, width), jnp.bfloat16),
+            pltpu.SemaphoreType.DMA((3,)),
+        ]
+
+    def slice_of(self, target, part):
+        return self.more[5].at[
+            at(target * self.rows, self.rows), pl.ds(part * self.piece, self.piece)
+        ]
+
+    def tiles(self):
+        order = [
+            (step, names)
+            for step in reversed(range(self.groups))
+            for names in SIDE_PEERS
+            if "c" not in names
+        ]
+        return order
+
+    def first_row(self, step, names):
+        _, other, there, _ = self.around(self.here, step, names)
+        return (there * SIDES + (other // 2) * 2) * self.rows
+
+    def fetch(self, k):
+        step, names = self.tiles()[k]
+        left = self.src[0].at[:, at(self.first_row(step, names), 2 * self.rows)]
+        return pltpu.make_async_copy(left, self.more[3].at[k % 2], self.more[6].at[k % 2])
+
+    def begin(self):
+        self.right = pltpu.make_async_copy(self.src[1], self.more[4], self.more[6].at[2])
+        self.right.start()
+        self.fetch(0).start()
+        self.fetch(1).start()
+
+    def start(self, stage):
+        tiles = self.tiles()
+        _, _, _, lefts, right, result, _ = self.more
+        for k, (step, names) in enumerate(tiles):
+            if self.stages[1 if step else 0] != stage:
+                continue
+            if k == 0:
+                self.right.wait()
+            self.fetch(k).wait()
+            rows = at(self.first_row(step, names), 2 * self.rows)
+            wide = min(256, self.sources[1].shape[1])
+            left = lefts[k % 2]
+            for column in range(0, self.sources[1].shape[1], wide):
+                columns = pl.ds(column, min(wide, self.sources[1].shape[1] - column))
+                result[rows, columns] = lax.dot_general(
+                    left, right[:, columns], (((0,), (0,)), ((), ())),
+                    preferred_element_type=jnp.float32,
+                ).astype(jnp.bfloat16)
+            if k + 2 < len(tiles):
+                self.fetch(k + 2).start()
+            for _, copy, _, peer in self.copies:
+                if peer in ((step, names), (step, names + ("c",))):
+                    copy.start()
+
+
+class Pair(Load, Swap):
+    def __init__(self, source, **stages):
+        super().__init__(source, **stages)
+        self.outs = [jax.ShapeDtypeStruct(source.shape, source.dtype)] * 2
+
+    def spaces(self):
+        return [pltpu.VMEM], [pl.ANY] * 2
+
+    def moves(self):
+        return [((1, ()), 0)]
+
+    def reached(self):
+        return {(1, ()), (0, ("x",))}
+
+    def scratch(self):
+        shape = self.outs[0].shape
+        return self.semaphores() + self.swap_scratch() + [
+            pltpu.VMEM(shape, jnp.bfloat16), pltpu.VMEM(shape, jnp.bfloat16)
+        ]
+
+    def views(self, here, step, names, part):
+        return self.src[0], self.more[1], self.more[1]
+
+    def finish(self):
+        sems, came, total = self.more
+        total[...] = (
+            self.src[0][...].astype(jnp.float32) + came[...].astype(jnp.float32)
+        ).astype(jnp.bfloat16)
+        self.give(total, sems)
+
+    def leave(self):
+        super().leave()
+        self.given_wait()
 
 
 class Cargo:
     def __init__(self, loads):
         self.loads = loads
-        self.n = len(loads)
-        self.sources = [load.source for load in loads]
-        self.specs = [pl.BlockSpec(memory_space=load.space) for load in loads]
-        self.outs = [load.out for load in loads]
+        self.sources = [s for load in loads for s in load.sources]
+        self.outs = [o for load in loads for o in load.outs]
+        self.in_specs = [pl.BlockSpec(memory_space=s) for load in loads for s in load.spaces()[0]]
+        self.out_specs = [pl.BlockSpec(memory_space=s) for load in loads for s in load.spaces()[1]]
         self.scratch = [s for load in loads for s in load.scratch()]
+
+    def bind(self, here, sources, targets, scratch):
+        sources, targets, scratch = list(sources), list(targets), list(scratch)
+
+        def take(refs, count):
+            taken = refs[:count]
+            del refs[:count]
+            return taken
+
+        for load in self.loads:
+            load.bind(
+                here,
+                take(sources, len(load.sources)),
+                take(targets, len(load.outs)),
+                take(scratch, len(load.scratch())),
+            )
+            if hasattr(load, "begin"):
+                load.begin()
 
     def greet(self, here, names):
         reached = {(0, n) for n in names}
         for load in self.loads:
-            reached |= set(load.devices(here))
+            reached |= load.reached()
         groups = lax.axis_size("zh")
         greet([owner_at(here, groups, step, n) for step, n in sorted(reached)])
 
-    def prepare(self, here, sources, targets, semaphores):
-        self.copies = []
-        for k, load in enumerate(self.loads):
-            self.copies += load.copies(
-                here, sources[k], targets[k], semaphores[2 * k], semaphores[2 * k + 1]
-            )
-
     def start(self, stage):
-        for when, copy, _ in self.copies:
-            if when == stage:
-                copy.start()
-
-    def wait(self):
-        for _, copy, landing in self.copies:
-            if landing is None:
-                copy.wait()
-            else:
-                landing.wait()
-        for _, copy, landing in self.copies:
-            if landing is not None:
-                copy.wait_send()
+        for load in self.loads:
+            load.start(stage)
+
+    def finish(self, early=False):
+        for load in self.loads:
+            if load.early == early:
+                load.land()
+                load.finish()
+        if not early:
+            for load in self.loads:
+                load.leave()
 
 
 GATHER_STAGES = (0, 1, 2, 3)
 NEAR = [("x",), ("zl",), ("y",), ("c",)]
 
 
-def call(body, name, ident, cargo, operand, space, out, out_space, scratch, vmem=40):
+def call(body, name, ident, cargo, operand, space, out, out_space, scratch):
+    held = [out] * (out_space == pltpu.VMEM) + [operand] * (space == pltpu.VMEM)
+    held += [s for s in scratch + cargo.scratch if s.memory_space == pltpu.VMEM]
+    held += [s for load in cargo.loads if load.spaces()[0][0] == pltpu.VMEM for s in load.sources]
+    vmem = sum(math.prod(s.shape) * jnp.dtype(s.dtype).itemsize for s in held) + 6 * MIB
     return pl.pallas_call(
-        body,
+        functools.partial(body, cargo),
         out_shape=[out] + cargo.outs,
-        in_specs=[pl.BlockSpec(memory_space=space)] + cargo.specs,
-        out_specs=[pl.BlockSpec(memory_space=out_space)] + cargo.specs,
+        in_specs=[pl.BlockSpec(memory_space=space)] + cargo.in_specs,
+        out_specs=[pl.BlockSpec(memory_space=out_space)] + cargo.out_specs,
         scratch_shapes=scratch + cargo.scratch,
         compiler_params=pltpu.CompilerParams(
-            collective_id=ident, has_side_effects=True, vmem_limit_bytes=vmem * MIB
+            collective_id=ident, has_side_effects=True, vmem_limit_bytes=vmem
         ),
         cost_estimate=pl.CostEstimate(flops=0, bytes_accessed=100 * MIB, transcendentals=0),
         name=name,
@@ -228,33 +491,34 @@
 
 
 def gather_kernel(orders, cargo, x_ref, *refs):
-    n = cargo.n
-    sources, o_ref, targets = refs[:n], refs[n], refs[n + 1 : 2 * n + 1]
-    send_sem, recv_sem, core_send, core_recv, own_sem = refs[2 * n + 1 : 2 * n + 6]
+    n, m = len(cargo.sources), len(cargo.outs)
+    sources, o_ref, targets = refs[:n], refs[n], refs[n + 1 : n + 1 + m]
+    send_sem, recv_sem, core_send, core_recv, own_sem = refs[n + m + 1 : n + m + 6]
     here = place()
     spans = [pl.ds(r0, size) for _, r0, size in orders]
     orders = [o for o, _, _ in orders]
     pieces = range(len(orders))
-    cargo.prepare(here, sources, targets, refs[2 * n + 6 :])
+    cargo.bind(here, sources, targets, refs[n + m + 6 :])
     cargo.greet(here, NEAR)
-    own = pltpu.make_async_copy(x_ref, o_ref.at[with_bits(here, ())], own_sem)
-
-    def piece_of(p, mask):
-        spot = o_ref.at[with_bits(here, subset(orders[p], mask)), spans[p]]
-        return (x_ref.at[spans[p]] if mask == 0 else spot), spot
+    own = pltpu.make_async_copy(x_ref, o_ref.at[0], own_sem)
+
+    def spot(p, *names):
+        return o_ref.at[slot(*names), spans[p]]
+
+    def source(p, mask):
+        return spot(p, *subset(orders[p], mask)) if mask else x_ref.at[spans[p]]
 
     def over(p, mask, k):
-        source, spot = piece_of(p, mask)
+        whole = mask | 1 << k
         return pltpu.make_async_remote_copy(
-            src_ref=source, dst_ref=spot,
-            send_sem=send_sem.at[p, mask | 1 << k], recv_sem=recv_sem.at[p, mask | 1 << k],
+            src_ref=source(p, mask), dst_ref=spot(p, *subset(orders[p], whole)),
+            send_sem=send_sem.at[p, whole], recv_sem=recv_sem.at[p, whole],
             device_id=flip(here, orders[p][k]), device_id_type=MESH,
         )
 
     def across(p, mask):
-        source, spot = piece_of(p, mask)
         return pltpu.make_async_remote_copy(
-            src_ref=source, dst_ref=spot,
+            src_ref=source(p, mask), dst_ref=spot(p, "c", *subset(orders[p], mask)),
             send_sem=core_send.at[p, mask], recv_sem=core_recv.at[p, mask],
             device_id=flip(here, "c"), device_id_type=MESH,
         )
@@ -263,8 +527,8 @@
     for mask in range(8):
         for p in pieces:
             if mask:
-                _, spot = piece_of(p, mask)
-                pltpu.make_async_copy(spot, spot, recv_sem.at[p, mask]).wait()
+                landing = spot(p, *subset(orders[p], mask))
+                pltpu.make_async_copy(landing, landing, recv_sem.at[p, mask]).wait()
             for k in range(mask.bit_length(), 3):
                 sent.append(over(p, mask, k))
                 sent[-1].start()
@@ -277,21 +541,20 @@
             cargo.start(GATHER_STAGES.index(mask))
     for mask in range(8):
         for p in pieces:
-            spot = o_ref.at[with_bits(here, subset(orders[p], mask) + ("c",)), spans[p]]
-            pltpu.make_async_copy(spot, spot, core_recv.at[p, mask]).wait()
+            landing = spot(p, "c", *subset(orders[p], mask))
+            pltpu.make_async_copy(landing, landing, core_recv.at[p, mask]).wait()
     for copy in sent:
         copy.wait_send()
     own.wait()
-    cargo.wait()
+    cargo.finish()
 
 
 def gather_cube(block, ident, loads=(), orders=None):
     rows, width = block.shape
     orders = orders or thirds(rows)
-    cargo = Cargo(list(loads))
     out = call(
-        functools.partial(gather_kernel, orders, cargo),
-        "gather_cube", ident, cargo, block, pl.ANY,
+        functools.partial(gather_kernel, orders),
+        "gather_cube", ident, Cargo(list(loads)), block, pl.ANY,
         jax.ShapeDtypeStruct((MEMBERS, rows, width), block.dtype), pl.ANY,
         [pltpu.SemaphoreType.DMA((len(orders), 8))] * 4 + [pltpu.SemaphoreType.DMA(())],
     )
@@ -299,20 +562,19 @@
 
 
 def scatter_kernel(orders, cargo, p_ref, *refs):
-    n = cargo.n
-    sources, o_ref, targets = refs[:n], refs[n], refs[n + 1 : 2 * n + 1]
-    acc, rcore, came, core_send, core_recv, send_sem, recv_sem = refs[2 * n + 1 : 2 * n + 8]
+    n, m = len(cargo.sources), len(cargo.outs)
+    sources, o_ref, targets = refs[:n], refs[n], refs[n + 1 : n + 1 + m]
+    acc, rcore, came, core_send, core_recv, send_sem, recv_sem = refs[n + m + 1 : n + m + 8]
     here = place()
     spans = [pl.ds(r0, size) for _, r0, size in orders]
     orders = [o for o, _, _ in orders]
     pieces = range(len(orders))
-    cargo.prepare(here, sources, targets, refs[2 * n + 8 :])
+    cargo.bind(here, sources, targets, refs[n + m + 8 :])
     cargo.greet(here, NEAR)
 
     def away(p, mask):
-        names = subset(orders[p], mask)
         return pltpu.make_async_remote_copy(
-            src_ref=p_ref.at[with_bits(here, names + ("c",)), spans[p]],
+            src_ref=p_ref.at[slot("c", *subset(orders[p], mask)), spans[p]],
             dst_ref=rcore.at[mask, spans[p]],
             send_sem=core_send.at[p, mask], recv_sem=core_recv.at[p, mask],
             device_id=flip(here, "c"), device_id_type=MESH,
@@ -334,24 +596,18 @@
             device_id=flip(here, orders[p][k]), device_id_type=MESH,
         )
 
-    def add(p, mask, other):
-        acc[mask, spans[p]] = acc[mask, spans[p]] + other[...]
-
-    def first_sum(p, mask):
-        own = with_bits(here, subset(orders[p], mask))
-        acc[mask, spans[p]] = p_ref[own, spans[p]] + rcore[mask, spans[p]]
-
     for mask in sequence:
         for p in pieces:
             away(p, mask).wait_recv()
-            first_sum(p, mask)
+            own = slot(*subset(orders[p], mask))
+            acc[mask, spans[p]] = p_ref[own, spans[p]] + rcore[mask, spans[p]]
             if mask & 1:
                 sent.append(over(p, mask))
                 sent[-1].start()
     cargo.start(1)
     for k in range(3):
         low = 1 << k
-        for mask in [m for m in (6, 2, 4, 0) if m & (2 * low - 1) == 0]:
+        for mask in [b for b in (6, 2, 4, 0) if b & (2 * low - 1) == 0]:
             for p in pieces:
                 over(p, mask | low).wait_recv()
                 if mask == 0 and k == 2:
@@ -359,72 +615,56 @@
                         4, spans[p]
                     ].astype(jnp.float32)
                     continue
-                add(p, mask, came.at[mask | low, spans[p]])
+                acc[mask, spans[p]] = acc[mask, spans[p]] + came[mask | low, spans[p]]
                 if mask & (2 * low):
                     sent.append(over(p, mask))
                     sent[-1].start()
         if k < 2:
             cargo.start(2 + k)
+        if k == 1:
+            cargo.finish(early=True)
     for copy in sent:
         copy.wait_send()
-    cargo.wait()
+    cargo.finish()
 
 
 def scatter_cube(partial, ident, loads=(), orders=None):
     total, width = partial.shape
     rows = total // MEMBERS
     orders = orders or thirds(rows)
-    cargo = Cargo(list(loads))
     return call(
-        functools.partial(scatter_kernel, orders, cargo),
-        "scatter_cube", ident, cargo, partial.astype(jnp.bfloat16).reshape(MEMBERS, rows, width),
-        pltpu.VMEM,
+        functools.partial(scatter_kernel, orders),
+        "scatter_cube", ident, Cargo(list(loads)),
+        partial.astype(jnp.bfloat16).reshape(MEMBERS, rows, width), pltpu.VMEM,
         jax.ShapeDtypeStruct((rows, width), jnp.float32), pltpu.VMEM,
         [pltpu.VMEM((8, rows, width), jnp.bfloat16)] * 3
         + [pltpu.SemaphoreType.DMA((len(orders), 8))] * 4,
     )
-
-
-def carry_kernel(cargo, *refs):
-    n = cargo.n
-    here = place()
-    cargo.prepare(here, refs[:n], refs[n : 2 * n], refs[2 * n :])
-    cargo.greet(here, [])
-    cargo.start(0)
-    cargo.wait()
-
-
-def carry(ident, loads):
-    cargo = Cargo(list(loads))
-    return pl.pallas_call(
-        functools.partial(carry_kernel, cargo),
-        out_shape=cargo.outs,
-        in_specs=cargo.specs,
-        out_specs=cargo.specs,
-        scratch_shapes=cargo.scratch,
-        compiler_params=pltpu.CompilerParams(collective_id=ident, has_side_effects=True),
-        cost_estimate=pl.CostEstimate(flops=0, bytes_accessed=50 * MIB, transcendentals=0),
-        name="carry",
-    )(*cargo.sources)
 
 
 def exchange_kernel(v_ref, o_ref, slots, send_sem, recv_sem):
     here = place()
     greet([flip(here, *names) for names in PEERS])
     copies = []
-    for m in range(1, MEMBERS):
+    for names in PEERS:
+        k = slot(*names)
         copies.append(pltpu.make_async_remote_copy(
-            src_ref=v_ref, dst_ref=slots.at[m], send_sem=send_sem.at[m], recv_sem=recv_sem.at[m],
-            device_id=flip(here, *PEERS[m - 1]), device_id_type=MESH,
+            src_ref=v_ref, dst_ref=slots.at[k], send_sem=send_sem.at[k], recv_sem=recv_sem.at[k],
+            device_id=flip(here, *names), device_id_type=MESH,
         ))
         copies[-1].start()
     for copy in copies:
         copy.wait_recv()
     slots[0] = v_ref[...]
-    terms = [slots[m] for m in range(MEMBERS)]
-    while len(terms) > 1:
-        terms = [terms[2 * i] + terms[2 * i + 1] for i in range(len(terms) // 2)]
-    o_ref[...] = terms[0]
+    for row in range(v_ref.shape[0]):
+        kind, mine = divmod(row, MEMBERS)
+        terms = [
+            slots[k, pl.ds(kind * MEMBERS + SLOT[SLOTS[mine] ^ SLOTS[k]], 1), :]
+            for k in range(MEMBERS)
+        ]
+        while len(terms) > 1:
+            terms = [terms[2 * i] + terms[2 * i + 1] for i in range(len(terms) // 2)]
+        o_ref[pl.ds(row, 1), :] = terms[0]
     for copy in copies:
         copy.wait_send()
 
@@ -490,13 +730,9 @@
 
 def row_sums(pair, ident):
     total = pair[0].shape[0]
-    flat = jnp.concatenate([v.reshape(total // 128, 128) for v in pair], axis=0)
+    flat = jnp.concatenate([v.reshape(MEMBERS, total // MEMBERS) for v in pair], axis=0)
     summed = sum_cube(flat, ident).reshape(2, total, 1)
     return summed[0], summed[1]
-
-
-def owned_sum(terms):
-    return jnp.sum(terms.astype(jnp.float32), axis=0).astype(jnp.bfloat16)
 
 
 def finish_kernel(mine_ref, came_ref, o_ref):
@@ -523,6 +759,12 @@
     )(mine, came)
 
 
+def owners_product(left, right, parts=1, **options):
+    if left.shape[1] // (lax.axis_size("zh") * SIDES) % 128 == 0:
+        return Product(left, right, parts, **options)
+    return Owners(contract_first(left, right).astype(jnp.bfloat16), parts, **options)
+
+
 def heads_are_owners(rows):
     return lax.axis_size("zh") == 2 and rows == HD
 
@@ -560,9 +802,9 @@
 
     gain_part = jnp.pad(gains.astype(jnp.float32).T, ((0, 4), (0, 0)))
     begin_part = jnp.broadcast_to(seq_begin.astype(jnp.float32)[None, :], (8, count_rows))
-    loads = [Load("plane", gain_part), Load("cube", begin_part), Load("columns", w_qkv, 3)]
+    loads = [Few(gain_part, False), Few(begin_part, True), Columns(w_qkv, 3)]
     if direct:
-        loads.append(Load("zh", w_out))
+        loads.append(Whole(w_out, "zh"))
     tokens_all, gain_all, begin_all, qkv_cols, *out_other = gather_cube(
         tokens, 1, loads, halves(count_rows, "zl", "y", "x")
     )
@@ -620,12 +862,12 @@
     y_last = halves(count_rows, "zl", "x", "y")
     branch, down_cols = scatter_cube(
         jnp.dot(attended, out_rows, preferred_element_type=jnp.float32),
-        3, [Load("columns", w_down_t, near=1)], x_most,
+        3, [Columns(w_down_t, near=1)], x_most,
     )
     branch_norm, branch_inv = normalize(branch, gain_rows[2])
     middle = tokens.astype(jnp.float32) + branch_norm
     middle_all, gate_up_cols = gather_cube(
-        middle.astype(jnp.bfloat16), 4, [Load("columns", w_gate_up, 2, near=3)], x_last
+        middle.astype(jnp.bfloat16), 4, [Columns(w_gate_up, 2, near=3)], x_last
     )
     gate_up = jnp.dot(middle_all, gate_up_cols, preferred_element_type=jnp.float32)
     gate_part, up_part = jnp.split(gate_up, 2, axis=1)
@@ -637,22 +879,22 @@
     upstream = cotangent.astype(jnp.float32)
     feed_grad, gain_feed = norm_back(upstream, feed_out, feed_inv, gain_rows[3])
     (feed_all,) = gather_cube(feed_grad.astype(jnp.bfloat16), 6)
-    down_grad = contract_first(feed_all, hidden_bf).astype(jnp.bfloat16)
     hidden_grad = jnp.dot(feed_all, down_cols, preferred_element_type=jnp.float32)
     gate_up_bf = jnp.concatenate(silu_grads(hidden_grad, gate_part, up_part), axis=1)
-    gate_up_grad = contract_first(middle_all, gate_up_bf).astype(jnp.bfloat16)
     middle_part = contract_last(gate_up_bf, gate_up_cols)
-    middle_sum, gate_up_terms = scatter_cube(
-        middle_part, 7, [Load("owners", gate_up_grad, 2)], x_most
+    middle_sum, gate_up_sum = scatter_cube(
+        middle_part, 7, [owners_product(middle_all, gate_up_bf, 2, near=1)], x_most
     )
     middle_grad = upstream + middle_sum
     branch_grad, gain_branch = norm_back(middle_grad, branch, branch_inv, gain_rows[2])
-    gate_up_sum = owned_sum(gate_up_terms)
-    branch_all, down_terms, gate_up_other = gather_cube(
+    branch_all, down_sum, gate_up_other = gather_cube(
         branch_grad.astype(jnp.bfloat16), 8,
-        [Load("owners", down_grad, far=1, near=3), Load("x", gate_up_sum, near=1)], y_last,
-    )
-    down_sum = owned_sum(down_terms)
+        [
+            owners_product(feed_all, hidden_bf, far=1, near=3),
+            Whole(gate_up_sum, "x", near=1),
+        ], y_last,
+    )
+    down_other = lax.ppermute(down_sum, "x", [(0, 1), (1, 0)])
     out_grad = contract_first(attended, branch_all)
     attended_grad = blocks(contract_last(branch_all, out_rows).astype(jnp.bfloat16))
     prob_grad = jnp.einsum(
@@ -684,7 +926,6 @@
     projected_bf = jnp.concatenate([query_raw_grad, key_raw_grad, value_grad], axis=1).astype(
         jnp.bfloat16
     )
-    qkv_grad = contract_first(tokens_all, projected_bf).astype(jnp.bfloat16)
 
     gain_head = jnp.stack(
         [jnp.sum(query_grad * query_unit, axis=0), jnp.sum(key_grad * key_unit, axis=0)]
@@ -702,25 +943,18 @@
         gain_terms.reshape(4, groups * SIDES, owned).transpose(1, 0, 2),
         ((0, 0), (0, 4), (0, lanes - owned)),
     ).reshape(groups * SIDES * 8, lanes)
-    loads = [Load("owners", qkv_grad, 3), Load("x", down_sum, near=2), Load("owners", gain_terms)]
+    loads = [
+        owners_product(tokens_all, projected_bf, 3, swap=True, near=1, early=True),
+        Owners(gain_terms, swap=True, fold=True, early=True),
+    ]
     if direct:
-        out_bf = out_grad.astype(jnp.bfloat16)
-        loads.append(Load("zh", out_bf))
-    tokens_sum, qkv_terms, down_other, gain_came, *out_came = scatter_cube(
-        contract_last(projected_bf, qkv_cols), 10, loads, x_or_y
+        loads.append(Pair(out_grad.astype(jnp.bfloat16), early=True))
+    tokens_sum, qkv_sum, qkv_other, gain_sum, gain_other, *out_both = scatter_cube(
+        contract_last(projected_bf, qkv_cols), 10, loads, x_most
     )
     grad_tokens = middle_grad + tokens_sum
-    qkv_sum = owned_sum(qkv_terms)
-    gain_sum = jnp.sum(gain_came.reshape(groups, 8, SIDES, lanes), axis=(0, 2))
-    loads = [Load("x", qkv_sum), Load("x", gain_sum)]
     if direct:
-        out_sum = (out_bf.astype(jnp.float32) + out_came[0].astype(jnp.float32)).astype(
-            jnp.bfloat16
-        )
-        loads.append(Load("x", out_sum))
-    qkv_other, gain_other, *out_other = carry(11, loads)
-    if direct:
-        grad_out = jnp.where(same, out_sum, out_other[0]).astype(jnp.float32)
+        grad_out = jnp.where(same, out_both[0], out_both[1]).astype(jnp.float32)
     else:
         grad_out = summed_head_rows(out_grad, owned)
     grad_qkv = whole_rows(qkv_sum, qkv_other, 3)

time: 782 us -> 720 us (0.921)
  matrix products: 105 us -> 69.7 us
  Pallas kernels: 600 us -> 586 us
  local copies, waits for them, and re-layouts: 28.2 us -> 16.1 us
    dot_general x4 -> x1, matrix products: 35.3 us -> 1.28 us  [contract_first(): lax.dot_general(operand, matrix, (((0,), (0,)), ((), ())), preferred_elem...]
    pallas_call x9 -> x8, Pallas kernels: 571 us -> 556 us  [call(): pl.pallas_call(functools.partial(body, cargo), out_shape=[out] + cargo.ou...]
    unnamed x118 -> x100, local copies, waits for them, and re-layouts: 18.7 us -> 9.25 us
  transfers between devices with their start and end apart: 0 -> 1, of which waited for: 0 -> 0; matrix products, arithmetic and copies ran while one was open for 0% -> 6% of each run, Pallas kernels for 0% -> 14%
where the time goes in v4:
time: 720 us; the launch traced here: 713 us
  Pallas kernels  586 us (81%)
  matrix products  69.7 us (10%)
  other arithmetic  38.7 us (5%)
  local copies, waits for them, and re-layouts  16.1 us (2%)
    pallas_call x8, Pallas kernels, call(): pl.pallas_call(functools.partial(body, cargo), out_shape=[out] + cargo.ou...  556 us
    dot_general x4, matrix products, contract_last(): lax.dot_general(operand, matrix, (((1,), (1,)), ((), ())), preferred_elem...  27.9 us
    pallas_call x2, Pallas kernels, sum_cube(): pl.pallas_call(exchange_kernel, out_shape=jax.ShapeDtypeStruct(shape, jnp...  18.5 us
  transfers between devices with their start and end apart: 1, of which 0 were waited for; matrix products, arithmetic and copies ran while one was open for 6% of the time, Pallas kernels for 14%

profile of v4, /device:TPU:0, one launch (start us, length us, event | category | flops | bytes accessed | tf_op | source)
XLA Modules:
  0.0 713.4 jit_solution(13259699844320814470)
XLA Ops:
  0.6 0.7 pad_convert_fusion.refs_0_
  1.3 0.7 fusion.44
  2.4 1.0 copy-done.5
  3.4 1.0 copy-done.9
  4.5 1.4 copy-done.14
  5.9 68.6 %gather_cube.4 = (bf16[16,128,2048]{2,1,0:T(8,128)(2,1)S(1)}, f32[16,8,128]{2,1,0:T(8,128)S(1)}, f32[16,8,128]{2,1,0:T(8,128)S(1)}, bf16[2048,384]{1,0:T(8,128)(2,1)S(1)}, bf16[128,2048]{1,0:T(8,128)(2,1)S(1)}) custom-call(bf16[128,2048]{1,0:T(8,128)(2,1)S(1)} %copy-done.5, f32[8,128]{1,0:T(8,128)S(1)} %pad_convert_fusion.refs_0_, ...), custom_call_target="tpu_custom_call" | custom-call | bytes 104857600 | tf_op jit(solution)/shard_map/gather_cube/pallas_call | solution.py:479
  74.5 3.6 fusion.56
  78.3 1.2 fusion.53
  79.4 1.0 copy.54
  80.5 0.3 copy.55
  80.9 1.9 copy.56
  82.8 0.3 multiply_reduce_fusion.9
  83.2 0.3 multiply_reduce_fusion.10
  83.5 0.6 pad_maximum_fusion.14.v_ref
  84.2 9.2 %sum_cube.2 = f32[32,128]{1,0:T(8,128)} custom-call(f32[32,128]{1,0:T(8,128)} %pad_maximum_fusion.14.v_ref), custom_call_target="tpu_custom_call" | custom-call | bytes 20971520 | tf_op jit(solution)/shard_map/sum_cube/pallas_call | solution.py:674
  93.3 0.7 rsqrt_bitcast_fusion.1
  94.1 0.3 multiply_multiply_fusion.1
  94.4 0.3 multiply_multiply_fusion
  94.8 6.4 fusion.32
  101.2 3.5 fusion.55
  104.8 2.7 convolution_convert_fusion.6
  107.5 2.3 convolution_convert_fusion.3
  109.9 64.8 %scatter_cube.4 = (f32[128,2048]{1,0:T(8,128)S(1)}, bf16[2048,512]{1,0:T(8,128)(2,1)S(1)}) custom-call(bf16[16,128,2048]{2,1,0:T(8,128)(2,1)S(1)} %bitcast.83, bf16[128,8192]{1,0:T(8,128)(2,1)S(1)} %copy-done.8), custom_call_target="tpu_custom_call" | custom-call | bytes 104857600 | tf_op jit(solution)/shard_map/scatter_cube/pallas_call | solution.py:479
  174.9 0.2 fusion.40.x_ref
  175.1 84.0 %gather_cube.5 = (bf16[16,128,2048]{2,1,0:T(8,128)(2,1)S(1)}, bf16[2048,1024]{1,0:T(8,128)(2,1)S(1)}) custom-call(bf16[128,2048]{1,0:T(8,128)(2,1)S(1)} %fusion.40.x_ref, bf16[128,16384]{1,0:T(8,128)(2,1)S(1)} %copy-done.7), custom_call_target="tpu_custom_call" | custom-call | bytes 104857600 | tf_op jit(solution)/shard_map/gather_cube/pallas_call | solution.py:479
  259.2 3.2 copy-done.2
  262.4 11.0 %fusion.57 = f32[2048,1024]{1,0:T(8,128)} fusion(bf16[2048,2048]{1,0:T(8,128)(2,1)S(1)} %bitcast.92, bf16[2048,1024]{1,0:T(8,128)(2,1)S(1)} %get-tuple-element.35), kind=kOutput, calls=%fused_computation.131 | convolution fusion | flops 8589934592 | bytes 20971520 | tf_op jit(solution)/shard_map/dot_general | solution.py:872
  273.4 4.8 multiply_convert_fusion.2.refs_1_
  278.2 5.0 convolution_convert_fusion.2
  283.2 45.5 %scatter_cube.5 = f32[128,2048]{1,0:T(8,128)S(1)} custom-call(bf16[16,128,2048]{2,1,0:T(8,128)(2,1)S(1)} %bitcast.89), custom_call_target="tpu_custom_call" | custom-call | bytes 104857600 | tf_op jit(solution)/shard_map/scatter_cube/pallas_call | solution.py:479
  328.9 0.4 fusion.39
  329.3 0.3 fusion.26.x_ref
  329.6 33.1 %gather_cube.6 = bf16[16,128,2048]{2,1,0:T(8,128)(2,1)S(1)} custom-call(bf16[128,2048]{1,0:T(8,128)(2,1)S(1)} %fusion.26.x_ref), custom_call_target="tpu_custom_call" | custom-call | bytes 104857600 | tf_op jit(solution)/shard_map/gather_cube/pallas_call | solution.py:479
  362.7 9.7 %multiply_convert_fusion.1 = (bf16[2048,512]{1,0:T(8,128)(2,1)}, bf16[2048,512]{1,0:T(8,128)(2,1)}) fusion(f32[2048,1024]{1,0:T(8,128)} %fusion.57, bf16[2048,2048]{1,0:T(8,128)(2,1)S(1)} %bitcast.84, bf16[2048,512]{1,0:T(8,128)(2,1)S(1)} %copy-done.20), kind=kOutput, calls=%fused_computation.7 | convolution fusion | flops 4308598784 | bytes 23068672 | tf_op jit(solution)/shard_map/dot_general | solution.py:882
  372.4 13.4 %convolution_convert_fusion.1 = bf16[2048,2048]{1,0:T(8,128)(2,1)} fusion(bf16[2048,1024]{1,0:T(8,128)(2,1)S(1)} %copy-done.18, bf16[2048,512]{1,0:T(8,128)(2,1)} %get-tuple-element.58, bf16[2048,512]{1,0:T(8,128)(2,1)} %get-tuple-element.57), kind=kOutput, calls=%fused_computation.2 | convolution fusion | flops 8602517504 | bytes 16777216 | tf_op jit(solution)/shard_map/dot_general | solution.py:720
  385.9 2.8 pad_maximum_fusion.refs_1_
  388.7 99.1 %scatter_cube.6 = (f32[128,2048]{1,0:T(8,128)S(1)}, bf16[128,8192]{1,0:T(8,128)(2,1)S(1)}) custom-call(bf16[16,128,2048]{2,1,0:T(8,128)(2,1)} %bitcast.97, bf16[2048,2048]{1,0:T(8,128)(2,1)} %bitcast.93, bf16[2048,1024]{1,0:T(8,128)(2,1)S(1)} %pad_maximum_fusion.refs_1_), custom_call_target="tpu_custom_call" | custom-call | bytes 104857600 | tf_op jit(solution)/shard_map/scatter_cube/pallas_call | solution.py:479
  487.8 0.4 multiply_reduce_fusion
  488.2 1.3 multiply_convert_fusion.6
  489.5 76.2 %gather_cube.7 = (bf16[16,128,2048]{2,1,0:T(8,128)(2,1)S(1)}, bf16[128,4096]{1,0:T(8,128)(2,1)}, bf16[128,8192]{1,0:T(8,128)(2,1)S(1)}) custom-call(bf16[128,2048]{1,0:T(8,128)(2,1)S(1)} %get-tuple-element.65.x_ref, bf16[2048,2048]{1,0:T(8,128)(2,1)S(1)} %bitcast.85, bf16[2048,512]{1,0:T(8,128)(2,1)S(1)} %multiply_convert_fusion.2.refs_1_, ...), custom_call_target="tpu_custom_call" | custom-call | bytes 104857600 | tf_op jit(solution)/shard_map/gather_cube/pallas_call | solution.py:479
  565.7 0.9 collective-permute-start
  566.7 3.3 convolution_convert_fusion.4
  569.9 3.3 convolution_convert_fusion.5
  573.3 2.2 multiply_reduce_fusion.5
  575.7 0.6 convolution_multiply_fusion.1
  576.3 1.6 convolution_multiply_fusion
  577.9 1.3 copy.43
  579.2 2.5 copy.45
  581.8 7.6 %fusion.27 = (f32[2048,64]{1,0:T(8,128)S(1)}, f32[2048,64]{1,0:T(8,128)S(1)}, f32[2048,64]{1,0:T(8,128)S(1)}, f32[2048,64]{1,0:T(8,128)S(1)}) fusion(f32[2048,128]{1,0:T(8,128)} %bitcast.95, f32[64]{0:T(128)S(1)} %multiply_power_fusion, f32[2048]{0:T(1024)S(1)} %bitcast_subtract_fusion, f32[2048,128]{1,0:T(8,128)} %bitcast.96), kind=kLoop, calls=%fused_computation.49 | loop fusion | flops 1835008 | bytes 4202752 | tf_op jit(solution)/shard_map/sub | solution.py:701
  589.4 1.9 multiply_reduce_fusion.1
  591.4 0.6 pad_maximum_fusion.15.v_ref
  592.0 9.3 %sum_cube.3 = f32[32,128]{1,0:T(8,128)} custom-call(f32[32,128]{1,0:T(8,128)} %pad_maximum_fusion.15.v_ref), custom_call_target="tpu_custom_call" | custom-call | bytes 20971520 | tf_op jit(solution)/shard_map/sum_cube/pallas_call | solution.py:674
  601.4 0.9 multiply_bitcast_fusion.1
  602.3 2.6 multiply_convert_fusion.3
  604.9 1.0 multiply_convert_fusion.4
  605.9 6.2 convolution_convert_fusion
  612.4 1.3 fusion.1.refs_3_
  613.8 84.7 %scatter_cube.7 = (f32[128,2048]{1,0:T(8,128)S(1)}, bf16[128,3072]{1,0:T(8,128)(2,1)S(1)}, bf16[128,3072]{1,0:T(8,128)(2,1)S(1)}, f32[8,128]{1,0:T(8,128)S(1)}, ...) custom-call(bf16[16,128,2048]{2,1,0:T(8,128)(2,1)S(1)} %bitcast.94, ...), custom_call_target="tpu_custom_call" | custom-call | bytes 104857600 | tf_op jit(solution)/shard_map/scatter_cube/pallas_call | solution.py:479
  698.5 0.6 slice_bitcast_fusion.2
  699.1 4.9 whole_rows.4
  704.0 2.8 whole_rows.3
  706.8 1.0 select_convert_fusion
  707.8 1.2 fusion.43
  709.0 4.2 whole_rows.5
  (123 shorter events, 1.8 us)
Async XLA Ops:
  2.4 1.0 copy-start.5
  3.4 1.0 copy-start.9
  4.5 1.4 copy-start.14
  74.5 3.6 copy-start.1
  74.5 3.7 copy-start.21
  74.5 33.0 %copy-start.15 = (bf16[128,2048]{1,0:T(8,128)(2,1)}, bf16[128,2048]{1,0:T(8,128)(2,1)S(1)}, u32[]{:S(2)}) copy-start(bf16[128,2048]{1,0:T(8,128)(2,1)S(1)} %get-tuple-element.32) | copy-start | bytes 1572868
  80.9 13.9 %copy-start.23 = (f32[2048,128]{1,0:T(8,128)}, f32[2048,128]{1,0:T(8,128)S(1)}, u32[]{:S(2)}) copy-start(f32[2048,128]{1,0:T(8,128)S(1)} %copy.55) | copy-start | bytes 3145732
  82.8 27.0 %copy-start.25 = (f32[2048,128]{1,0:T(8,128)}, f32[2048,128]{1,0:T(8,128)S(1)}, u32[]{:S(2)}) copy-start(f32[2048,128]{1,0:T(8,128)S(1)} %copy.56) | copy-start | bytes 3145732
  101.2 3.6 copy-start.38
  101.2 6.3 copy-start.10
  107.5 2.4 copy-start.36
  107.5 2.4 copy-start.8
  109.9 65.0 %copy-start.6 = (bf16[128,2048]{1,0:T(8,128)(2,1)S(1)}, bf16[128,2048]{1,0:T(8,128)(2,1)}, u32[]{:S(2)}) copy-start(bf16[128,2048]{1,0:T(8,128)(2,1)} %x_ref.1) | copy-start | bytes 1572868
  109.9 65.2 %copy-start.7 = (bf16[128,16384]{1,0:T(8,128)(2,1)S(1)}, bf16[128,16384]{1,0:T(8,128)(2,1)}, u32[]{:S(2)}) copy-start(bf16[128,16384]{1,0:T(8,128)(2,1)} %refs_0_.3) | copy-start | bytes 12582916
  174.7 103.5 %copy-start.19 = (bf16[2048,512]{1,0:T(8,128)(2,1)}, bf16[2048,512]{1,0:T(8,128)(2,1)S(1)}, u32[]{:S(2)}) copy-start(bf16[2048,512]{1,0:T(8,128)(2,1)S(1)} %get-tuple-element.36) | copy-start | bytes 6291460
  259.1 3.2 copy-start.2
  259.1 14.2 %copy-start.17 = (bf16[2048,1024]{1,0:T(8,128)(2,1)}, bf16[2048,1024]{1,0:T(8,128)(2,1)S(1)}, u32[]{:S(2)}) copy-start(bf16[2048,1024]{1,0:T(8,128)(2,1)S(1)} %get-tuple-element.35) | copy-start | bytes 12582916
  283.2 45.7 %copy-start.27 = (bf16[128,2048]{1,0:T(8,128)(2,1)S(1)}, bf16[128,2048]{1,0:T(8,128)(2,1)}, u32[]{:S(2)}) copy-start(bf16[128,2048]{1,0:T(8,128)(2,1)} %param.15) | copy-start | bytes 1572868
  329.6 33.1 %copy-start.20 = (bf16[2048,512]{1,0:T(8,128)(2,1)S(1)}, bf16[2048,512]{1,0:T(8,128)(2,1)}, u32[]{:S(2)}) copy-start(bf16[2048,512]{1,0:T(8,128)(2,1)} %copy-done.19) | copy-start | bytes 6291460
  362.7 9.8 %copy-start.18 = (bf16[2048,1024]{1,0:T(8,128)(2,1)S(1)}, bf16[2048,1024]{1,0:T(8,128)(2,1)}, u32[]{:S(2)}) copy-start(bf16[2048,1024]{1,0:T(8,128)(2,1)} %copy-done.17) | copy-start | bytes 12582916
  388.7 99.1 %copy-start.28 = (bf16[128,2048]{1,0:T(8,128)(2,1)S(1)}, bf16[128,2048]{1,0:T(8,128)(2,1)}, u32[]{:S(2)}) copy-start(bf16[128,2048]{1,0:T(8,128)(2,1)} %param.15) | copy-start | bytes 1572868
  487.7 78.0 %copy-start.3 = (bf16[128,8192]{1,0:T(8,128)(2,1)}, bf16[128,8192]{1,0:T(8,128)(2,1)S(1)}, u32[]{:S(2)}) copy-start(bf16[128,8192]{1,0:T(8,128)(2,1)S(1)} %get-tuple-element.38.refs_2_.mine_ref) | copy-start | bytes 6291460
  489.5 77.1 %copy-start.11 = (bf16[128,2048]{1,0:T(8,128)(2,1)S(1)}, bf16[128,2048]{1,0:T(8,128)(2,1)}, u32[]{:S(2)}) copy-start(bf16[128,2048]{1,0:T(8,128)(2,1)} %refs_3_.1) | copy-start | bytes 1572868
  489.5 77.1 %copy-start.16 = (bf16[128,2048]{1,0:T(8,128)(2,1)S(1)}, bf16[128,2048]{1,0:T(8,128)(2,1)}, u32[]{:S(2)}) copy-start(bf16[128,2048]{1,0:T(8,128)(2,1)} %copy-done.15) | copy-start | bytes 1572868
  565.7 4.2 copy-start
  565.7 4.2 copy-start.12
  565.7 143.3 %collective-permute-start = (bf16[128,4096]{1,0:T(8,128)(2,1)}, bf16[128,4096]{1,0:T(8,128)(2,1)S(1)}, u32[]{:S(2)}, u32[]{:S(2)}) collective-permute-start(bf16[128,4096]{1,0:T(8,128)(2,1)} %get-tuple-element.46.mine_ref), channel_id=1, source_target_pairs={{0,16},{16,0},{1,17},{17,1},{2,18},{18,2},{3,19},{19,3},{4,20},{20... | collective-permute-start | bytes 3145736 | tf_op jit(solution)/shard_map/ppermute | solution.py:897
  566.6 3.3 copy-start.39
  566.6 3.3 copy-start.41
  573.2 2.2 copy-start.45
  573.2 2.4 copy-start.43
  573.2 2.4 copy-start.44
  573.3 3.0 copy-start.40
  573.3 3.0 copy-start.42
  581.7 7.7 %copy-start.24 = (f32[2048,128]{1,0:T(8,128)S(1)}, f32[2048,128]{1,0:T(8,128)}, u32[]{:S(2)}) copy-start(f32[2048,128]{1,0:T(8,128)} %copy-done.23) | copy-start | bytes 3145732
  581.8 7.7 %copy-start.26 = (f32[2048,128]{1,0:T(8,128)S(1)}, f32[2048,128]{1,0:T(8,128)}, u32[]{:S(2)}) copy-start(f32[2048,128]{1,0:T(8,128)} %copy-done.25) | copy-start | bytes 3145732
  589.4 2.0 copy-start.30
  589.4 2.0 copy-start.32
  589.4 2.0 copy-start.34
  589.4 2.0 copy-start.35
  601.4 3.5 copy-start.31
  601.4 3.5 copy-start.33
  601.4 4.5 copy-start.22
  604.9 7.5 %slice-start = ((s8[8388608]{0:T(1024)(128)(4,1)}), s8[4194304]{0:T(1024)(128)(4,1)S(1)}, s32[]{:S(2)}) async-start(s8[8388608]{0:T(1024)(128)(4,1)} %bitcast.87), calls=%async_computation | async-start | bytes 8388608
  605.9 6.2 copy-start.46
  605.9 6.5 slice-start.1
  605.9 6.5 copy-start.37
  613.8 85.3 %copy-start.4 = (bf16[128,8192]{1,0:T(8,128)(2,1)S(1)}, bf16[128,8192]{1,0:T(8,128)(2,1)}, u32[]{:S(2)}) copy-start(bf16[128,8192]{1,0:T(8,128)(2,1)} %copy-done.3) | copy-start | bytes 6291460
  613.8 85.3 %copy-start.13 = (bf16[128,8192]{1,0:T(8,128)(2,1)S(1)}, bf16[128,8192]{1,0:T(8,128)(2,1)}, u32[]{:S(2)}) copy-start(bf16[128,8192]{1,0:T(8,128)(2,1)} %copy-done.12) | copy-start | bytes 6291460
  704.0 3.8 copy-start.29

commit v5 on v4

--- a/solution.py
+++ b/solution.py
@@ -90,7 +90,7 @@
 
 
 class Load:
-    space = pl.ANY
+    space = pltpu.HBM
     parts = 1
 
     def __init__(self, source, far=0, near=0, early=False):
@@ -264,7 +264,7 @@
         return super().reached() | ({(0, ("x",))} if self.swap else set())
 
     def spaces(self):
-        return [pltpu.VMEM if self.fold else pl.ANY] * len(self.sources), [pl.ANY] * len(self.outs)
+        return [pltpu.VMEM if self.fold else pltpu.HBM] * len(self.sources), [pltpu.HBM] * len(self.outs)
 
     def scratch(self):
         return self.semaphores() + self.swap_scratch() + [
@@ -316,13 +316,14 @@
 
 
 class Product(Owners):
-    def __init__(self, left, right, parts=1, swap=False, **stages):
+    def __init__(self, left, right, parts=1, swap=False, columns=None, **stages):
         Load.__init__(self, left, **stages)
         self.sources = [left, right]
-        self.setup(left.shape[1], right.shape[1], jnp.bfloat16, parts, swap, False)
+        self.columns = columns or (0, right.shape[1])
+        self.setup(left.shape[1], self.columns[1], jnp.bfloat16, parts, swap, False)
 
     def scratch(self):
-        depth, width = self.sources[0].shape[0], self.sources[1].shape[1]
+        depth, width = self.sources[0].shape[0], self.columns[1]
         return super().scratch() + [
             pltpu.VMEM((2, depth, 2 * self.rows), jnp.bfloat16),
             pltpu.VMEM((depth, width), jnp.bfloat16),
@@ -354,7 +355,8 @@
         return pltpu.make_async_copy(left, self.more[3].at[k % 2], self.more[6].at[k % 2])
 
     def begin(self):
-        self.right = pltpu.make_async_copy(self.src[1], self.more[4], self.more[6].at[2])
+        right = self.src[1].at[:, pl.ds(*self.columns)]
+        self.right = pltpu.make_async_copy(right, self.more[4], self.more[6].at[2])
         self.right.start()
         self.fetch(0).start()
         self.fetch(1).start()
@@ -369,10 +371,10 @@
                 self.right.wait()
             self.fetch(k).wait()
             rows = at(self.first_row(step, names), 2 * self.rows)
-            wide = min(256, self.sources[1].shape[1])
+            width = self.columns[1]
             left = lefts[k % 2]
-            for column in range(0, self.sources[1].shape[1], wide):
-                columns = pl.ds(column, min(wide, self.sources[1].shape[1] - column))
+            for column in range(0, width, 256):
+                columns = pl.ds(column, min(256, width - column))
                 result[rows, columns] = lax.dot_general(
                     left, right[:, columns], (((0,), (0,)), ((), ())),
                     preferred_element_type=jnp.float32,
@@ -390,7 +392,7 @@
         self.outs = [jax.ShapeDtypeStruct(source.shape, source.dtype)] * 2
 
     def spaces(self):
-        return [pltpu.VMEM], [pl.ANY] * 2
+        return [pltpu.VMEM], [pltpu.HBM] * 2
 
     def moves(self):
         return [((1, ()), 0)]
@@ -467,43 +469,247 @@
                 load.leave()
 
 
+class Work:
+    operands = ()
+
+    def __init__(self, *sources):
+        self.sources = list(sources)
+
+    def bind(self, sources, targets, scratch):
+        self.src, self.dst, self.more = list(sources), list(targets), list(scratch)
+        self.copies = []
+
+    def begin(self):
+        pass
+
+    def keep(self, copy):
+        self.copies.append(copy)
+        copy.start()
+
+    def close(self):
+        for copy in self.copies:
+            copy.wait()
+
+
+class FeedForward(Work):
+    def __init__(self, gate_up_cols, total):
+        super().__init__(gate_up_cols)
+        width, both = gate_up_cols.shape
+        self.half, self.pair = both // 2, 2 * total // MEMBERS
+        self.in_spaces = [pltpu.HBM]
+        self.outs = [
+            jax.ShapeDtypeStruct((total, self.half), jnp.bfloat16),
+            jax.ShapeDtypeStruct((total, both), jnp.float32),
+            jax.ShapeDtypeStruct((total, width), jnp.bfloat16),
+        ]
+        self.out_spaces = [pltpu.HBM, pltpu.HBM, pltpu.HBM]
+        self.scratch = [
+            pltpu.VMEM((2, self.pair, both), jnp.float32),
+            pltpu.SemaphoreType.DMA((3, SIDES)),
+            pltpu.VMEM(gate_up_cols.shape, gate_up_cols.dtype),
+            pltpu.SemaphoreType.DMA(()),
+            pltpu.VMEM((total, self.half), jnp.bfloat16),
+        ]
+
+    def begin(self):
+        self.load = pltpu.make_async_copy(self.src[0], self.more[2], self.more[3])
+        self.load.start()
+
+    def tile(self, k, rows_ref):
+        (hidden_out, gate_up, rows_out), (staged, sems, cols, _, hidden) = self.dst, self.more
+        if k == 0:
+            self.load.wait()
+        rows = pl.ds(k * self.pair, self.pair)
+        self.keep(pltpu.make_async_copy(rows_ref, rows_out.at[rows], sems.at[0, k]))
+        if k >= 2:
+            self.last[k - 2].wait()
+        value = rows_ref[...]
+        for start in range(0, self.half, 256):
+            columns = pl.ds(start, 256)
+            others = pl.ds(self.half + start, 256)
+            gate = jnp.dot(value, cols[:, columns], preferred_element_type=jnp.float32)
+            up = jnp.dot(value, cols[:, others], preferred_element_type=jnp.float32)
+            staged[k % 2, :, columns] = gate
+            staged[k % 2, :, others] = up
+            hidden[rows, columns] = (gate * jax.nn.sigmoid(gate) * up).astype(jnp.bfloat16)
+        self.keep(pltpu.make_async_copy(hidden.at[rows], hidden_out.at[rows], sems.at[2, k]))
+        copy = pltpu.make_async_copy(staged.at[k % 2], gate_up.at[rows], sems.at[1, k])
+        copy.start()
+        if k == 0:
+            self.last = []
+        self.last.append(copy)
+
+    def close(self):
+        super().close()
+        for copy in self.last[-2:]:
+            copy.wait()
+
+
+class FeedBack(Work):
+    def __init__(self, down_cols, gate_up_cols, gate_up):
+        super().__init__(down_cols, gate_up_cols, gate_up)
+        total, both = gate_up.shape
+        width = down_cols.shape[0]
+        self.half, self.width, self.pair = both // 2, width, 2 * total // MEMBERS
+        self.in_spaces = [pltpu.HBM] * 3
+        self.outs = [
+            jax.ShapeDtypeStruct((total, both), jnp.bfloat16),
+            jax.ShapeDtypeStruct((total, width), jnp.bfloat16),
+            jax.ShapeDtypeStruct((total, width), jnp.bfloat16),
+        ]
+        self.out_spaces = [pltpu.HBM, pltpu.VMEM, pltpu.HBM]
+        self.scratch = [
+            pltpu.VMEM((2, self.pair, both), jnp.float32),
+            pltpu.SemaphoreType.DMA((3, SIDES)),
+            pltpu.VMEM(down_cols.shape, down_cols.dtype),
+            pltpu.VMEM(gate_up_cols.shape, gate_up_cols.dtype),
+            pltpu.SemaphoreType.DMA((2,)),
+            pltpu.VMEM((total, both), jnp.bfloat16),
+        ]
+
+    def fetch(self, k):
+        rows = pl.ds(k * self.pair, self.pair)
+        return pltpu.make_async_copy(
+            self.src[2].at[rows], self.more[0].at[k % 2], self.more[1].at[0, k]
+        )
+
+    def begin(self):
+        self.loads = [
+            pltpu.make_async_copy(self.src[i], self.more[2 + i], self.more[4].at[i])
+            for i in range(2)
+        ]
+        for copy in self.loads:
+            copy.start()
+        self.fetch(0).start()
+        self.fetch(1).start()
+
+    def tile(self, k, rows_ref):
+        (grads_out, part, rows_out), (saved, sems, down, cols, _, grads) = self.dst, self.more
+        if k == 0:
+            for copy in self.loads:
+                copy.wait()
+        rows = pl.ds(k * self.pair, self.pair)
+        self.keep(pltpu.make_async_copy(rows_ref, rows_out.at[rows], sems.at[1, k]))
+        self.fetch(k).wait()
+        value = rows_ref[...]
+        for start in range(0, self.half, 256):
+            columns = pl.ds(start, 256)
+            others = pl.ds(self.half + start, 256)
+            hidden_grad = jnp.dot(value, down[:, columns], preferred_element_type=jnp.float32)
+            gate_bf, up_bf = silu_grads(
+                hidden_grad, saved[k % 2, :, columns], saved[k % 2, :, others]
+            )
+            grads[rows, columns] = gate_bf
+            grads[rows, others] = up_bf
+        if k + 2 < SIDES:
+            self.fetch(k + 2).start()
+        self.keep(pltpu.make_async_copy(grads.at[rows], grads_out.at[rows], sems.at[2, k]))
+        both = grads[rows]
+        for start in range(0, self.width, 256):
+            columns = pl.ds(start, 256)
+            part[rows, columns] = contract_last(both, cols[columns, :]).astype(jnp.bfloat16)
+
+
+class BranchBack(Work):
+    def __init__(self, out_rows, attended):
+        super().__init__(out_rows, attended)
+        total, width = attended.shape[0], out_rows.shape[1]
+        self.width, self.pair = width, 2 * total // MEMBERS
+        self.in_spaces = [pltpu.VMEM, pltpu.VMEM]
+        self.outs = [
+            jax.ShapeDtypeStruct((total, HD), jnp.bfloat16),
+            jax.ShapeDtypeStruct((HD, width), jnp.bfloat16),
+        ]
+        self.out_spaces = [pltpu.VMEM, pltpu.VMEM]
+        self.scratch = [pltpu.VMEM((HD, width), jnp.float32)]
+
+    def tile(self, k, rows_ref):
+        (out_rows, attended), (grad, _), (total,) = self.src, self.dst, self.more
+        rows = pl.ds(k * self.pair, self.pair)
+        value = rows_ref[...]
+        grad[rows] = contract_last(value, out_rows[...]).astype(jnp.bfloat16)
+        for start in range(0, self.width, 512):
+            columns = pl.ds(start, 512)
+            term = contract_first(attended[rows], rows_ref[:, columns])
+            total[:, columns] = term if k == 0 else total[:, columns] + term
+
+    def close(self):
+        self.dst[1][...] = self.more[0][...].astype(jnp.bfloat16)
+
+
 GATHER_STAGES = (0, 1, 2, 3)
 NEAR = [("x",), ("zl",), ("y",), ("c",)]
 
 
-def call(body, name, ident, cargo, operand, space, out, out_space, scratch):
-    held = [out] * (out_space == pltpu.VMEM) + [operand] * (space == pltpu.VMEM)
+def room_for(*held):
+    sizes = [math.prod(s.shape) * jnp.dtype(s.dtype).itemsize for s in held]
+    return sum(sizes) + 8 * MIB
+
+
+def only_vmem(arrays, spaces):
+    return [a for a, space in zip(arrays, spaces) if space == pltpu.VMEM]
+
+
+def in_hbm(value, space):
+    return pltpu.with_memory_space_constraint(value, pltpu.HBM) if space == pltpu.HBM else value
+
+
+def call(body, name, ident, cargo, operands, spaces, outs, out_spaces, scratch):
+    cargo_in = [space for load in cargo.loads for space in load.spaces()[0]]
+    operands = [in_hbm(v, space) for v, space in zip(operands, spaces)]
+    sources = [in_hbm(v, space) for v, space in zip(cargo.sources, cargo_in)]
+    cargo_out = [space for load in cargo.loads for space in load.spaces()[1]]
+    kept = [
+        space(out.shape, out.dtype)
+        for out, space in zip(list(outs) + cargo.outs, list(out_spaces) + cargo_out)
+    ]
+    held = only_vmem(operands, spaces) + only_vmem(outs, out_spaces)
+    held += only_vmem(cargo.sources, cargo_in)
     held += [s for s in scratch + cargo.scratch if s.memory_space == pltpu.VMEM]
-    held += [s for load in cargo.loads if load.spaces()[0][0] == pltpu.VMEM for s in load.sources]
-    vmem = sum(math.prod(s.shape) * jnp.dtype(s.dtype).itemsize for s in held) + 6 * MIB
     return pl.pallas_call(
         functools.partial(body, cargo),
-        out_shape=[out] + cargo.outs,
-        in_specs=[pl.BlockSpec(memory_space=space)] + cargo.in_specs,
-        out_specs=[pl.BlockSpec(memory_space=out_space)] + cargo.out_specs,
+        out_shape=kept,
+        in_specs=[pl.BlockSpec(memory_space=s) for s in spaces] + cargo.in_specs,
+        out_specs=[pl.BlockSpec(memory_space=s) for s in out_spaces] + cargo.out_specs,
         scratch_shapes=scratch + cargo.scratch,
         compiler_params=pltpu.CompilerParams(
-            collective_id=ident, has_side_effects=True, vmem_limit_bytes=vmem
+            collective_id=ident, has_side_effects=True, vmem_limit_bytes=room_for(*held)
         ),
         cost_estimate=pl.CostEstimate(flops=0, bytes_accessed=100 * MIB, transcendentals=0),
         name=name,
-    )(operand, *cargo.sources)
-
-
-def gather_kernel(orders, cargo, x_ref, *refs):
-    n, m = len(cargo.sources), len(cargo.outs)
-    sources, o_ref, targets = refs[:n], refs[n], refs[n + 1 : n + 1 + m]
-    send_sem, recv_sem, core_send, core_recv, own_sem = refs[n + m + 1 : n + m + 6]
+    )(*operands, *sources)
+
+
+def take(refs, count):
+    taken = refs[:count]
+    del refs[:count]
+    return taken
+
+
+def gather_kernel(orders, work, eager, cargo, x_ref, *refs):
+    refs = list(refs)
+    work_in = take(refs, len(work.sources)) if work else []
+    sources = take(refs, len(cargo.sources))
+    work_out = take(refs, len(work.outs) if work else 1)
+    targets = take(refs, len(cargo.outs))
+    send_sem, recv_sem, core_send, core_recv, own_sem = take(refs, 5)
     here = place()
     spans = [pl.ds(r0, size) for _, r0, size in orders]
     orders = [o for o, _, _ in orders]
     pieces = range(len(orders))
-    cargo.bind(here, sources, targets, refs[n + m + 6 :])
+    if work:
+        (o_ref,) = take(refs, 1)
+        work.bind(work_in, work_out, take(refs, len(work.scratch)))
+        work.begin()
+    else:
+        o_ref = work_out[0]
+    rows, width = x_ref.shape
+    cargo.bind(here, sources, targets, refs)
     cargo.greet(here, NEAR)
-    own = pltpu.make_async_copy(x_ref, o_ref.at[0], own_sem)
+    own = pltpu.make_async_copy(x_ref, spots(o_ref, slice(0, 1), rows), own_sem)
 
     def spot(p, *names):
-        return o_ref.at[slot(*names), spans[p]]
+        return spots(o_ref, slot(*names), rows, spans[p])
 
     def source(p, mask):
         return spot(p, *subset(orders[p], mask)) if mask else x_ref.at[spans[p]]
@@ -524,7 +730,8 @@
         )
 
     sent = []
-    for mask in range(8):
+
+    def pass_on(mask):
         for p in pieces:
             if mask:
                 landing = spot(p, *subset(orders[p], mask))
@@ -539,26 +746,72 @@
             own.start()
         if mask in GATHER_STAGES:
             cargo.start(GATHER_STAGES.index(mask))
-    for mask in range(8):
-        for p in pieces:
-            landing = spot(p, "c", *subset(orders[p], mask))
-            pltpu.make_async_copy(landing, landing, core_recv.at[p, mask]).wait()
+
+    def from_core(*masks):
+        for mask in masks:
+            for p in pieces:
+                landing = spot(p, "c", *subset(orders[p], mask))
+                pltpu.make_async_copy(landing, landing, core_recv.at[p, mask]).wait()
+
+    def tiles(*numbers):
+        for k in numbers:
+            work.tile(k, o_ref.at[pl.ds(2 * rows * k, 2 * rows)])
+
+    if eager:
+        pass_on(0)
+        own.wait()
+        from_core(0)
+        tiles(0)
+        for mask in (1, 2, 3, 4):
+            pass_on(mask)
+        from_core(1, 2, 4)
+        tiles(1, 2)
+        pass_on(5)
+        tiles(3)
+        pass_on(6)
+        from_core(3, 5, 6)
+        tiles(4)
+        pass_on(7)
+        tiles(5, 6)
+        from_core(7)
+        tiles(7)
+    else:
+        for mask in range(8):
+            pass_on(mask)
+        from_core(*range(8))
+        own.wait()
+        if work:
+            tiles(*range(SIDES))
     for copy in sent:
         copy.wait_send()
-    own.wait()
+    if work:
+        work.close()
     cargo.finish()
 
 
-def gather_cube(block, ident, loads=(), orders=None):
+def spots(ref, index, rows, span=None):
+    if isinstance(index, slice):
+        return ref.at[pl.ds(index.start * rows, rows)]
+    if span is None:
+        return ref.at[pl.ds(index * rows, rows)]
+    return ref.at[pl.ds(index * rows + span.start, span.size)]
+
+
+def gather_cube(block, ident, loads=(), orders=None, work=None, eager=False):
     rows, width = block.shape
     orders = orders or thirds(rows)
-    out = call(
-        functools.partial(gather_kernel, orders),
-        "gather_cube", ident, Cargo(list(loads)), block, pl.ANY,
-        jax.ShapeDtypeStruct((MEMBERS, rows, width), block.dtype), pl.ANY,
-        [pltpu.SemaphoreType.DMA((len(orders), 8))] * 4 + [pltpu.SemaphoreType.DMA(())],
-    )
-    return [out[0].reshape(MEMBERS * rows, width)] + list(out[1:])
+    whole = jax.ShapeDtypeStruct((MEMBERS * rows, width), block.dtype)
+    scratch = [pltpu.SemaphoreType.DMA((len(orders), 8))] * 4 + [pltpu.SemaphoreType.DMA(())]
+    if work:
+        operands, spaces = [block] + work.sources, [pltpu.HBM] + work.in_spaces
+        outs, out_spaces = work.outs, work.out_spaces
+        scratch += [pltpu.VMEM(whole.shape, whole.dtype)] + work.scratch
+    else:
+        operands, spaces, outs, out_spaces = [block], [pltpu.HBM], [whole], [pltpu.HBM]
+    return call(
+        functools.partial(gather_kernel, orders, work, eager),
+        "gather_cube", ident, Cargo(list(loads)), operands, spaces, outs, out_spaces, scratch,
+    )
 
 
 def scatter_kernel(orders, cargo, p_ref, *refs):
@@ -635,8 +888,8 @@
     return call(
         functools.partial(scatter_kernel, orders),
         "scatter_cube", ident, Cargo(list(loads)),
-        partial.astype(jnp.bfloat16).reshape(MEMBERS, rows, width), pltpu.VMEM,
-        jax.ShapeDtypeStruct((rows, width), jnp.float32), pltpu.VMEM,
+        [partial.astype(jnp.bfloat16).reshape(MEMBERS, rows, width)], [pltpu.VMEM],
+        [jax.ShapeDtypeStruct((rows, width), jnp.float32)], [pltpu.VMEM],
         [pltpu.VMEM((8, rows, width), jnp.bfloat16)] * 3
         + [pltpu.SemaphoreType.DMA((len(orders), 8))] * 4,
     )
@@ -735,33 +988,46 @@
     return summed[0], summed[1]
 
 
-def finish_kernel(mine_ref, came_ref, o_ref):
+def finish_kernel(parts, *refs):
+    *halves_refs, o_ref = refs
     own = pl.program_id(1) == lax.axis_index("x")
-    o_ref[...] = jnp.where(own, mine_ref[...], came_ref[...]).astype(jnp.float32)
-
-
-def whole_rows(mine, came, parts):
-    rows, width = mine.shape
-    step = min(2048, width // parts)
-    steps = width // parts // step
-    half = pl.BlockSpec((rows, step), lambda p, x, k: (0, p * steps + k))
+    for part in range(parts):
+
+        @pl.when(pl.program_id(0) == part)
+        def _(mine_ref=halves_refs[2 * part], came_ref=halves_refs[2 * part + 1]):
+            o_ref[...] = jnp.where(own, mine_ref[...], came_ref[...]).astype(jnp.float32)
+
+
+def whole_rows(*pairs):
+    rows, width = pairs[0][0].shape
+    parts = len(pairs)
+    step = min(2048, width)
+    steps = width // step
+
+    def half(part):
+        return pl.BlockSpec(
+            (rows, step), lambda p, x, k, part=part: (0, jnp.where(p == part, k, 0))
+        )
+
     return pl.pallas_call(
-        finish_kernel,
+        functools.partial(finish_kernel, parts),
         grid=(parts, 2, steps),
-        out_shape=jax.ShapeDtypeStruct((rows, 2 * width), jnp.float32),
-        in_specs=[half, half],
+        out_shape=jax.ShapeDtypeStruct((rows, 2 * parts * width), jnp.float32),
+        in_specs=[half(part) for part in range(parts) for _ in range(2)],
         out_specs=pl.BlockSpec((rows, step), lambda p, x, k: (0, (2 * p + x) * steps + k)),
         compiler_params=pltpu.CompilerParams(vmem_limit_bytes=32 * MIB),
         cost_estimate=pl.CostEstimate(
-            flops=0, bytes_accessed=16 * rows * width, transcendentals=0
+            flops=0, bytes_accessed=12 * parts * rows * width, transcendentals=0
         ),
         name="whole_rows",
-    )(mine, came)
-
-
-def owners_product(left, right, parts=1, **options):
+    )(*[half for pair in pairs for half in pair])
+
+
+def owners_product(left, right, parts=1, columns=None, **options):
     if left.shape[1] // (lax.axis_size("zh") * SIDES) % 128 == 0:
-        return Product(left, right, parts, **options)
+        return Product(left, right, parts, columns=columns, **options)
+    if columns is not None:
+        right = right[:, columns[0] : sum(columns)]
     return Owners(contract_first(left, right).astype(jnp.bfloat16), parts, **options)
 
 
@@ -855,48 +1121,53 @@
     )
     x_most = halves(count_rows, "x", "y", "zl")
     x_last = halves(count_rows, "zl", "y", "x")
-    x_or_y = (
-        (("x", "y", "zl"), 0, count_rows // 2),
-        (("y", "x", "zl"), count_rows // 2, count_rows // 2),
-    )
-    y_last = halves(count_rows, "zl", "x", "y")
-    branch, down_cols = scatter_cube(
+    z_first = (
+        (("zl", "x", "y"), 0, count_rows // 2),
+        (("zl", "y", "x"), count_rows // 2, count_rows // 2),
+    )
+    branch, gate_up_cols = scatter_cube(
         jnp.dot(attended, out_rows, preferred_element_type=jnp.float32),
-        3, [Columns(w_down_t, near=1)], x_most,
+        3, [Columns(w_gate_up, 2, near=1)], x_most,
     )
     branch_norm, branch_inv = normalize(branch, gain_rows[2])
     middle = tokens.astype(jnp.float32) + branch_norm
-    middle_all, gate_up_cols = gather_cube(
-        middle.astype(jnp.bfloat16), 4, [Columns(w_gate_up, 2, near=3)], x_last
-    )
-    gate_up = jnp.dot(middle_all, gate_up_cols, preferred_element_type=jnp.float32)
-    gate_part, up_part = jnp.split(gate_up, 2, axis=1)
-    hidden_bf = (gate_part * jax.nn.sigmoid(gate_part) * up_part).astype(jnp.bfloat16)
+    hidden_bf, gate_up, middle_all, down_cols = gather_cube(
+        middle.astype(jnp.bfloat16), 4, [Columns(w_down_t, far=1, near=3)], x_last,
+        FeedForward(gate_up_cols, total), eager=True,
+    )
     (feed_out,) = scatter_cube(contract_last(hidden_bf, down_cols), 5)
     feed_norm, feed_inv = normalize(feed_out, gain_rows[3])
     mixed = (middle + feed_norm).astype(jnp.bfloat16)
 
     upstream = cotangent.astype(jnp.float32)
     feed_grad, gain_feed = norm_back(upstream, feed_out, feed_inv, gain_rows[3])
-    (feed_all,) = gather_cube(feed_grad.astype(jnp.bfloat16), 6)
-    hidden_grad = jnp.dot(feed_all, down_cols, preferred_element_type=jnp.float32)
-    gate_up_bf = jnp.concatenate(silu_grads(hidden_grad, gate_part, up_part), axis=1)
-    middle_part = contract_last(gate_up_bf, gate_up_cols)
-    middle_sum, gate_up_sum = scatter_cube(
-        middle_part, 7, [owners_product(middle_all, gate_up_bf, 2, near=1)], x_most
+    gate_up_bf, middle_part, feed_all = gather_cube(
+        feed_grad.astype(jnp.bfloat16), 6, work=FeedBack(down_cols, gate_up_cols, gate_up),
+        eager=True,
+    )
+    feed_width = hidden_bf.shape[1]
+    middle_sum, gate_sum, gate_other, up_sum = scatter_cube(
+        middle_part, 7,
+        [
+            owners_product(
+                middle_all, gate_up_bf, columns=(0, feed_width), near=1, swap=True, early=True
+            ),
+            owners_product(
+                middle_all, gate_up_bf, columns=(feed_width, feed_width), far=1, near=2
+            ),
+        ], x_most,
     )
     middle_grad = upstream + middle_sum
     branch_grad, gain_branch = norm_back(middle_grad, branch, branch_inv, gain_rows[2])
-    branch_all, down_sum, gate_up_other = gather_cube(
+    attended_grad, out_grad, down_sum, up_other = gather_cube(
         branch_grad.astype(jnp.bfloat16), 8,
         [
             owners_product(feed_all, hidden_bf, far=1, near=3),
-            Whole(gate_up_sum, "x", near=1),
-        ], y_last,
-    )
+            Whole(up_sum, "x", near=3),
+        ], z_first, BranchBack(out_rows, attended),
+    )
+    attended_grad = blocks(attended_grad)
     down_other = lax.ppermute(down_sum, "x", [(0, 1), (1, 0)])
-    out_grad = contract_first(attended, branch_all)
-    attended_grad = blocks(contract_last(branch_all, out_rows).astype(jnp.bfloat16))
     prob_grad = jnp.einsum(
         "bqd,bkd->bqk", attended_grad, value_bf, preferred_element_type=jnp.float32
     )
@@ -948,7 +1219,7 @@
         Owners(gain_terms, swap=True, fold=True, early=True),
     ]
     if direct:
-        loads.append(Pair(out_grad.astype(jnp.bfloat16), early=True))
+        loads.append(Pair(out_grad, early=True))
     tokens_sum, qkv_sum, qkv_other, gain_sum, gain_other, *out_both = scatter_cube(
         contract_last(projected_bf, qkv_cols), 10, loads, x_most
     )
@@ -956,10 +1227,16 @@
     if direct:
         grad_out = jnp.where(same, out_both[0], out_both[1]).astype(jnp.float32)
     else:
-        grad_out = summed_head_rows(out_grad, owned)
-    grad_qkv = whole_rows(qkv_sum, qkv_other, 3)
-    grad_gate_up = whole_rows(gate_up_sum, gate_up_other, 2)
-    grad_down_t = whole_rows(down_sum, down_other, 1)
+        grad_out = summed_head_rows(out_grad.astype(jnp.float32), owned)
+    third = width // 2
+    grad_qkv = whole_rows(
+        *[
+            (qkv_sum[:, k * third : (k + 1) * third], qkv_other[:, k * third : (k + 1) * third])
+            for k in range(3)
+        ]
+    )
+    grad_gate_up = whole_rows((gate_sum, gate_other), (up_sum, up_other))
+    grad_down_t = whole_rows((down_sum, down_other))
     grad_gains = (gain_sum + gain_other)[:4, :owned].T
     return (mixed, grad_tokens, grad_qkv, grad_out, grad_gate_up, grad_down_t, grad_gains)
 

time: 720 us -> 681 us (0.946)
  matrix products: 69.7 us -> 30.7 us
    dot_general x3 -> x0, matrix products: 22 us -> none  [the longest x1 11 us: shards(): jnp.dot(middle_all, gate_up_cols, preferred_element_type=jnp.float32)]
    dot_general x4 -> x2, matrix products: 27.9 us -> 11.8 us  [contract_last(): lax.dot_general(operand, matrix, (((1,), (1,)), ((), ())), preferred_elem...]
  transfers between devices with their start and end apart: 1 -> 1, of which waited for: 0 -> 0; matrix products, arithmetic and copies ran while one was open for 6% -> 6% of each run, Pallas kernels for 14% -> 15%
where the time goes in v5:
time: 681 us; the launch traced here: 675 us
  Pallas kernels  591 us (87%)
  other arithmetic  34.3 us (5%)
  matrix products  30.7 us (5%)
  local copies, waits for them, and re-layouts  16.1 us (2%)
    pallas_call x8, Pallas kernels, call(): pl.pallas_call(functools.partial(body, cargo), out_shape=kept, in_specs=[...  562 us
    pallas_call x2, Pallas kernels, sum_cube(): pl.pallas_call(exchange_kernel, out_shape=jax.ShapeDtypeStruct(shape, jnp...  18.5 us
  transfers between devices with their start and end apart: 1, of which 0 were waited for; matrix products, arithmetic and copies ran while one was open for 6% of the time, Pallas kernels for 15%

profile of v5, /device:TPU:0, one launch (start us, length us, event | category | flops | bytes accessed | tf_op | source)
XLA Modules:
  0.0 674.8 jit_solution(11155900711946225471)
XLA Ops:
  0.7 0.7 fusion.43
  1.4 0.2 reduce-window.8
  1.7 0.7 pad_convert_fusion.refs_0_
  2.4 68.9 %gather_cube.4 = (bf16[2048,2048]{1,0:T(8,128)(2,1)}, f32[16,8,128]{2,1,0:T(8,128)S(1)}, f32[16,8,128]{2,1,0:T(8,128)S(1)}, bf16[2048,384]{1,0:T(8,128)(2,1)}, bf16[128,2048]{1,0:T(8,128)(2,1)}) custom-call(bf16[128,2048]{1,0:T(8,128)(2,1)} %x_ref.1, f32[8,128]{1,0:T(8,128)S(1)} %pad_convert_fusion.refs_0_, f32[8,128]{1,0:T(8,128)S(1)} %broadcast_in_dim.12.refs_1_, ...), custom_call_target="tpu_custom_call" | custom-call | bytes 104857600 | tf_op jit(solution)/shard_map/gather_cube/pallas_call | solution.py:669
  71.4 6.4 fusion.57
  77.9 0.9 slice.162
  78.8 0.3 copy.42
  79.1 0.3 multiply_reduce_fusion.10
  79.5 0.3 copy.43
  79.8 0.3 multiply_reduce_fusion.9
  80.2 0.6 pad_maximum_fusion.13.v_ref
  80.8 9.2 %sum_cube.2 = f32[32,128]{1,0:T(8,128)} custom-call(f32[32,128]{1,0:T(8,128)} %pad_maximum_fusion.13.v_ref), custom_call_target="tpu_custom_call" | custom-call | bytes 20971520 | tf_op jit(solution)/shard_map/sum_cube/pallas_call | solution.py:927
  90.0 0.7 rsqrt_bitcast_fusion.1
  90.8 2.0 copy.41
  92.9 0.3 multiply_multiply_fusion
  93.2 0.3 multiply_multiply_fusion.1
  93.6 5.2 fusion.31
  98.9 1.9 fusion.56
  100.8 1.2 convolution_convert_fusion.4
  102.0 1.1 broadcast_select_fusion.refs_0_
  103.1 2.3 convolution_convert_fusion.2
  105.5 90.5 %scatter_cube.4 = (f32[128,2048]{1,0:T(8,128)S(1)}, bf16[2048,1024]{1,0:T(8,128)(2,1)}) custom-call(bf16[16,128,2048]{2,1,0:T(8,128)(2,1)S(1)} %bitcast.68, bf16[128,16384]{1,0:T(8,128)(2,1)} %refs_0_.1), custom_call_target="tpu_custom_call" | custom-call | bytes 104857600 | tf_op jit(solution)/shard_map/scatter_cube/pallas_call | solution.py:669
  195.9 0.2 multiply_reduce_fusion.8
  196.1 1.0 fusion.39.x_ref
  197.2 69.2 %gather_cube.5 = (bf16[2048,512]{1,0:T(8,128)(2,1)}, f32[2048,1024]{1,0:T(8,128)}, bf16[2048,2048]{1,0:T(8,128)(2,1)}, bf16[2048,512]{1,0:T(8,128)(2,1)}) custom-call(bf16[128,2048]{1,0:T(8,128)(2,1)} %fusion.39.x_ref, bf16[2048,1024]{1,0:T(8,128)(2,1)} %get-tuple-element.42.refs_0_.refs_1_, bf16[128,8192]{1,0:T(8,128)(2,1)} %refs_1_.1), custom_call_target="tpu_custom_call" | custom-call | bytes 104857600 | tf_op jit(solution)/shard_map/gather_cube/pallas_call | solution.py:669
  266.4 6.8 %convolution_convert_fusion.1 = bf16[2048,2048]{1,0:T(8,128)(2,1)S(1)} fusion(bf16[2048,512]{1,0:T(8,128)(2,1)} %get-tuple-element.43.refs_3_, bf16[2048,512]{1,0:T(8,128)(2,1)} %get-tuple-element.44.refs_0_), kind=kOutput, calls=%fused_computation.2 | convolution fusion | flops 4299161600 | bytes 12582912 | tf_op jit(solution)/shard_map/dot_general | solution.py:973
  273.1 33.9 %scatter_cube.5 = f32[128,2048]{1,0:T(8,128)S(1)} custom-call(bf16[16,128,2048]{2,1,0:T(8,128)(2,1)S(1)} %bitcast.69), custom_call_target="tpu_custom_call" | custom-call | bytes 104857600 | tf_op jit(solution)/shard_map/scatter_cube/pallas_call | solution.py:669
  307.3 0.4 fusion.38
  307.7 1.1 fusion.25.x_ref
  308.7 43.1 %gather_cube.6 = (bf16[2048,1024]{1,0:T(8,128)(2,1)}, bf16[2048,2048]{1,0:T(8,128)(2,1)S(1)}, bf16[2048,2048]{1,0:T(8,128)(2,1)}) custom-call(bf16[128,2048]{1,0:T(8,128)(2,1)} %fusion.25.x_ref, bf16[2048,512]{1,0:T(8,128)(2,1)} %get-tuple-element.44.refs_0_, bf16[2048,1024]{1,0:T(8,128)(2,1)} %get-tuple-element.42.refs_0_.refs_1_, ...), custom_call_target="tpu_custom_call" | custom-call | bytes 104857600 | tf_op jit(solution)/shard_map/gather_cube/pallas_call | solution.py:669
  351.9 3.4 copy-done
  355.2 102.8 %scatter_cube.6 = (f32[128,2048]{1,0:T(8,128)S(1)}, bf16[128,4096]{1,0:T(8,128)(2,1)}, bf16[128,4096]{1,0:T(8,128)(2,1)}, bf16[128,4096]{1,0:T(8,128)(2,1)}) custom-call(bf16[16,128,2048]{2,1,0:T(8,128)(2,1)} %bitcast.71, bf16[2048,2048]{1,0:T(8,128)(2,1)} %get-tuple-element.47.refs_0_.refs_2_, bf16[2048,1024]{1,0:T(8,128)(2,1)} %get-tuple-element.48.refs_1_.refs_3_, ...), custom_call_target="tpu_custom_call" | custom-call | bytes 104857600 | tf_op jit(solution)/shard_map/scatter_cube/pallas_call | solution.py:669
  458.0 0.4 multiply_reduce_fusion
  458.4 1.5 multiply_convert_fusion.3
  459.9 68.0 %gather_cube.7 = (bf16[2048,128]{1,0:T(8,128)(2,1)S(1)}, bf16[128,2048]{1,0:T(8,128)(2,1)S(1)}, bf16[128,4096]{1,0:T(8,128)(2,1)}, bf16[128,4096]{1,0:T(8,128)(2,1)}) custom-call(bf16[128,2048]{1,0:T(8,128)(2,1)} %get-tuple-element.79.x_ref, bf16[128,2048]{1,0:T(8,128)(2,1)S(1)} %broadcast_select_fusion.refs_0_, bf16[2048,128]{1,0:T(8,128)(2,1)S(1)} %bitcast.73, ...), custom_call_target="tpu_custom_call" | custom-call | bytes 104857600 | tf_op jit(solution)/shard_map/gather_cube/pallas_call | solution.py:669
  527.9 0.5 collective-permute-start
  528.4 0.5 multiply_reduce_fusion.5
  528.9 0.2 multiply_convert_fusion.2
  529.2 0.3 copy-done.21
  529.5 0.2 copy-done.23
  529.6 1.6 convolution_multiply_fusion
  531.2 1.6 convolution_multiply_fusion.1
  532.8 3.4 convolution_convert_fusion.3
  536.2 2.5 copy.36
  538.7 2.5 copy.34
  541.3 7.6 %fusion.26 = (f32[2048,64]{1,0:T(8,128)S(1)}, f32[2048,64]{1,0:T(8,128)S(1)}, f32[2048,64]{1,0:T(8,128)S(1)}, f32[2048,64]{1,0:T(8,128)S(1)}) fusion(f32[2048,128]{1,0:T(8,128)} %bitcast.77, f32[64]{0:T(128)S(1)} %multiply_power_fusion, f32[2048]{0:T(1024)S(1)} %bitcast_subtract_fusion, f32[2048,128]{1,0:T(8,128)} %bitcast.76), kind=kLoop, calls=%fused_computation.40 | loop fusion | flops 1835008 | bytes 4202752 | tf_op jit(solution)/shard_map/sub | solution.py:954
  549.0 1.8 multiply_reduce_fusion.1
  550.9 0.6 pad_maximum_fusion.14.v_ref
  551.5 9.3 %sum_cube.3 = f32[32,128]{1,0:T(8,128)} custom-call(f32[32,128]{1,0:T(8,128)} %pad_maximum_fusion.14.v_ref), custom_call_target="tpu_custom_call" | custom-call | bytes 20971520 | tf_op jit(solution)/shard_map/sum_cube/pallas_call | solution.py:927
  560.9 0.9 multiply_bitcast_fusion.1
  561.7 2.4 multiply_convert_fusion.1
  564.2 1.0 multiply_convert_fusion
  565.2 1.3 pad_maximum_fusion.refs_1_
  566.6 5.1 convolution_convert_fusion
  571.7 86.0 %scatter_cube.7 = (f32[128,2048]{1,0:T(8,128)S(1)}, bf16[128,3072]{1,0:T(8,128)(2,1)}, bf16[128,3072]{1,0:T(8,128)(2,1)}, f32[8,128]{1,0:T(8,128)}, f32[8,128]{1...) custom-call(bf16[16,128,2048]{2,1,0:T(8,128)(2,1)S(1)} %bitcast.70, ...), custom_call_target="tpu_custom_call" | custom-call | bytes 104857600 | tf_op jit(solution)/shard_map/scatter_cube/pallas_call | solution.py:669
  657.8 1.3 fusion.53
  659.1 1.2 fusion.54
  660.3 0.7 add.94
  661.0 0.6 slice_bitcast_fusion.2
  661.6 5.1 whole_rows.4
  666.7 2.7 whole_rows.3
  669.4 1.0 select_convert_fusion
  670.5 1.2 fusion.42
  671.7 2.7 whole_rows.5
  (92 shorter events, 1.0 us)
Async XLA Ops:
  79.1 14.1 %copy-start.9 = (f32[2048,128]{1,0:T(8,128)}, f32[2048,128]{1,0:T(8,128)S(1)}, u32[]{:S(2)}) copy-start(f32[2048,128]{1,0:T(8,128)S(1)} %copy.42) | copy-start | bytes 3145732
  79.8 13.8 %copy-start.6 = (f32[2048,128]{1,0:T(8,128)}, f32[2048,128]{1,0:T(8,128)S(1)}, u32[]{:S(2)}) copy-start(f32[2048,128]{1,0:T(8,128)S(1)} %copy.43) | copy-start | bytes 3145732
  98.8 3.2 copy-start.20
  98.8 3.2 copy-start.22
  98.8 3.2 copy-start.24
  98.9 3.2 copy-start.26
  98.9 1.9 copy-start.31
  105.5 90.7 %copy-start.19 = (bf16[128,2048]{1,0:T(8,128)(2,1)S(1)}, bf16[128,2048]{1,0:T(8,128)(2,1)}, u32[]{:S(2)}) copy-start(bf16[128,2048]{1,0:T(8,128)(2,1)} %x_ref.1) | copy-start | bytes 1572868
  273.1 34.1 %copy-start.11 = (bf16[128,2048]{1,0:T(8,128)(2,1)S(1)}, bf16[128,2048]{1,0:T(8,128)(2,1)}, u32[]{:S(2)}) copy-start(bf16[128,2048]{1,0:T(8,128)(2,1)} %param.15) | copy-start | bytes 1572868
  351.8 3.4 copy-start
  459.9 68.5 %copy-start.28 = (f32[16,128,128]{1,2,0:T(8,128)S(1)}, f32[16,128,128]{1,2,0:T(8,128)}, u32[]{:S(2)}) copy-start(f32[16,128,128]{1,2,0:T(8,128)} %get-tuple-element.106) | copy-start | bytes 3145732
  459.9 68.5 %copy-start.32 = (bf16[2048,128]{1,0:T(8,128)(2,1)S(1)}, bf16[2048,128]{1,0:T(8,128)(2,1)}, u32[]{:S(2)}) copy-start(bf16[2048,128]{1,0:T(8,128)(2,1)} %copy.41) | copy-start | bytes 1572868
  527.9 143.8 %collective-permute-start = (bf16[128,4096]{1,0:T(8,128)(2,1)}, bf16[128,4096]{1,0:T(8,128)(2,1)S(1)}, u32[]{:S(2)}, u32[]{:S(2)}) collective-permute-start(bf16[128,4096]{1,0:T(8,128)(2,1)} %get-tuple-element.62.refs_0_), channel_id=1, source_target_pairs={{0,16},{16,0},{1,17},{17,1},{2,18},{18,2},{3,19},{19,3},{4,20},{20... | collective-permute-start | bytes 3145736 | tf_op jit(solution)/shard_map/ppermute | solution.py:1170
  528.4 1.0 copy-start.21
  528.4 1.2 copy-start.23
  528.9 2.3 copy-start.25
  528.9 2.3 copy-start.27
  541.3 7.7 %copy-start.7 = (f32[2048,128]{1,0:T(8,128)S(1)}, f32[2048,128]{1,0:T(8,128)}, u32[]{:S(2)}) copy-start(f32[2048,128]{1,0:T(8,128)} %copy-done.6) | copy-start | bytes 3145732
  541.3 7.7 %copy-start.10 = (f32[2048,128]{1,0:T(8,128)S(1)}, f32[2048,128]{1,0:T(8,128)}, u32[]{:S(2)}) copy-start(f32[2048,128]{1,0:T(8,128)} %copy-done.9) | copy-start | bytes 3145732
  548.9 1.9 copy-start.13
  548.9 1.9 copy-start.15
  548.9 1.9 copy-start.17
  548.9 2.0 copy-start.18
  560.8 3.3 copy-start.8
  560.8 3.3 copy-start.14
  560.8 3.3 copy-start.16
  561.7 3.5 copy-start.33
  564.2 2.4 copy-start.35
  571.7 89.9 %copy-start.4 = (bf16[128,4096]{1,0:T(8,128)(2,1)S(1)}, bf16[128,4096]{1,0:T(8,128)(2,1)}, u32[]{:S(2)}) copy-start(bf16[128,4096]{1,0:T(8,128)(2,1)} %get-tuple-element.61.refs_3_) | copy-start | bytes 3145732
  657.8 2.5 copy-start.34
  657.8 3.8 copy-start.1
  657.8 3.8 copy-start.2
  657.8 3.8 copy-start.3
  666.7 2.7 copy-start.29
  666.7 2.7 copy-start.30
  666.7 3.8 copy-start.12
  669.4 2.2 copy-start.5

commit v6 on v5

--- a/solution.py
+++ b/solution.py
@@ -386,39 +386,108 @@
                     copy.start()
 
 
-class Pair(Load, Swap):
-    def __init__(self, source, **stages):
-        super().__init__(source, **stages)
-        self.outs = [jax.ShapeDtypeStruct(source.shape, source.dtype)] * 2
-
-    def spaces(self):
-        return [pltpu.VMEM], [pltpu.HBM] * 2
+class HeadRows(Load):
+    def __init__(self, source):
+        super().__init__(source)
+        self.outs = [jax.ShapeDtypeStruct(source.shape, source.dtype)]
 
     def moves(self):
-        return [((1, ()), 0)]
-
-    def reached(self):
-        return {(1, ()), (0, ("x",))}
+        return [((1, ()), 0), ((1, ("x",)), 0)]
+
+    def bind(self, here, sources, targets, scratch):
+        (source,), (target,), (send, recv) = sources, targets, scratch
+        half = source.shape[0] // 2
+        self.home = here["x"] == here["zh"]
+        mine = jnp.where(self.home, 0, 1)
+        rows = at(mine * half, half)
+        self.copy = pltpu.make_async_remote_copy(
+            src_ref=source.at[rows], dst_ref=target.at[rows],
+            send_sem=send.at[0], recv_sem=recv.at[mine],
+            device_id={"x": here["zh"], "zh": 1 - here["zh"]}, device_id_type=MESH,
+        )
+        spots_here = [target.at[pl.ds(k * half, half)] for k in range(2)]
+        self.landed = [
+            pltpu.make_async_copy(spot, spot, recv.at[k]) for k, spot in enumerate(spots_here)
+        ]
+
+    def start(self, stage):
+        if stage == 0:
+            self.copy.start()
+
+    def land(self):
+        @pl.when(jnp.logical_not(self.home))
+        def _():
+            for landed in self.landed:
+                landed.wait()
+
+    def leave(self):
+        self.copy.wait_send()
+
+
+class FinalRows(Load):
+    def __init__(self, *pairs, near=4):
+        super().__init__(None, near=near)
+        self.sources = [half for pair in pairs for half in pair]
+        rows, self.width = pairs[0][0].shape
+        self.step = min(2048, self.width)
+        self.outs = [jax.ShapeDtypeStruct((rows, len(self.sources) * self.width), jnp.float32)]
+
+    def moves(self):
+        return []
 
     def scratch(self):
-        shape = self.outs[0].shape
-        return self.semaphores() + self.swap_scratch() + [
-            pltpu.VMEM(shape, jnp.bfloat16), pltpu.VMEM(shape, jnp.bfloat16)
-        ]
-
-    def views(self, here, step, names, part):
-        return self.src[0], self.more[1], self.more[1]
-
-    def finish(self):
-        sems, came, total = self.more
-        total[...] = (
-            self.src[0][...].astype(jnp.float32) + came[...].astype(jnp.float32)
-        ).astype(jnp.bfloat16)
-        self.give(total, sems)
+        rows = self.outs[0].shape[0]
+        return [
+            pltpu.VMEM((2, rows, self.step), jnp.bfloat16),
+            pltpu.VMEM((2, rows, self.step), jnp.float32),
+            pltpu.SemaphoreType.DMA((4,)),
+        ]
+
+    def bind(self, here, sources, targets, scratch):
+        self.here, self.src, self.dst = here, sources, targets
+        self.halves, self.wholes, self.sems = scratch
+
+    def start(self, stage):
+        if stage != self.stages[0]:
+            return
+        x = self.here["x"]
+        steps = [
+            (k, start) for k in range(len(self.sources)) for start in range(0, self.width, self.step)
+        ]
+
+        def fetch(n):
+            k, start = steps[n]
+            return pltpu.make_async_copy(
+                self.src[k].at[:, pl.ds(start, self.step)], self.halves.at[n % 2],
+                self.sems.at[n % 2],
+            )
+
+        def store(n):
+            k, start = steps[n]
+            half = x if k % 2 == 0 else 1 - x
+            first = (2 * (k // 2) + half) * self.width + start
+            return pltpu.make_async_copy(
+                self.wholes.at[n % 2], self.dst[0].at[:, at(first, self.step)],
+                self.sems.at[2 + n % 2],
+            )
+
+        fetch(0).start()
+        for n in range(len(steps)):
+            if n + 1 < len(steps):
+                fetch(n + 1).start()
+            fetch(n).wait()
+            if n >= 2:
+                store(n - 2).wait()
+            self.wholes[n % 2] = self.halves[n % 2].astype(jnp.float32)
+            store(n).start()
+        for n in range(max(0, len(steps) - 2), len(steps)):
+            store(n).wait()
+
+    def land(self):
+        pass
 
     def leave(self):
-        super().leave()
-        self.given_wait()
+        pass
 
 
 class Cargo:
@@ -557,14 +626,15 @@
             jax.ShapeDtypeStruct((total, width), jnp.bfloat16),
             jax.ShapeDtypeStruct((total, width), jnp.bfloat16),
         ]
-        self.out_spaces = [pltpu.HBM, pltpu.VMEM, pltpu.HBM]
+        self.out_spaces = [pltpu.HBM, pltpu.HBM, pltpu.HBM]
         self.scratch = [
             pltpu.VMEM((2, self.pair, both), jnp.float32),
-            pltpu.SemaphoreType.DMA((3, SIDES)),
+            pltpu.SemaphoreType.DMA((4, SIDES)),
             pltpu.VMEM(down_cols.shape, down_cols.dtype),
             pltpu.VMEM(gate_up_cols.shape, gate_up_cols.dtype),
             pltpu.SemaphoreType.DMA((2,)),
             pltpu.VMEM((total, both), jnp.bfloat16),
+            pltpu.VMEM((total, width), jnp.bfloat16),
         ]
 
     def fetch(self, k):
@@ -584,7 +654,8 @@
         self.fetch(1).start()
 
     def tile(self, k, rows_ref):
-        (grads_out, part, rows_out), (saved, sems, down, cols, _, grads) = self.dst, self.more
+        grads_out, part_out, rows_out = self.dst
+        saved, sems, down, cols, _, grads, part = self.more
         if k == 0:
             for copy in self.loads:
                 copy.wait()
@@ -608,6 +679,7 @@
         for start in range(0, self.width, 256):
             columns = pl.ds(start, 256)
             part[rows, columns] = contract_last(both, cols[columns, :]).astype(jnp.bfloat16)
+        self.keep(pltpu.make_async_copy(part.at[rows], part_out.at[rows], sems.at[3, k]))
 
 
 class BranchBack(Work):
@@ -814,32 +886,101 @@
     )
 
 
-def scatter_kernel(orders, cargo, p_ref, *refs):
-    n, m = len(cargo.sources), len(cargo.outs)
-    sources, o_ref, targets = refs[:n], refs[n], refs[n + 1 : n + 1 + m]
-    acc, rcore, came, core_send, core_recv, send_sem, recv_sem = refs[n + m + 1 : n + m + 8]
+class Partial:
+    def __init__(self, left, right, last=True):
+        self.sources = [left, right]
+        self.last = last
+        self.pair = 2 * left.shape[0] // MEMBERS
+        self.width = right.shape[0 if last else 1]
+        self.scratch = [
+            pltpu.VMEM(left.shape, left.dtype),
+            pltpu.VMEM(right.shape, right.dtype),
+            pltpu.SemaphoreType.DMA((2,)),
+            pltpu.VMEM((left.shape[0], self.width), jnp.bfloat16),
+        ]
+
+    def begin(self, sources, scratch):
+        self.left, self.right, sems, self.made = scratch
+        self.loads = [
+            pltpu.make_async_copy(source, held, sems.at[k])
+            for k, (source, held) in enumerate(zip(sources, (self.left, self.right)))
+        ]
+        for copy in self.loads:
+            copy.start()
+
+    def wait(self):
+        for copy in self.loads:
+            copy.wait()
+
+    def tile(self, k):
+        rows = pl.ds(k * self.pair, self.pair)
+        for start in range(0, self.width, 512):
+            columns = pl.ds(start, 512)
+            if self.last:
+                value = contract_last(self.left[rows], self.right[columns, :])
+            else:
+                value = jnp.dot(
+                    self.left[rows], self.right[:, columns], preferred_element_type=jnp.float32
+                )
+            self.made[rows, columns] = value.astype(jnp.bfloat16)
+
+
+def scatter_kernel(orders, maker, cargo, *refs):
+    refs = list(refs)
+    heads = take(refs, len(maker.sources) if maker else 1)
+    sources = take(refs, len(cargo.sources))
+    (o_ref,) = take(refs, 1)
+    targets = take(refs, len(cargo.outs))
+    acc, rcore, came, core_send, core_recv, send_sem, recv_sem = take(refs, 7)
     here = place()
+    rows = o_ref.shape[0]
     spans = [pl.ds(r0, size) for _, r0, size in orders]
     orders = [o for o, _, _ in orders]
     pieces = range(len(orders))
-    cargo.bind(here, sources, targets, refs[n + m + 8 :])
+    if maker:
+        maker.begin(heads, take(refs, len(maker.scratch)))
+        p_ref = maker.made
+    else:
+        p_ref = heads[0]
+        (load_sem,) = take(refs, 1)
+    cargo.bind(here, sources, targets, refs)
     cargo.greet(here, NEAR)
 
     def away(p, mask):
         return pltpu.make_async_remote_copy(
-            src_ref=p_ref.at[slot("c", *subset(orders[p], mask)), spans[p]],
+            src_ref=spots(p_ref, slot("c", *subset(orders[p], mask)), rows, spans[p]),
             dst_ref=rcore.at[mask, spans[p]],
             send_sem=core_send.at[p, mask], recv_sem=core_recv.at[p, mask],
             device_id=flip(here, "c"), device_id_type=MESH,
         )
 
+    def mine(p, mask):
+        return spots(p_ref, slot(*subset(orders[p], mask)), rows, spans[p])
+
+    def fetch(p, mask):
+        return pltpu.make_async_copy(mine(p, mask), acc.at[mask, spans[p]], load_sem.at[p, mask])
+
+    sent = []
+
+    def hand_over(*masks):
+        for mask in masks:
+            for p in pieces:
+                sent.append(away(p, mask))
+                sent[-1].start()
+                if not maker:
+                    fetch(p, mask).start()
+
     sequence = [7, 3, 5, 1, 6, 2, 4, 0]
-    sent = []
-    for mask in sequence:
-        for p in pieces:
-            sent.append(away(p, mask))
-            sent[-1].start()
-    cargo.start(0)
+    if maker:
+        cargo.start(0)
+        maker.wait()
+        for pairs, masks in (((7,), (7,)), ((4, 5, 6), (3, 5, 6)), ((1, 2, 3), (1, 2, 4)), ((0,), (0,))):
+            for k in pairs:
+                maker.tile(k)
+            hand_over(*masks)
+    else:
+        hand_over(*sequence)
+        cargo.start(0)
 
     def over(p, mask):
         k = (mask & -mask).bit_length() - 1
@@ -852,8 +993,11 @@
     for mask in sequence:
         for p in pieces:
             away(p, mask).wait_recv()
-            own = slot(*subset(orders[p], mask))
-            acc[mask, spans[p]] = p_ref[own, spans[p]] + rcore[mask, spans[p]]
+            if maker:
+                acc[mask, spans[p]] = mine(p, mask)[...] + rcore[mask, spans[p]]
+            else:
+                fetch(p, mask).wait()
+                acc[mask, spans[p]] = acc[mask, spans[p]] + rcore[mask, spans[p]]
             if mask & 1:
                 sent.append(over(p, mask))
                 sent[-1].start()
@@ -876,22 +1020,25 @@
             cargo.start(2 + k)
         if k == 1:
             cargo.finish(early=True)
+            cargo.start(4)
     for copy in sent:
         copy.wait_send()
     cargo.finish()
 
 
 def scatter_cube(partial, ident, loads=(), orders=None):
-    total, width = partial.shape
+    maker = partial if isinstance(partial, Partial) else None
+    total, width = (maker.sources[0].shape[0], maker.width) if maker else partial.shape
     rows = total // MEMBERS
     orders = orders or thirds(rows)
+    operands = maker.sources if maker else [partial]
+    semaphores = pltpu.SemaphoreType.DMA((len(orders), 8))
     return call(
-        functools.partial(scatter_kernel, orders),
-        "scatter_cube", ident, Cargo(list(loads)),
-        [partial.astype(jnp.bfloat16).reshape(MEMBERS, rows, width)], [pltpu.VMEM],
+        functools.partial(scatter_kernel, orders, maker),
+        "scatter_cube", ident, Cargo(list(loads)), operands, [pltpu.HBM] * len(operands),
         [jax.ShapeDtypeStruct((rows, width), jnp.float32)], [pltpu.VMEM],
-        [pltpu.VMEM((8, rows, width), jnp.bfloat16)] * 3
-        + [pltpu.SemaphoreType.DMA((len(orders), 8))] * 4,
+        [pltpu.VMEM((8, rows, width), jnp.bfloat16)] * 3 + [semaphores] * 4
+        + (maker.scratch if maker else [semaphores]),
     )
 
 
@@ -988,39 +1135,27 @@
     return summed[0], summed[1]
 
 
-def finish_kernel(parts, *refs):
-    *halves_refs, o_ref = refs
+def finish_kernel(mine_ref, came_ref, o_ref):
     own = pl.program_id(1) == lax.axis_index("x")
-    for part in range(parts):
-
-        @pl.when(pl.program_id(0) == part)
-        def _(mine_ref=halves_refs[2 * part], came_ref=halves_refs[2 * part + 1]):
-            o_ref[...] = jnp.where(own, mine_ref[...], came_ref[...]).astype(jnp.float32)
-
-
-def whole_rows(*pairs):
-    rows, width = pairs[0][0].shape
-    parts = len(pairs)
-    step = min(2048, width)
-    steps = width // step
-
-    def half(part):
-        return pl.BlockSpec(
-            (rows, step), lambda p, x, k, part=part: (0, jnp.where(p == part, k, 0))
-        )
-
+    o_ref[...] = jnp.where(own, mine_ref[...], came_ref[...]).astype(jnp.float32)
+
+
+def whole_rows(mine, came, parts):
+    rows, width = mine.shape
+    step = width // parts
+    half = pl.BlockSpec((rows, step), lambda p, x: (0, p))
     return pl.pallas_call(
-        functools.partial(finish_kernel, parts),
-        grid=(parts, 2, steps),
-        out_shape=jax.ShapeDtypeStruct((rows, 2 * parts * width), jnp.float32),
-        in_specs=[half(part) for part in range(parts) for _ in range(2)],
-        out_specs=pl.BlockSpec((rows, step), lambda p, x, k: (0, (2 * p + x) * steps + k)),
+        finish_kernel,
+        grid=(parts, 2),
+        out_shape=jax.ShapeDtypeStruct((rows, 2 * width), jnp.float32),
+        in_specs=[half, half],
+        out_specs=pl.BlockSpec((rows, step), lambda p, x: (0, 2 * p + x)),
         compiler_params=pltpu.CompilerParams(vmem_limit_bytes=32 * MIB),
         cost_estimate=pl.CostEstimate(
-            flops=0, bytes_accessed=12 * parts * rows * width, transcendentals=0
+            flops=0, bytes_accessed=12 * rows * width, transcendentals=0
         ),
         name="whole_rows",
-    )(*[half for pair in pairs for half in pair])
+    )(mine, came)
 
 
 def owners_product(left, right, parts=1, columns=None, **options):
@@ -1068,11 +1203,15 @@
 
     gain_part = jnp.pad(gains.astype(jnp.float32).T, ((0, 4), (0, 0)))
     begin_part = jnp.broadcast_to(seq_begin.astype(jnp.float32)[None, :], (8, count_rows))
-    loads = [Few(gain_part, False), Few(begin_part, True), Columns(w_qkv, 3)]
+    z_first = (
+        (("zl", "x", "y"), 0, count_rows // 2),
+        (("zl", "y", "x"), count_rows // 2, count_rows // 2),
+    )
+    loads = [Few(gain_part, False), Few(begin_part, True), Columns(w_qkv, 3, near=3)]
     if direct:
-        loads.append(Whole(w_out, "zh"))
+        loads.append(HeadRows(w_out))
     tokens_all, gain_all, begin_all, qkv_cols, *out_other = gather_cube(
-        tokens, 1, loads, halves(count_rows, "zl", "y", "x")
+        tokens, 1, loads, z_first
     )
     same = lax.axis_index("x") == lax.axis_index("zh")
     if direct:
@@ -1120,13 +1259,13 @@
         .astype(jnp.bfloat16)
     )
     x_most = halves(count_rows, "x", "y", "zl")
+    x_or_y = (
+        (("x", "y", "zl"), 0, count_rows // 2),
+        (("y", "x", "zl"), count_rows // 2, count_rows // 2),
+    )
     x_last = halves(count_rows, "zl", "y", "x")
-    z_first = (
-        (("zl", "x", "y"), 0, count_rows // 2),
-        (("zl", "y", "x"), count_rows // 2, count_rows // 2),
-    )
     branch, gate_up_cols = scatter_cube(
-        jnp.dot(attended, out_rows, preferred_element_type=jnp.float32),
+        Partial(attended, out_rows, False),
         3, [Columns(w_gate_up, 2, near=1)], x_most,
     )
     branch_norm, branch_inv = normalize(branch, gain_rows[2])
@@ -1135,7 +1274,7 @@
         middle.astype(jnp.bfloat16), 4, [Columns(w_down_t, far=1, near=3)], x_last,
         FeedForward(gate_up_cols, total), eager=True,
     )
-    (feed_out,) = scatter_cube(contract_last(hidden_bf, down_cols), 5)
+    (feed_out,) = scatter_cube(Partial(hidden_bf, down_cols), 5)
     feed_norm, feed_inv = normalize(feed_out, gain_rows[3])
     mixed = (middle + feed_norm).astype(jnp.bfloat16)
 
@@ -1168,6 +1307,8 @@
     )
     attended_grad = blocks(attended_grad)
     down_other = lax.ppermute(down_sum, "x", [(0, 1), (1, 0)])
+    if direct:
+        out_came = lax.ppermute(out_grad, "zh", [(0, 1), (1, 0)])
     prob_grad = jnp.einsum(
         "bqd,bkd->bqk", attended_grad, value_bf, preferred_element_type=jnp.float32
     )
@@ -1217,26 +1358,24 @@
     loads = [
         owners_product(tokens_all, projected_bf, 3, swap=True, near=1, early=True),
         Owners(gain_terms, swap=True, fold=True, early=True),
+        FinalRows((gate_sum, gate_other), (up_sum, up_other)),
+        FinalRows((down_sum, down_other)),
     ]
     if direct:
-        loads.append(Pair(out_grad, early=True))
-    tokens_sum, qkv_sum, qkv_other, gain_sum, gain_other, *out_both = scatter_cube(
-        contract_last(projected_bf, qkv_cols), 10, loads, x_most
+        out_sum = out_grad.astype(jnp.float32) + out_came.astype(jnp.float32)
+        out_sum = out_sum.astype(jnp.bfloat16)
+        loads.append(Whole(out_sum, "x", near=1))
+    (
+        tokens_sum, qkv_sum, qkv_other, gain_sum, gain_other, grad_gate_up, grad_down_t, *out_other
+    ) = scatter_cube(
+        Partial(projected_bf, qkv_cols), 10, loads, x_or_y
     )
     grad_tokens = middle_grad + tokens_sum
     if direct:
-        grad_out = jnp.where(same, out_both[0], out_both[1]).astype(jnp.float32)
+        grad_out = jnp.where(same, out_sum, out_other[0]).astype(jnp.float32)
     else:
         grad_out = summed_head_rows(out_grad.astype(jnp.float32), owned)
-    third = width // 2
-    grad_qkv = whole_rows(
-        *[
-            (qkv_sum[:, k * third : (k + 1) * third], qkv_other[:, k * third : (k + 1) * third])
-            for k in range(3)
-        ]
-    )
-    grad_gate_up = whole_rows((gate_sum, gate_other), (up_sum, up_other))
-    grad_down_t = whole_rows((down_sum, down_other))
+    grad_qkv = whole_rows(qkv_sum, qkv_other, 3)
     grad_gains = (gain_sum + gain_other)[:4, :owned].T
     return (mixed, grad_tokens, grad_qkv, grad_out, grad_gate_up, grad_down_t, grad_gains)
 

time: 681 us -> 670 us (0.984)
  matrix products: 30.7 us -> 18.5 us
  Pallas kernels: 591 us -> 581 us
    dot_general x3 -> x0, matrix products: 14.2 us -> none  [the longest x2 11.8 us: contract_last(): lax.dot_general(operand, matrix, (((1,), (1,)), ((), ())), preferred_elem...]
    pallas_call x3 -> x1, Pallas kernels: 10.5 us -> 2.79 us  [whole_rows(): pl.pallas_call(finish_kernel, grid=(parts, 2), out_shape=jax.ShapeDtypeSt...]
  transfers between devices with their start and end apart: 1 -> 2, of which waited for: 0 -> 0; matrix products, arithmetic and copies ran while one was open for 6% -> 5% of each run, Pallas kernels for 15% -> 1%
where the time goes in v6:
time: 670 us; the launch traced here: 663 us
  Pallas kernels  581 us (87%)
  other arithmetic  39.9 us (6%)
  local copies, waits for them, and re-layouts  20.5 us (3%)
  matrix products  18.5 us (3%)
    pallas_call x8, Pallas kernels, call(): pl.pallas_call(functools.partial(body, cargo), out_shape=kept, in_specs=[...  559 us
    pallas_call x2, Pallas kernels, sum_cube(): pl.pallas_call(exchange_kernel, out_shape=jax.ShapeDtypeStruct(shape, jnp...  18.8 us
  transfers between devices with their start and end apart: 2, of which 0 were waited for; matrix products, arithmetic and copies ran while one was open for 5% of the time, Pallas kernels for 1%

profile of v6, /device:TPU:0, one launch (start us, length us, event | category | flops | bytes accessed | tf_op | source)
XLA Modules:
  0.0 663.1 jit_solution(5421483538564494890)
XLA Ops:
  0.7 0.7 fusion.43
  1.4 0.2 reduce-window.8
  1.7 0.7 pad_convert_fusion.refs_0_
  2.4 61.2 %gather_cube.4 = (bf16[2048,2048]{1,0:T(8,128)(2,1)}, f32[16,8,128]{2,1,0:T(8,128)S(1)}, f32[16,8,128]{2,1,0:T(8,128)S(1)}, bf16[2048,384]{1,0:T(8,128)(2,1)}, bf16[128,2048]{1,0:T(8,128)(2,1)}) custom-call(bf16[128,2048]{1,0:T(8,128)(2,1)} %x_ref.1, f32[8,128]{1,0:T(8,128)S(1)} %pad_convert_fusion.refs_0_, f32[8,128]{1,0:T(8,128)S(1)} %broadcast_in_dim.12.refs_1_, ...), custom_call_target="tpu_custom_call" | custom-call | bytes 104857600 | tf_op jit(solution)/shard_map/gather_cube/pallas_call | solution.py:741
  63.6 6.4 fusion.55
  70.0 1.2 fusion.52
  71.2 0.9 slice.138
  72.1 1.6 copy.42
  73.6 0.3 multiply_reduce_fusion.10
  74.0 0.3 copy.43
  74.3 0.3 multiply_reduce_fusion.9
  74.7 0.6 pad_maximum_fusion.13.v_ref
  75.3 9.6 %sum_cube.2 = f32[32,128]{1,0:T(8,128)} custom-call(f32[32,128]{1,0:T(8,128)} %pad_maximum_fusion.13.v_ref), custom_call_target="tpu_custom_call" | custom-call | bytes 20971520 | tf_op jit(solution)/shard_map/sum_cube/pallas_call | solution.py:1074
  84.9 0.7 rsqrt_bitcast_fusion.1
  85.8 2.0 copy.41
  87.8 0.3 multiply_multiply_fusion
  88.2 0.3 multiply_multiply_fusion.1
  88.5 5.2 fusion.31
  93.8 1.9 fusion.54
  95.7 3.0 convolution_convert_fusion.1
  98.7 1.9 broadcast_select_fusion.refs_1_.refs_0_
  100.7 91.8 %scatter_cube.4 = (f32[128,2048]{1,0:T(8,128)S(1)}, bf16[2048,1024]{1,0:T(8,128)(2,1)}) custom-call(bf16[2048,128]{1,0:T(8,128)(2,1)} %bitcast.59, bf16[128,2048]{1,0:T(8,128)(2,1)} %broadcast_select_fusion.refs_1_.refs_0_, bf16[128,16384]{1,0:T(8,128)(2,1)} %refs_2_.3), custom_call_target="tpu_custom_call" | custom-call | bytes 104857600 | tf_op jit(solution)/shard_map/scatter_cube/pallas_call | solution.py:741
  192.5 0.2 multiply_reduce_fusion.8
  192.7 1.0 fusion.39.x_ref
  193.7 67.7 %gather_cube.5 = (bf16[2048,512]{1,0:T(8,128)(2,1)}, f32[2048,1024]{1,0:T(8,128)}, bf16[2048,2048]{1,0:T(8,128)(2,1)}, bf16[2048,512]{1,0:T(8,128)(2,1)}) custom-call(bf16[128,2048]{1,0:T(8,128)(2,1)} %fusion.39.x_ref, bf16[2048,1024]{1,0:T(8,128)(2,1)} %get-tuple-element.43.refs_0_.refs_1_, bf16[128,8192]{1,0:T(8,128)(2,1)} %refs_1_.1), custom_call_target="tpu_custom_call" | custom-call | bytes 104857600 | tf_op jit(solution)/shard_map/gather_cube/pallas_call | solution.py:741
  261.4 39.1 %scatter_cube.5 = f32[128,2048]{1,0:T(8,128)S(1)} custom-call(bf16[2048,512]{1,0:T(8,128)(2,1)} %get-tuple-element.44.refs_0_.refs_3_, bf16[2048,512]{1,0:T(8,128)(2,1)} %get-tuple-element.45.refs_1_.refs_0_), custom_call_target="tpu_custom_call" | custom-call | bytes 104857600 | tf_op jit(solution)/shard_map/scatter_cube/pallas_call | solution.py:741
  300.5 0.2 multiply_reduce_fusion.7
  300.7 0.4 fusion.38
  301.1 1.1 fusion.25.x_ref
  302.2 44.1 %gather_cube.6 = (bf16[2048,1024]{1,0:T(8,128)(2,1)}, bf16[2048,2048]{1,0:T(8,128)(2,1)}, bf16[2048,2048]{1,0:T(8,128)(2,1)}) custom-call(bf16[128,2048]{1,0:T(8,128)(2,1)} %fusion.25.x_ref, bf16[2048,512]{1,0:T(8,128)(2,1)} %get-tuple-element.45.refs_1_.refs_0_, bf16[2048,1024]{1,0:T(8,128)(2,1)} %get-tuple-element.43.refs_0_.refs_1_, ...), custom_call_target="tpu_custom_call" | custom-call | bytes 104857600 | tf_op jit(solution)/shard_map/gather_cube/pallas_call | solution.py:741
  346.3 98.9 %scatter_cube.6 = (f32[128,2048]{1,0:T(8,128)S(1)}, bf16[128,4096]{1,0:T(8,128)(2,1)}, bf16[128,4096]{1,0:T(8,128)(2,1)}, bf16[128,4096]{1,0:T(8,128)(2,1)}) custom-call(bf16[2048,2048]{1,0:T(8,128)(2,1)} %get-tuple-element.47.refs_0_, bf16[2048,2048]{1,0:T(8,128)(2,1)} %get-tuple-element.48.refs_1_.refs_3_, ...), custom_call_target="tpu_custom_call" | custom-call | bytes 104857600 | tf_op jit(solution)/shard_map/scatter_cube/pallas_call | solution.py:741
  445.2 0.4 multiply_reduce_fusion
  445.7 1.5 multiply_convert_fusion.3
  447.2 70.9 %gather_cube.7 = (bf16[2048,128]{1,0:T(8,128)(2,1)S(1)}, bf16[128,2048]{1,0:T(8,128)(2,1)S(1)}, bf16[128,4096]{1,0:T(8,128)(2,1)}, bf16[128,4096]{1,0:T(8,128)(2,1)}) custom-call(bf16[128,2048]{1,0:T(8,128)(2,1)} %get-tuple-element.81.x_ref, bf16[128,2048]{1,0:T(8,128)(2,1)S(1)} %copy-done, bf16[2048,128]{1,0:T(8,128)(2,1)S(1)} %bitcast.60, ...), custom_call_target="tpu_custom_call" | custom-call | bytes 104857600 | tf_op jit(solution)/shard_map/gather_cube/pallas_call | solution.py:741
  518.1 0.6 collective-permute-start.1
  518.7 1.2 collective-permute-start
  519.9 0.5 multiply_reduce_fusion.5
  520.4 0.2 multiply_convert_fusion.2
  520.6 0.3 copy-done.19
  520.9 0.2 copy-done.21
  521.1 1.6 convolution_multiply_fusion
  522.7 1.6 convolution_multiply_fusion.1
  524.3 2.5 copy.36
  526.8 2.5 copy.34
  529.3 7.6 %fusion.26 = (f32[2048,64]{1,0:T(8,128)S(1)}, f32[2048,64]{1,0:T(8,128)S(1)}, f32[2048,64]{1,0:T(8,128)S(1)}, f32[2048,64]{1,0:T(8,128)S(1)}) fusion(f32[2048,128]{1,0:T(8,128)} %bitcast.64, f32[64]{0:T(128)S(1)} %multiply_power_fusion, f32[2048]{0:T(1024)S(1)} %bitcast_subtract_fusion, f32[2048,128]{1,0:T(8,128)} %bitcast.63), kind=kLoop, calls=%fused_computation.37 | loop fusion | flops 1835008 | bytes 4202752 | tf_op jit(solution)/shard_map/sub | solution.py:1101
  536.9 1.8 multiply_reduce_fusion.1
  538.9 0.6 pad_maximum_fusion.14.v_ref
  539.5 9.2 %sum_cube.3 = f32[32,128]{1,0:T(8,128)} custom-call(f32[32,128]{1,0:T(8,128)} %pad_maximum_fusion.14.v_ref), custom_call_target="tpu_custom_call" | custom-call | bytes 20971520 | tf_op jit(solution)/shard_map/sum_cube/pallas_call | solution.py:1074
  548.7 0.9 multiply_bitcast_fusion.1
  549.6 3.0 multiply_convert_fusion.1
  552.6 1.9 multiply_convert_fusion
  554.6 3.5 convolution_convert_fusion
  558.1 2.5 pad_maximum_fusion.refs_0_.refs_3_
  560.7 2.0 add_convert_fusion.refs_11_
  562.6 85.4 %scatter_cube.7 = (f32[128,2048]{1,0:T(8,128)S(1)}, bf16[128,3072]{1,0:T(8,128)(2,1)}, bf16[128,3072]{1,0:T(8,128)(2,1)}, f32[8,128]{1,0:T(8,128)}, f32[8,128]{1...) custom-call(bf16[2048,384]{1,0:T(8,128)(2,1)} %pad_maximum_fusion.refs_0_.refs_3_, ...), custom_call_target="tpu_custom_call" | custom-call | bytes 104857600 | tf_op jit(solution)/shard_map/scatter_cube/pallas_call | solution.py:741
  648.1 0.8 add.98
  648.9 0.6 slice_bitcast_fusion.2
  649.5 1.0 select_convert_fusion
  650.5 1.2 fusion.42
  651.7 2.8 whole_rows.1
  654.5 0.9 copy-done.14
  655.4 4.3 copy.47
  659.7 1.0 copy-done.17
  660.6 2.0 copy.48
  (76 shorter events, 0.7 us)
Async XLA Ops:
  73.6 14.5 %copy-start.4 = (f32[2048,128]{1,0:T(8,128)}, f32[2048,128]{1,0:T(8,128)S(1)}, u32[]{:S(2)}) copy-start(f32[2048,128]{1,0:T(8,128)S(1)} %copy.42) | copy-start | bytes 3145732
  93.7 5.0 copy-start.18
  93.7 5.0 copy-start.20
  93.8 5.0 copy-start.22
  93.8 5.0 copy-start.24
  100.7 92.0 %copy-start.15 = (bf16[128,2048]{1,0:T(8,128)(2,1)S(1)}, bf16[128,2048]{1,0:T(8,128)(2,1)}, u32[]{:S(2)}) copy-start(bf16[128,2048]{1,0:T(8,128)(2,1)} %x_ref.1) | copy-start | bytes 1572868
  261.4 39.3 %copy-start.6 = (bf16[128,2048]{1,0:T(8,128)(2,1)S(1)}, bf16[128,2048]{1,0:T(8,128)(2,1)}, u32[]{:S(2)}) copy-start(bf16[128,2048]{1,0:T(8,128)(2,1)} %param.15) | copy-start | bytes 1572868
  445.6 1.5 copy-start
  445.6 1.5 copy-start.1
  447.2 72.7 %copy-start.27 = (f32[16,128,128]{1,2,0:T(8,128)S(1)}, f32[16,128,128]{1,2,0:T(8,128)}, u32[]{:S(2)}) copy-start(f32[16,128,128]{1,2,0:T(8,128)} %get-tuple-element.102) | copy-start | bytes 3145732
  447.2 72.7 %copy-start.28 = (bf16[2048,128]{1,0:T(8,128)(2,1)S(1)}, bf16[2048,128]{1,0:T(8,128)(2,1)}, u32[]{:S(2)}) copy-start(bf16[2048,128]{1,0:T(8,128)(2,1)} %copy.41) | copy-start | bytes 1572868
  518.1 42.6 %collective-permute-start.1 = (bf16[128,2048]{1,0:T(8,128)(2,1)S(1)}, bf16[128,2048]{1,0:T(8,128)(2,1)}, u32[]{:S(2)}, u32[]{:S(2)}) collective-permute-start(bf16[128,2048]{1,0:T(8,128)(2,1)S(1)} %get-tuple-element.58), channel_id=1, source_target_pairs={{0,8},{8,0},{1,9},{9,1},{2,10},{10,2},{3,11},{11,3},{4,12},{12,4},... | collective-permute-start | bytes 1572872 | tf_op jit(solution)/shard_map/ppermute | solution.py:1311
  518.7 43.9 %collective-permute-start = (bf16[128,4096]{1,0:T(8,128)(2,1)}, bf16[128,4096]{1,0:T(8,128)(2,1)}, u32[]{:S(2)}, u32[]{:S(2)}) collective-permute-start(bf16[128,4096]{1,0:T(8,128)(2,1)} %get-tuple-element.57.refs_9_), channel_id=1, source_target_pairs={{0,16},{16,0},{1,17},{17,1},{2,18},{18,2},{3,19},{19,3},{4,20},{20... | collective-permute-start | bytes 3145736 | tf_op jit(solution)/shard_map/ppermute | solution.py:1309
  519.9 1.0 copy-start.19
  519.9 1.2 copy-start.21
  520.4 2.3 copy-start.23
  520.4 2.3 copy-start.25
  529.3 7.6 %copy-start.5 = (f32[2048,128]{1,0:T(8,128)S(1)}, f32[2048,128]{1,0:T(8,128)}, u32[]{:S(2)}) copy-start(f32[2048,128]{1,0:T(8,128)} %copy-done.4) | copy-start | bytes 3145732
  536.9 1.9 copy-start.8
  536.9 1.9 copy-start.10
  536.9 1.9 copy-start.12
  536.9 2.0 copy-start.13
  548.7 3.9 copy-start.9
  548.7 3.9 copy-start.11
  554.6 3.5 copy-start.26
  562.6 86.8 %copy-start.16 = (bf16[128,2048]{1,0:T(8,128)(2,1)S(1)}, bf16[128,2048]{1,0:T(8,128)(2,1)}, u32[]{:S(2)}) copy-start(bf16[128,2048]{1,0:T(8,128)(2,1)} %add_convert_fusion.refs_11_) | copy-start | bytes 1572868
  562.6 87.9 %copy-start.7 = (bf16[128,2048]{1,0:T(8,128)(2,1)S(1)}, bf16[128,2048]{1,0:T(8,128)(2,1)}, u32[]{:S(2)}) copy-start(bf16[128,2048]{1,0:T(8,128)(2,1)} %param.15) | copy-start | bytes 1572868
  648.0 3.6 copy-start.2
  648.1 3.6 copy-start.3
  650.5 4.9 copy-start.14
  655.4 5.2 copy-start.17

commit v7 on v6

--- a/solution.py
+++ b/solution.py
@@ -422,6 +422,90 @@
 
     def leave(self):
         self.copy.wait_send()
+
+
+class HeadSums(Load, Swap):
+    def __init__(self, source, **stages):
+        super().__init__(source, **stages)
+        rows, width = source.shape
+        self.half = jax.ShapeDtypeStruct((rows // 2, width), source.dtype)
+        self.outs = [self.half] * 2
+
+    def spaces(self):
+        return [pltpu.VMEM], [pltpu.HBM] * 2
+
+    def moves(self):
+        return [((1, ()), 0), ((0, ("x",)), 0), ((0, ("x",)), 0)]
+
+    def scratch(self):
+        return self.semaphores() + self.swap_scratch() + [
+            pltpu.VMEM((3,) + self.half.shape, jnp.bfloat16),
+            pltpu.VMEM(self.half.shape, jnp.bfloat16),
+        ]
+
+    def bind(self, here, sources, targets, scratch):
+        self.here, self.dst = here, targets
+        (self.source,) = sources
+        send, recv, self.sems, self.terms, self.total = scratch
+        self.home = here["x"] == here["zh"]
+        rows = self.half.shape[0]
+
+        def copy(source, term, k, device):
+            return pltpu.make_async_remote_copy(
+                src_ref=source, dst_ref=self.terms.at[term],
+                send_sem=send.at[k], recv_sem=recv.at[term],
+                device_id=device, device_id_type=MESH,
+            )
+
+        first, second = (self.source.at[pl.ds(k * rows, rows)] for k in range(2))
+        across = {"zh": 1 - here["zh"]}
+        self.near = copy(second, 0, 0, flip(here, "x"))
+        self.relay = copy(self.terms.at[2], 1, 1, across)
+        self.far = copy(first, 1, 1, across)
+        self.hand = copy(second, 2, 0, flip(here, "x"))
+
+    def start(self, stage):
+        if stage == self.stages[1]:
+
+            @pl.when(self.home)
+            def _():
+                self.near.start()
+
+            @pl.when(jnp.logical_not(self.home))
+            def _():
+                self.hand.start()
+                self.far.start()
+
+        if stage == self.stages[0]:
+
+            @pl.when(self.home)
+            def _():
+                self.hand.wait_recv()
+                self.relay.start()
+
+    def land(self):
+        self.far.wait_recv()
+
+        @pl.when(jnp.logical_not(self.home))
+        def _():
+            self.near.wait_recv()
+
+    def finish(self):
+        rows = self.half.shape[0]
+
+        @pl.when(self.home)
+        def _():
+            self.terms[0] = self.source[pl.ds(0, rows)]
+
+        self.total[...] = (
+            self.terms[0].astype(jnp.float32) + self.terms[1].astype(jnp.float32)
+        ).astype(jnp.bfloat16)
+        self.give(self.total, self.sems)
+
+    def leave(self):
+        self.near.wait_send()
+        self.far.wait_send()
+        self.given_wait()
 
 
 class FinalRows(Load):
@@ -1056,6 +1140,7 @@
     for copy in copies:
         copy.wait_recv()
     slots[0] = v_ref[...]
+    o_ref[...] = jnp.zeros_like(o_ref)
     for row in range(v_ref.shape[0]):
         kind, mine = divmod(row, MEMBERS)
         terms = [
@@ -1064,7 +1149,7 @@
         ]
         while len(terms) > 1:
             terms = [terms[2 * i] + terms[2 * i + 1] for i in range(len(terms) // 2)]
-        o_ref[pl.ds(row, 1), :] = terms[0]
+        o_ref[mine, pl.ds(kind, 1), :] = terms[0]
     for copy in copies:
         copy.wait_send()
 
@@ -1073,7 +1158,7 @@
     shape = values.shape
     return pl.pallas_call(
         exchange_kernel,
-        out_shape=jax.ShapeDtypeStruct(shape, jnp.float32),
+        out_shape=jax.ShapeDtypeStruct((MEMBERS, 8, shape[1]), jnp.float32),
         in_specs=[pl.BlockSpec(memory_space=pltpu.VMEM)],
         out_specs=pl.BlockSpec(memory_space=pltpu.VMEM),
         scratch_shapes=[
@@ -1090,16 +1175,8 @@
 def rope_tables(positions):
     frequency = theta_base ** (-2.0 * jnp.arange(HD // 2).astype(jnp.float32) / HD)
     angles = positions[:, None] * frequency[None, :]
-    return (jnp.cos(angles), jnp.sin(angles))
-
-
-def rotate(values, cos_table, sin_table):
-    half_width = values.shape[-1] // 2
-    former = values[..., :half_width]
-    latter = values[..., half_width:]
-    return jnp.concatenate(
-        [former * cos_table - latter * sin_table, latter * cos_table + former * sin_table], axis=-1
-    )
+    cosines, sines = jnp.cos(angles), jnp.sin(angles)
+    return jnp.concatenate([cosines, cosines, -sines, sines], axis=1)
 
 
 def normalize(values, scales):
@@ -1128,11 +1205,145 @@
     )
 
 
-def row_sums(pair, ident):
-    total = pair[0].shape[0]
-    flat = jnp.concatenate([v.reshape(MEMBERS, total // MEMBERS) for v in pair], axis=0)
-    summed = sum_cube(flat, ident).reshape(2, total, 1)
-    return summed[0], summed[1]
+TOGETHER = 8
+
+
+def turn(values, cos_table, sin_table):
+    return values * cos_table + pltpu.roll(values, HD // 2, 1) * sin_table
+
+
+def project_kernel(x_ref, w_ref, o_ref, sums_out):
+    value = jnp.dot(x_ref[...], w_ref[...], preferred_element_type=jnp.float32)
+    o_ref[...] = value
+    rows = x_ref.shape[0] // TOGETHER
+    for block in range(TOGETHER):
+        for kind in range(2):
+            part = value[block * rows : (block + 1) * rows, kind * HD : (kind + 1) * HD]
+            sums_out[pl.ds(kind * MEMBERS + pl.program_id(0) * TOGETHER + block, 1)] = jnp.sum(
+                (part * part).T, axis=0, keepdims=True
+            )
+
+
+def rope_of(positions, table):
+    place_of = lax.broadcasted_iota(jnp.int32, (positions.shape[0], table.shape[0]), 1)
+    chosen = (place_of.astype(jnp.float32) == positions).astype(jnp.float32)
+    found = jnp.dot(
+        chosen, table, preferred_element_type=jnp.float32, precision=lax.Precision.HIGHEST
+    )
+    return found[:, :HD], found[:, HD:]
+
+
+def attend_kernel(width, p_ref, s_ref, b_ref, t_ref, g_ref, *outs):
+    q_out, k_out, v_out, qu_out, ku_out, a_out, o_out = outs
+    rows = p_ref.shape[0] // TOGETHER
+    for block in range(TOGETHER):
+        span = pl.ds(block * rows, rows)
+        scales = lax.rsqrt(s_ref[block].T / width + epsilon)
+        begin = b_ref[block].T[:, 0:1]
+        row = lax.broadcasted_iota(jnp.int32, (rows, 1), 0).astype(jnp.float32)
+        cos_table, sin_table = rope_of(row - begin, t_ref[...])
+        query_unit = p_ref[span, 0:HD] * scales[:, 0:1]
+        key_unit = p_ref[span, HD : 2 * HD] * scales[:, 1:2]
+        values = p_ref[span, 2 * HD : 3 * HD].astype(jnp.bfloat16)
+        queries = turn(query_unit * g_ref[0:1], cos_table, sin_table).astype(jnp.bfloat16)
+        keys = turn(key_unit * g_ref[1:2], cos_table, sin_table).astype(jnp.bfloat16)
+        scores = contract_last(queries, keys) * (1.0 / math.sqrt(HD))
+        column = lax.broadcasted_iota(jnp.int32, scores.shape, 1).astype(jnp.float32)
+        scores = jnp.where((column <= row) & (column >= begin), scores, -1e30)
+        exponent = jnp.exp(scores - jnp.max(scores, axis=1, keepdims=True))
+        attention = exponent / jnp.sum(exponent, axis=1, keepdims=True)
+        q_out[span] = queries
+        k_out[span] = keys
+        v_out[span] = values
+        qu_out[span] = query_unit
+        ku_out[span] = key_unit
+        a_out[span] = attention
+        o_out[span] = jnp.dot(
+            attention.astype(jnp.bfloat16), values, preferred_element_type=jnp.float32
+        ).astype(jnp.bfloat16)
+
+
+def attend_back_kernel(
+    d_ref, q_ref, k_ref, v_ref, qu_ref, ku_ref, a_ref, b_ref, t_ref, g_ref, *outs
+):
+    qs_out, ks_out, vg_out, dots_out, gains_out = outs
+    rows = d_ref.shape[0] // TOGETHER
+    step = pl.program_id(0)
+    scale = 1.0 / math.sqrt(HD)
+
+    @pl.when(step == 0)
+    def _():
+        gains_out[...] = jnp.zeros_like(gains_out)
+
+    for block in range(TOGETHER):
+        span = pl.ds(block * rows, rows)
+        grad, attention = d_ref[span], a_ref[span]
+        prob_grad = contract_last(grad, v_ref[span])
+        weighed = jnp.sum(attention * prob_grad, axis=1, keepdims=True)
+        score_grad = (attention * (prob_grad - weighed)).astype(jnp.bfloat16)
+        vg_out[span] = contract_first(attention.astype(jnp.bfloat16), grad).astype(jnp.bfloat16)
+        query_grad = jnp.dot(score_grad, k_ref[span], preferred_element_type=jnp.float32) * scale
+        key_grad = contract_first(score_grad, q_ref[span]) * scale
+        row = lax.broadcasted_iota(jnp.int32, (rows, 1), 0).astype(jnp.float32)
+        cos_table, sin_table = rope_of(row - b_ref[block].T[:, 0:1], t_ref[...])
+        sin_table = -sin_table
+        query_grad = turn(query_grad, cos_table, sin_table)
+        key_grad = turn(key_grad, cos_table, sin_table)
+        query_unit, key_unit = qu_ref[span], ku_ref[span]
+        gains_out[0:1] += jnp.sum(query_grad * query_unit, axis=0, keepdims=True)
+        gains_out[1:2] += jnp.sum(key_grad * key_unit, axis=0, keepdims=True)
+        query_grad = query_grad * g_ref[0:1]
+        key_grad = key_grad * g_ref[1:2]
+        qs_out[span] = query_grad
+        ks_out[span] = key_grad
+        query_dot = jnp.sum((query_grad * query_unit).T, axis=0, keepdims=True)
+        key_dot = jnp.sum((key_grad * key_unit).T, axis=0, keepdims=True)
+        dots_out[pl.ds(step * TOGETHER + block, 1)] = query_dot
+        dots_out[pl.ds(MEMBERS + step * TOGETHER + block, 1)] = key_dot
+
+
+def project_back_kernel(width, s_ref, t_ref, qu_ref, ku_ref, qs_ref, ks_ref, vg_ref, o_ref):
+    rows = qu_ref.shape[0] // TOGETHER
+    for block in range(TOGETHER):
+        span = pl.ds(block * rows, rows)
+        scales = lax.rsqrt(s_ref[block].T / width + epsilon)
+        means = t_ref[block].T / width
+        query_grad = scales[:, 0:1] * (qs_ref[span] - qu_ref[span] * means[:, 0:1])
+        key_grad = scales[:, 1:2] * (ks_ref[span] - ku_ref[span] * means[:, 1:2])
+        o_ref[span, 0:HD] = query_grad.astype(jnp.bfloat16)
+        o_ref[span, HD : 2 * HD] = key_grad.astype(jnp.bfloat16)
+        o_ref[span, 2 * HD : 3 * HD] = vg_ref[span]
+
+
+def by_blocks(body, name, operands, outs, whole=()):
+    total = operands[0].shape[0]
+    if operands[0].ndim == 3:
+        total = total * operands[0].shape[2]
+    span = total // MEMBERS * TOGETHER
+
+    def spec(array):
+        shape = array.shape
+        if len(shape) == 3:
+            return pl.BlockSpec((TOGETHER,) + shape[1:], lambda k: (k, 0, 0))
+        if shape[0] == total:
+            return pl.BlockSpec((span, shape[1]), lambda k: (k, 0))
+        return pl.BlockSpec(shape, lambda k: (0, 0))
+
+    return pl.pallas_call(
+        body,
+        grid=(MEMBERS // TOGETHER,),
+        out_shape=[pltpu.HBM(v.shape, v.dtype) for v in outs],
+        in_specs=[
+            pl.BlockSpec(v.shape, lambda k: (0, 0)) if n in whole else spec(v)
+            for n, v in enumerate(operands)
+        ],
+        out_specs=[spec(v) for v in outs],
+        compiler_params=pltpu.CompilerParams(vmem_limit_bytes=24 * MIB),
+        cost_estimate=pl.CostEstimate(
+            flops=4 * total * HD * HD, bytes_accessed=8 * MIB, transcendentals=total * HD
+        ),
+        name=name,
+    )(*[in_hbm(v, pltpu.HBM) for v in operands])
 
 
 def finish_kernel(mine_ref, came_ref, o_ref):
@@ -1196,11 +1407,11 @@
     owned = gains.shape[0]
     groups = lax.axis_size("zh")
     total = MEMBERS * count_rows
-    score_scale = 1.0 / math.sqrt(HD)
     direct = heads_are_owners(owned)
     local_rows = jnp.arange(count_rows, dtype=jnp.int32)
     seq_begin = lax.cummax(jnp.where(starts == 1, local_rows, 0), axis=0)
 
+    rope_table = rope_tables(local_rows.astype(jnp.float32))
     gain_part = jnp.pad(gains.astype(jnp.float32).T, ((0, 4), (0, 0)))
     begin_part = jnp.broadcast_to(seq_begin.astype(jnp.float32)[None, :], (8, count_rows))
     z_first = (
@@ -1219,44 +1430,22 @@
     else:
         out_rows = gathered_head_rows(w_out)
     gain_rows = gain_all[:, :4].transpose(1, 0, 2).reshape(4, width)
-    begin_all = begin_all[:, 0]
     head = lax.axis_index(("x", "zl", "y", "c"))
     head_gains = lax.dynamic_slice_in_dim(gain_rows, head * HD, HD, axis=1)
-    rows_f32 = local_rows.astype(jnp.float32)
-    positions = (rows_f32[None, :] - begin_all).reshape(total)
-    cos_table, sin_table = rope_tables(positions)
-    allowed = (rows_f32[None, None, :] <= rows_f32[None, :, None]) & (
-        rows_f32[None, None, :] >= begin_all[:, :, None]
-    )
-
-    def blocks(values):
-        return values.reshape(MEMBERS, count_rows, HD)
-
-    projected = jnp.dot(tokens_all, qkv_cols, preferred_element_type=jnp.float32)
-    query_raw = projected[:, :HD]
-    key_raw = projected[:, HD : 2 * HD]
-    value_bf = blocks(projected[:, 2 * HD :].astype(jnp.bfloat16))
-    query_sq, key_sq = row_sums(
-        (jnp.sum(query_raw * query_raw, axis=1), jnp.sum(key_raw * key_raw, axis=1)), 2
-    )
-    query_inv = lax.rsqrt(query_sq / width + epsilon)
-    key_inv = lax.rsqrt(key_sq / width + epsilon)
-    query_unit = query_raw * query_inv
-    key_unit = key_raw * key_inv
-    query_bf = blocks(rotate(query_unit * head_gains[0], cos_table, sin_table).astype(jnp.bfloat16))
-    key_bf = blocks(rotate(key_unit * head_gains[1], cos_table, sin_table).astype(jnp.bfloat16))
-    scores = (
-        jnp.einsum("bqd,bkd->bqk", query_bf, key_bf, preferred_element_type=jnp.float32)
-        * score_scale
-    )
-    scores = jnp.where(allowed, scores, -1e30)
-    exponent = jnp.exp(scores - jnp.max(scores, axis=-1, keepdims=True))
-    attention_f32 = exponent / jnp.sum(exponent, axis=-1, keepdims=True)
-    attention = attention_f32.astype(jnp.bfloat16)
-    attended = (
-        jnp.einsum("bqk,bkd->bqd", attention, value_bf, preferred_element_type=jnp.float32)
-        .reshape(total, HD)
-        .astype(jnp.bfloat16)
+    def of(width, kind):
+        return jax.ShapeDtypeStruct((total, width), kind)
+
+    narrow, wide = of(HD, jnp.bfloat16), of(HD, jnp.float32)
+    sums = jax.ShapeDtypeStruct((2 * MEMBERS, count_rows), jnp.float32)
+    projected, squares = by_blocks(
+        project_kernel, "project", [tokens_all, qkv_cols], [of(3 * HD, jnp.float32), sums],
+        whole=(1,),
+    )
+    squares = sum_cube(squares, 2)
+    query_bf, key_bf, value_bf, query_unit, key_unit, attention, attended = by_blocks(
+        functools.partial(attend_kernel, width), "attend",
+        [projected, squares, begin_all, rope_table, head_gains],
+        [narrow, narrow, narrow, wide, wide, wide, narrow],
     )
     x_most = halves(count_rows, "x", "y", "zl")
     x_or_y = (
@@ -1305,47 +1494,29 @@
             Whole(up_sum, "x", near=3),
         ], z_first, BranchBack(out_rows, attended),
     )
-    attended_grad = blocks(attended_grad)
-    down_other = lax.ppermute(down_sum, "x", [(0, 1), (1, 0)])
-    if direct:
-        out_came = lax.ppermute(out_grad, "zh", [(0, 1), (1, 0)])
-    prob_grad = jnp.einsum(
-        "bqd,bkd->bqk", attended_grad, value_bf, preferred_element_type=jnp.float32
-    )
-    score_bf = (
-        attention_f32 * (prob_grad - jnp.sum(attention_f32 * prob_grad, axis=-1, keepdims=True))
-    ).astype(jnp.bfloat16)
-    value_grad = jnp.einsum(
-        "bqk,bqd->bkd", attention, attended_grad, preferred_element_type=jnp.float32
-    ).reshape(total, HD)
-    query_grad = (
-        jnp.einsum("bqk,bkd->bqd", score_bf, key_bf, preferred_element_type=jnp.float32)
-        * score_scale
-    ).reshape(total, HD)
-    key_grad = (
-        jnp.einsum("bqk,bqd->bkd", score_bf, query_bf, preferred_element_type=jnp.float32)
-        * score_scale
-    ).reshape(total, HD)
-    query_grad = rotate(query_grad, cos_table, -sin_table)
-    key_grad = rotate(key_grad, cos_table, -sin_table)
-    query_scaled = query_grad * head_gains[0]
-    key_scaled = key_grad * head_gains[1]
-    query_dot, key_dot = row_sums(
-        (jnp.sum(query_scaled * query_unit, axis=1), jnp.sum(key_scaled * key_unit, axis=1)), 9
-    )
-    query_raw_grad = query_inv * (query_scaled - query_unit * (query_dot / width))
-    key_raw_grad = key_inv * (key_scaled - key_unit * (key_dot / width))
-    projected_bf = jnp.concatenate([query_raw_grad, key_raw_grad, value_grad], axis=1).astype(
-        jnp.bfloat16
-    )
-
-    gain_head = jnp.stack(
-        [jnp.sum(query_grad * query_unit, axis=0), jnp.sum(key_grad * key_unit, axis=0)]
-    )
+    query_scaled, key_scaled, value_grad, dots, gain_head = by_blocks(
+        attend_back_kernel, "attend_back",
+        [
+            attended_grad, query_bf, key_bf, value_bf, query_unit, key_unit, attention,
+            begin_all, rope_table, head_gains,
+        ],
+        [
+            wide, wide, narrow,
+            sums,
+            jax.ShapeDtypeStruct((8, HD), jnp.float32),
+        ],
+    )
+    dots = sum_cube(dots, 9)
+    (projected_bf,) = by_blocks(
+        functools.partial(project_back_kernel, width), "project_back",
+        [squares, dots, query_unit, key_unit, query_scaled, key_scaled, value_grad],
+        [of(3 * HD, jnp.bfloat16)],
+    )
+
     gain_terms = jnp.concatenate(
         [
             lax.dynamic_update_slice_in_dim(
-                jnp.zeros((2, width), jnp.float32), gain_head, head * HD, axis=1
+                jnp.zeros((2, width), jnp.float32), gain_head[:2], head * HD, axis=1
             ),
             jnp.stack([gain_branch, gain_feed]),
         ]
@@ -1359,23 +1530,23 @@
         owners_product(tokens_all, projected_bf, 3, swap=True, near=1, early=True),
         Owners(gain_terms, swap=True, fold=True, early=True),
         FinalRows((gate_sum, gate_other), (up_sum, up_other)),
-        FinalRows((down_sum, down_other)),
+        Whole(down_sum, "x", near=1),
     ]
     if direct:
-        out_sum = out_grad.astype(jnp.float32) + out_came.astype(jnp.float32)
-        out_sum = out_sum.astype(jnp.bfloat16)
-        loads.append(Whole(out_sum, "x", near=1))
+        loads.append(HeadSums(out_grad, near=1, early=True))
     (
-        tokens_sum, qkv_sum, qkv_other, gain_sum, gain_other, grad_gate_up, grad_down_t, *out_other
+        tokens_sum, qkv_sum, qkv_other, gain_sum, gain_other, grad_gate_up, down_other, *out_both
     ) = scatter_cube(
         Partial(projected_bf, qkv_cols), 10, loads, x_or_y
     )
     grad_tokens = middle_grad + tokens_sum
     if direct:
-        grad_out = jnp.where(same, out_sum, out_other[0]).astype(jnp.float32)
+        first, second = (jnp.where(same, out_both[k], out_both[1 - k]) for k in range(2))
+        grad_out = jnp.concatenate([first, second], axis=0).astype(jnp.float32)
     else:
         grad_out = summed_head_rows(out_grad.astype(jnp.float32), owned)
     grad_qkv = whole_rows(qkv_sum, qkv_other, 3)
+    grad_down_t = whole_rows(down_sum, down_other, 1)
     grad_gains = (gain_sum + gain_other)[:4, :owned].T
     return (mixed, grad_tokens, grad_qkv, grad_out, grad_gate_up, grad_down_t, grad_gains)
 

time: 670 us -> 658 us (0.982)
  Pallas kernels: 581 us -> 631 us
  other arithmetic: 39.9 us -> 11.3 us
  matrix products: 18.5 us -> 0 us
  local copies, waits for them, and re-layouts: 20.5 us -> 8.1 us
    pallas_call x2 -> x6, Pallas kernels: 18.8 us -> 55.9 us  [the longest x4 36.9 us: by_blocks(): pl.pallas_call(body, grid=(MEMBERS // TOGETHER,), out_shape=[pltpu.HBM(v....]
    dot_general x6 -> x0, matrix products: 16.5 us -> none  [the longest x1 6.37 us: shards(): jnp.dot(tokens_all, qkv_cols, preferred_element_type=jnp.float32)]
    pallas_call x8, Pallas kernels: 559 us -> 570 us  [call(): pl.pallas_call(functools.partial(body, cargo), out_shape=kept, in_specs=[...]
    another operation x5 -> x2, other arithmetic: 11 us -> 0.83 us
    sub x2 -> x0, other arithmetic: 7.56 us -> none  [the longest x1 7.56 us: rotate(): former * cos_table - latter * sin_table]
  transfers between devices with their start and end apart: 2 -> 0, of which waited for: 0 -> 0; matrix products, arithmetic and copies ran while one was open for 5% -> 0% of each run, Pallas kernels for 1% -> 0%
where the time goes in v7:
time: 658 us; the launch traced here: 652 us
  Pallas kernels  631 us (96%)
  other arithmetic  11.3 us (2%)
  local copies, waits for them, and re-layouts  8.1 us (1%)
    pallas_call x8, Pallas kernels, call(): pl.pallas_call(functools.partial(body, cargo), out_shape=kept, in_specs=[...  570 us
    pallas_call x4, Pallas kernels, by_blocks(): pl.pallas_call(body, grid=(MEMBERS // TOGETHER,), out_shape=[pltpu.HBM(v....  36.9 us
    pallas_call x2, Pallas kernels, sum_cube(): pl.pallas_call(exchange_kernel, out_shape=jax.ShapeDtypeStruct((MEMBERS,...  19 us

profile of v7, /device:TPU:0, one launch (start us, length us, event | category | flops | bytes accessed | tf_op | source)
XLA Modules:
  0.0 651.8 jit_solution(14866332383956272874)
XLA Ops:
  0.6 0.7 fusion.9
  1.3 0.1 copy.17
  1.4 0.2 reduce-window.8
  1.6 0.1 convert_reduce_fusion
  1.7 0.7 pad_convert_fusion.refs_0_
  2.4 61.2 %gather_cube.4 = (bf16[2048,2048]{1,0:T(8,128)(2,1)}, f32[16,8,128]{2,1,0:T(8,128)S(1)}, f32[16,8,128]{2,1,0:T(8,128)S(1)}, bf16[2048,384]{1,0:T(8,128)(2,1)}, bf16[128,2048]{1,0:T(8,128)(2,1)}) custom-call(bf16[128,2048]{1,0:T(8,128)(2,1)} %x_ref.1, f32[8,128]{1,0:T(8,128)S(1)} %pad_convert_fusion.refs_0_, f32[8,128]{1,0:T(8,128)S(1)} %broadcast_in_dim.9.refs_1_, ...), custom_call_target="tpu_custom_call" | custom-call | bytes 104857600 | tf_op jit(solution)/shard_map/gather_cube/pallas_call | solution.py:825
  63.6 0.0 copy-start.7
  63.6 0.6 copy-done.7
  64.2 0.6 constant_dynamic-slice_fusion.g_ref
  64.8 8.6 %project.1 = (f32[2048,384]{1,0:T(8,128)}, f32[32,128]{1,0:T(8,128)}) custom-call(bf16[2048,2048]{1,0:T(8,128)(2,1)} %get-tuple-element.52.x_ref.refs_2_, bf16[2048,384]{1,0:T(8,128)(2,1)} %get-tuple-element.53.w_ref.refs_1_), custom_call_target="tpu_custom_call" | custom-call | flops 134217728 | bytes 8388608 | tf_op jit(solution)/shard_map/project/pallas_call | solution.py:1332
  73.4 0.0 copy-start.10
  73.4 0.0 copy-start.11
  73.4 9.8 %sum_cube.2.s_ref = f32[16,8,128]{2,1,0:T(8,128)} custom-call(f32[32,128]{1,0:T(8,128)} %get-tuple-element.55.v_ref), custom_call_target="tpu_custom_call" | custom-call | bytes 20971520 | tf_op jit(solution)/shard_map/sum_cube/pallas_call | solution.py:1159
  83.2 0.3 multiply_cosine_fusion
  83.5 0.8 pad_maximum_fusion.t_ref
  84.2 15.4 %attend.1 = (bf16[2048,128]{1,0:T(8,128)(2,1)}, bf16[2048,128]{1,0:T(8,128)(2,1)}, bf16[2048,128]{1,0:T(8,128)(2,1)}, f32[2048,128]{1,0:T(8,128)}, f32[2048,128]...) custom-call(f32[2048,384]{1,0:T(8,128)} %get-tuple-element.54.p_ref, f32[16,8,128]{2,1,0:T(8,128)} %sum_cube.2.s_ref, ...), custom_call_target="tpu_custom_call" | custom-call | flops 134217728 | bytes 8388608 | tf_op jit(solution)/shard_map/attend/pallas_call | solution.py:1332
  99.7 0.0 copy-start.9
  99.7 0.0 copy-done.10
  99.7 0.0 copy-done.11
  99.7 0.9 broadcast_select_fusion.refs_1_.refs_0_
  100.6 91.8 %scatter_cube.4 = (f32[128,2048]{1,0:T(8,128)S(1)}, bf16[2048,1024]{1,0:T(8,128)(2,1)}) custom-call(bf16[2048,128]{1,0:T(8,128)(2,1)} %get-tuple-element.58.refs_0_.refs_1_, bf16[128,2048]{1,0:T(8,128)(2,1)} %broadcast_select_fusion.refs_1_.refs_0_, bf16[128,16384]{1,0:T(8,128)(2,1)} %refs_2_.3), custom_call_target="tpu_custom_call" | custom-call | bytes 104857600 | tf_op jit(solution)/shard_map/scatter_cube/pallas_call | solution.py:825
  192.4 0.2 multiply_reduce_fusion.3
  192.6 0.0 copy-done.9
  192.6 1.0 fusion.6.x_ref
  193.6 67.7 %gather_cube.5 = (bf16[2048,512]{1,0:T(8,128)(2,1)}, f32[2048,1024]{1,0:T(8,128)}, bf16[2048,2048]{1,0:T(8,128)(2,1)}, bf16[2048,512]{1,0:T(8,128)(2,1)}) custom-call(bf16[128,2048]{1,0:T(8,128)(2,1)} %fusion.6.x_ref, bf16[2048,1024]{1,0:T(8,128)(2,1)} %get-tuple-element.61.refs_0_.refs_1_, bf16[128,8192]{1,0:T(8,128)(2,1)} %refs_1_.1), custom_call_target="tpu_custom_call" | custom-call | bytes 104857600 | tf_op jit(solution)/shard_map/gather_cube/pallas_call | solution.py:825
  261.3 0.0 copy-start.8
  261.3 39.1 %scatter_cube.5 = f32[128,2048]{1,0:T(8,128)S(1)} custom-call(bf16[2048,512]{1,0:T(8,128)(2,1)} %get-tuple-element.62.refs_0_.refs_3_, bf16[2048,512]{1,0:T(8,128)(2,1)} %get-tuple-element.63.refs_1_.refs_0_), custom_call_target="tpu_custom_call" | custom-call | bytes 104857600 | tf_op jit(solution)/shard_map/scatter_cube/pallas_call | solution.py:825
  300.4 0.2 multiply_reduce_fusion.2
  300.6 0.0 copy-done.8
  300.6 0.4 fusion.5
  301.0 1.1 fusion.4.x_ref
  302.1 44.1 %gather_cube.6 = (bf16[2048,1024]{1,0:T(8,128)(2,1)}, bf16[2048,2048]{1,0:T(8,128)(2,1)}, bf16[2048,2048]{1,0:T(8,128)(2,1)}) custom-call(bf16[128,2048]{1,0:T(8,128)(2,1)} %fusion.4.x_ref, bf16[2048,512]{1,0:T(8,128)(2,1)} %get-tuple-element.63.refs_1_.refs_0_, bf16[2048,1024]{1,0:T(8,128)(2,1)} %get-tuple-element.61.refs_0_.refs_1_, ...), custom_call_target="tpu_custom_call" | custom-call | bytes 104857600 | tf_op jit(solution)/shard_map/gather_cube/pallas_call | solution.py:825
  346.2 98.9 %scatter_cube.6 = (f32[128,2048]{1,0:T(8,128)S(1)}, bf16[128,4096]{1,0:T(8,128)(2,1)}, bf16[128,4096]{1,0:T(8,128)(2,1)}, bf16[128,4096]{1,0:T(8,128)(2,1)}) custom-call(bf16[2048,2048]{1,0:T(8,128)(2,1)} %get-tuple-element.65.refs_0_, bf16[2048,2048]{1,0:T(8,128)(2,1)} %get-tuple-element.66.refs_1_.refs_3_, ...), custom_call_target="tpu_custom_call" | custom-call | bytes 104857600 | tf_op jit(solution)/shard_map/scatter_cube/pallas_call | solution.py:825
  445.1 0.0 copy-start
  445.1 0.0 copy-start.2
  445.1 0.4 multiply_reduce_fusion
  445.5 1.5 multiply_convert_fusion
  447.1 0.0 copy-done
  447.1 0.0 copy-done.2
  447.1 70.8 %gather_cube.7 = (bf16[2048,128]{1,0:T(8,128)(2,1)S(1)}, bf16[128,2048]{1,0:T(8,128)(2,1)S(1)}, bf16[128,4096]{1,0:T(8,128)(2,1)}, bf16[128,4096]{1,0:T(8,128)(2,1)}) custom-call(bf16[128,2048]{1,0:T(8,128)(2,1)} %get-tuple-element.101.x_ref, bf16[128,2048]{1,0:T(8,128)(2,1)S(1)} %copy-done, bf16[2048,128]{1,0:T(8,128)(2,1)S(1)} %copy-done.2, ...), custom_call_target="tpu_custom_call" | custom-call | bytes 104857600 | tf_op jit(solution)/shard_map/gather_cube/pallas_call | solution.py:825
  517.9 0.0 copy-start.6
  517.9 0.8 copy-done.6
  518.7 8.4 %attend_back.1 = (f32[2048,128]{1,0:T(8,128)}, f32[2048,128]{1,0:T(8,128)}, bf16[2048,128]{1,0:T(8,128)(2,1)}, f32[32,128]{1,0:T(8,128)}, f32[8,128]{1,0:T(8,128)}) custom-call(bf16[2048,128]{1,0:T(8,128)(2,1)} %copy-done.6, bf16[2048,128]{1,0:T(8,128)(2,1)} %get-tuple-element.72.q_ref, bf16[2048,128]{1,0:T(8,128)(2,1)} %get-tuple-element.73.k_ref, ...), custom_call_target="tpu_custom_call" | custom-call | flops 134217728 | bytes 8388608 | tf_op jit(solution)/shard_map/attend_back/pallas_call | solution.py:1332
  527.1 0.7 slice_dynamic-update-slice_fusion
  527.9 9.2 %sum_cube.3.t_ref = f32[16,8,128]{2,1,0:T(8,128)} custom-call(f32[32,128]{1,0:T(8,128)} %get-tuple-element.78.v_ref), custom_call_target="tpu_custom_call" | custom-call | bytes 20971520 | tf_op jit(solution)/shard_map/sum_cube/pallas_call | solution.py:1159
  537.1 4.5 project_back.1.refs_0_.refs_3_
  541.6 96.4 %scatter_cube.7 = (f32[128,2048]{1,0:T(8,128)S(1)}, bf16[128,3072]{1,0:T(8,128)(2,1)}, bf16[128,3072]{1,0:T(8,128)(2,1)}, f32[8,128]{1,0:T(8,128)}, f32[8,128]{1...) custom-call(bf16[2048,384]{1,0:T(8,128)(2,1)} %project_back.1.refs_0, ...), custom_call_target="tpu_custom_call" | custom-call | bytes 104857600 | tf_op jit(solution)/shard_map/scatter_cube/pallas_call | solution.py:825
  638.0 0.7 add.58
  638.7 0.6 slice_bitcast_fusion.2
  639.3 0.0 copy-done.1
  639.3 1.2 copy-done.3
  640.5 0.0 slice-start
  640.5 2.3 whole_rows.3
  642.9 0.0 copy-done.12
  642.9 0.0 copy-done.13
  642.9 0.0 slice-start.1
  642.9 1.1 maximum_convert_fusion
  644.0 0.0 copy-done.4
  644.0 0.0 copy-done.5
  644.0 2.8 whole_rows.2
  646.8 1.2 fusion.7
  648.0 0.0 slice-done
  648.0 0.0 slice-done.1
  648.0 3.4 copy.21
  (20 shorter events, 0.2 us)
Async XLA Ops:
  63.6 0.6 copy-start.7
  73.4 26.3 %copy-start.10 = (bf16[128,2048]{1,0:T(8,128)(2,1)S(1)}, bf16[128,2048]{1,0:T(8,128)(2,1)}, u32[]{:S(2)}) copy-start(bf16[128,2048]{1,0:T(8,128)(2,1)} %refs_3_.1) | copy-start | bytes 1572868
  73.4 26.3 %copy-start.11 = (bf16[128,2048]{1,0:T(8,128)(2,1)S(1)}, bf16[128,2048]{1,0:T(8,128)(2,1)}, u32[]{:S(2)}) copy-start(bf16[128,2048]{1,0:T(8,128)(2,1)} %get-tuple-element.59) | copy-start | bytes 1572868
  99.7 92.9 %copy-start.9 = (bf16[128,2048]{1,0:T(8,128)(2,1)S(1)}, bf16[128,2048]{1,0:T(8,128)(2,1)}, u32[]{:S(2)}) copy-start(bf16[128,2048]{1,0:T(8,128)(2,1)} %x_ref.1) | copy-start | bytes 1572868
  261.3 39.3 %copy-start.8 = (bf16[128,2048]{1,0:T(8,128)(2,1)S(1)}, bf16[128,2048]{1,0:T(8,128)(2,1)}, u32[]{:S(2)}) copy-start(bf16[128,2048]{1,0:T(8,128)(2,1)} %param.15) | copy-start | bytes 1572868
  445.1 2.0 copy-start
  445.1 1.9 copy-start.2
  517.9 0.8 copy-start.6
  541.6 97.7 %copy-start.1 = (bf16[128,4096]{1,0:T(8,128)(2,1)S(1)}, bf16[128,4096]{1,0:T(8,128)(2,1)}, u32[]{:S(2)}) copy-start(bf16[128,4096]{1,0:T(8,128)(2,1)} %get-tuple-element.86.refs_9_.mine_ref) | copy-start | bytes 3145732
  639.3 1.2 copy-start.3
  640.5 2.3 copy-start.12
  640.5 2.3 copy-start.13
  640.5 3.5 copy-start.4
  640.5 3.5 copy-start.5
  640.5 7.4 %slice-start = ((s8[8388608]{0:T(1024)(128)(4,1)}), s8[4194304]{0:T(1024)(128)(4,1)S(1)}, s32[]{:S(2)}) async-start(s8[8388608]{0:T(1024)(128)(4,1)} %bitcast.19), calls=%async_computation | async-start | bytes 8388608
  642.9 5.1 slice-start.1

commit v8 on v7

--- a/solution.py
+++ b/solution.py
@@ -1494,6 +1494,8 @@
             Whole(up_sum, "x", near=3),
         ], z_first, BranchBack(out_rows, attended),
     )
+    half = down_sum.shape[0] // 2
+    down_first = lax.ppermute(down_sum[:half], "x", [(0, 1), (1, 0)])
     query_scaled, key_scaled, value_grad, dots, gain_head = by_blocks(
         attend_back_kernel, "attend_back",
         [
@@ -1530,7 +1532,7 @@
         owners_product(tokens_all, projected_bf, 3, swap=True, near=1, early=True),
         Owners(gain_terms, swap=True, fold=True, early=True),
         FinalRows((gate_sum, gate_other), (up_sum, up_other)),
-        Whole(down_sum, "x", near=1),
+        Whole(down_sum[half:], "x", near=1),
     ]
     if direct:
         loads.append(HeadSums(out_grad, near=1, early=True))
@@ -1546,6 +1548,7 @@
     else:
         grad_out = summed_head_rows(out_grad.astype(jnp.float32), owned)
     grad_qkv = whole_rows(qkv_sum, qkv_other, 3)
+    down_other = jnp.concatenate([down_first, down_other], axis=0)
     grad_down_t = whole_rows(down_sum, down_other, 1)
     grad_gains = (gain_sum + gain_other)[:4, :owned].T
     return (mixed, grad_tokens, grad_qkv, grad_out, grad_gate_up, grad_down_t, grad_gains)

time: 658 us -> 658 us (level)
  transfers between devices with their start and end apart: 0 -> 1, of which waited for: 0 -> 0; matrix products, arithmetic and copies ran while one was open for 0% -> 1% of each run, Pallas kernels for 0% -> 18%
where the time goes in v8:
time: 658 us; the launch traced here: 652 us
  Pallas kernels  626 us (95%)
  other arithmetic  12.4 us (2%)
  local copies, waits for them, and re-layouts  11.9 us (2%)
    pallas_call x8, Pallas kernels, call(): pl.pallas_call(functools.partial(body, cargo), out_shape=kept, in_specs=[...  564 us
    pallas_call x4, Pallas kernels, by_blocks(): pl.pallas_call(body, grid=(MEMBERS // TOGETHER,), out_shape=[pltpu.HBM(v....  37.1 us
    pallas_call x2, Pallas kernels, sum_cube(): pl.pallas_call(exchange_kernel, out_shape=jax.ShapeDtypeStruct((MEMBERS,...  19.4 us
  transfers between devices with their start and end apart: 1, of which 0 were waited for; matrix products, arithmetic and copies ran while one was open for 1% of the time, Pallas kernels for 18%

profile of v8, /device:TPU:0, one launch (start us, length us, event | category | flops | bytes accessed | tf_op | source)
XLA Modules:
  0.0 651.8 jit_solution(1098755942202771329)
XLA Ops:
  0.7 0.7 fusion.9
  1.3 0.1 copy.17
  1.4 0.2 reduce-window.8
  1.6 0.1 convert_reduce_fusion
  1.7 0.7 pad_convert_fusion.refs_0_
  2.4 61.2 %gather_cube.4 = (bf16[2048,2048]{1,0:T(8,128)(2,1)}, f32[16,8,128]{2,1,0:T(8,128)S(1)}, f32[16,8,128]{2,1,0:T(8,128)S(1)}, bf16[2048,384]{1,0:T(8,128)(2,1)}, bf16[128,2048]{1,0:T(8,128)(2,1)}) custom-call(bf16[128,2048]{1,0:T(8,128)(2,1)} %x_ref.1, f32[8,128]{1,0:T(8,128)S(1)} %pad_convert_fusion.refs_0_, f32[8,128]{1,0:T(8,128)S(1)} %broadcast_in_dim.9.refs_1_, ...), custom_call_target="tpu_custom_call" | custom-call | bytes 104857600 | tf_op jit(solution)/shard_map/gather_cube/pallas_call | solution.py:825
  63.6 0.0 copy-start.6
  63.6 0.6 copy-done.6
  64.3 0.0 copy-start.9
  64.3 0.0 copy-start.10
  64.3 8.6 %project.1 = (f32[2048,384]{1,0:T(8,128)}, f32[32,128]{1,0:T(8,128)}) custom-call(bf16[2048,2048]{1,0:T(8,128)(2,1)} %get-tuple-element.52.x_ref.refs_2_, bf16[2048,384]{1,0:T(8,128)(2,1)} %get-tuple-element.53.w_ref.refs_1_), custom_call_target="tpu_custom_call" | custom-call | flops 134217728 | bytes 8388608 | tf_op jit(solution)/shard_map/project/pallas_call | solution.py:1332
  72.9 9.7 %sum_cube.2.s_ref = f32[16,8,128]{2,1,0:T(8,128)} custom-call(f32[32,128]{1,0:T(8,128)} %get-tuple-element.55.v_ref), custom_call_target="tpu_custom_call" | custom-call | bytes 20971520 | tf_op jit(solution)/shard_map/sum_cube/pallas_call | solution.py:1159
  82.6 0.6 constant_dynamic-slice_fusion.g_ref
  83.2 0.3 multiply_cosine_fusion
  83.5 0.0 copy-done.9
  83.5 0.0 copy-done.10
  83.5 0.9 broadcast_select_fusion.refs_1_.refs_0_
  84.4 0.8 pad_maximum_fusion.1.t_ref
  85.2 15.5 %attend.1 = (bf16[2048,128]{1,0:T(8,128)(2,1)}, bf16[2048,128]{1,0:T(8,128)(2,1)}, bf16[2048,128]{1,0:T(8,128)(2,1)}, f32[2048,128]{1,0:T(8,128)}, f32[2048,128]...) custom-call(f32[2048,384]{1,0:T(8,128)} %get-tuple-element.54.p_ref, f32[16,8,128]{2,1,0:T(8,128)} %sum_cube.2.s_ref, ...), custom_call_target="tpu_custom_call" | custom-call | flops 134217728 | bytes 8388608 | tf_op jit(solution)/shard_map/attend/pallas_call | solution.py:1332
  100.7 91.9 %scatter_cube.4 = (f32[128,2048]{1,0:T(8,128)S(1)}, bf16[2048,1024]{1,0:T(8,128)(2,1)}) custom-call(bf16[2048,128]{1,0:T(8,128)(2,1)} %get-tuple-element.58.refs_0_.refs_1_, bf16[128,2048]{1,0:T(8,128)(2,1)} %broadcast_select_fusion.refs_1_.refs_0_, bf16[128,16384]{1,0:T(8,128)(2,1)} %refs_2_.3), custom_call_target="tpu_custom_call" | custom-call | bytes 104857600 | tf_op jit(solution)/shard_map/scatter_cube/pallas_call | solution.py:825
  192.6 0.2 multiply_reduce_fusion.3
  192.8 0.0 copy-done.8
  192.8 1.0 fusion.6.x_ref
  193.8 67.7 %gather_cube.5 = (bf16[2048,512]{1,0:T(8,128)(2,1)}, f32[2048,1024]{1,0:T(8,128)}, bf16[2048,2048]{1,0:T(8,128)(2,1)}, bf16[2048,512]{1,0:T(8,128)(2,1)}) custom-call(bf16[128,2048]{1,0:T(8,128)(2,1)} %fusion.6.x_ref, bf16[2048,1024]{1,0:T(8,128)(2,1)} %get-tuple-element.61.refs_0_.refs_1_, bf16[128,8192]{1,0:T(8,128)(2,1)} %refs_1_.1), custom_call_target="tpu_custom_call" | custom-call | bytes 104857600 | tf_op jit(solution)/shard_map/gather_cube/pallas_call | solution.py:825
  261.5 0.0 copy-start.7
  261.6 39.1 %scatter_cube.5 = f32[128,2048]{1,0:T(8,128)S(1)} custom-call(bf16[2048,512]{1,0:T(8,128)(2,1)} %get-tuple-element.62.refs_0_.refs_3_, bf16[2048,512]{1,0:T(8,128)(2,1)} %get-tuple-element.63.refs_1_.refs_0_), custom_call_target="tpu_custom_call" | custom-call | bytes 104857600 | tf_op jit(solution)/shard_map/scatter_cube/pallas_call | solution.py:825
  300.7 0.2 multiply_reduce_fusion.2
  300.8 0.0 copy-done.7
  300.8 0.4 fusion.5
  301.2 1.1 fusion.4.x_ref
  302.3 44.1 %gather_cube.6 = (bf16[2048,1024]{1,0:T(8,128)(2,1)}, bf16[2048,2048]{1,0:T(8,128)(2,1)}, bf16[2048,2048]{1,0:T(8,128)(2,1)}) custom-call(bf16[128,2048]{1,0:T(8,128)(2,1)} %fusion.4.x_ref, bf16[2048,512]{1,0:T(8,128)(2,1)} %get-tuple-element.63.refs_1_.refs_0_, bf16[2048,1024]{1,0:T(8,128)(2,1)} %get-tuple-element.61.refs_0_.refs_1_, ...), custom_call_target="tpu_custom_call" | custom-call | bytes 104857600 | tf_op jit(solution)/shard_map/gather_cube/pallas_call | solution.py:825
  346.4 99.0 %scatter_cube.6 = (f32[128,2048]{1,0:T(8,128)S(1)}, bf16[128,4096]{1,0:T(8,128)(2,1)}, bf16[128,4096]{1,0:T(8,128)(2,1)}, bf16[128,4096]{1,0:T(8,128)(2,1)}) custom-call(bf16[2048,2048]{1,0:T(8,128)(2,1)} %get-tuple-element.65.refs_0_, bf16[2048,2048]{1,0:T(8,128)(2,1)} %get-tuple-element.66.refs_1_.refs_3_, ...), custom_call_target="tpu_custom_call" | custom-call | bytes 104857600 | tf_op jit(solution)/shard_map/scatter_cube/pallas_call | solution.py:825
  445.4 0.0 copy-start
  445.4 0.0 copy-start.2
  445.4 0.4 multiply_reduce_fusion
  445.8 1.5 multiply_convert_fusion
  447.3 0.0 copy-done
  447.3 0.0 copy-done.2
  447.3 70.7 %gather_cube.7 = (bf16[2048,128]{1,0:T(8,128)(2,1)S(1)}, bf16[128,2048]{1,0:T(8,128)(2,1)S(1)}, bf16[128,4096]{1,0:T(8,128)(2,1)}, bf16[128,4096]{1,0:T(8,128)(2,1)}) custom-call(bf16[128,2048]{1,0:T(8,128)(2,1)} %get-tuple-element.101.x_ref, bf16[128,2048]{1,0:T(8,128)(2,1)S(1)} %copy-done, bf16[2048,128]{1,0:T(8,128)(2,1)S(1)} %copy-done.2, ...), custom_call_target="tpu_custom_call" | custom-call | bytes 104857600 | tf_op jit(solution)/shard_map/gather_cube/pallas_call | solution.py:825
  518.0 0.0 copy-start.5
  518.0 2.3 fusion.10
  520.3 0.1 collective-permute-start
  520.4 0.0 copy-done.5
  520.4 8.4 %attend_back.1 = (f32[2048,128]{1,0:T(8,128)}, f32[2048,128]{1,0:T(8,128)}, bf16[2048,128]{1,0:T(8,128)(2,1)}, f32[32,128]{1,0:T(8,128)}, f32[8,128]{1,0:T(8,128)}) custom-call(bf16[2048,128]{1,0:T(8,128)(2,1)} %copy-done.5, bf16[2048,128]{1,0:T(8,128)(2,1)} %get-tuple-element.72.q_ref, bf16[2048,128]{1,0:T(8,128)(2,1)} %get-tuple-element.73.k_ref, ...), custom_call_target="tpu_custom_call" | custom-call | flops 134217728 | bytes 8388608 | tf_op jit(solution)/shard_map/attend_back/pallas_call | solution.py:1332
  528.8 0.7 slice_dynamic-update-slice_fusion
  529.6 9.7 %sum_cube.3.t_ref = f32[16,8,128]{2,1,0:T(8,128)} custom-call(f32[32,128]{1,0:T(8,128)} %get-tuple-element.78.v_ref), custom_call_target="tpu_custom_call" | custom-call | bytes 20971520 | tf_op jit(solution)/shard_map/sum_cube/pallas_call | solution.py:1159
  539.3 4.5 project_back.1.refs_0_.refs_3_
  543.8 90.8 %scatter_cube.7 = (f32[128,2048]{1,0:T(8,128)S(1)}, bf16[128,3072]{1,0:T(8,128)(2,1)}, bf16[128,3072]{1,0:T(8,128)(2,1)}, f32[8,128]{1,0:T(8,128)}, f32[8,128]{1...) custom-call(bf16[2048,384]{1,0:T(8,128)(2,1)} %project_back.1.refs_0, ...), custom_call_target="tpu_custom_call" | custom-call | bytes 104857600 | tf_op jit(solution)/shard_map/scatter_cube/pallas_call | solution.py:825
  634.6 0.7 add.58
  635.3 0.6 slice_bitcast_fusion.2
  635.9 1.1 broadcast_select_fusion.2
  636.9 1.1 maximum_convert_fusion
  638.0 1.1 copy-done.3
  639.2 1.1 copy-done.4
  640.3 2.8 whole_rows.2
  643.1 1.2 fusion.7
  644.3 0.0 collective-permute-done
  644.3 0.0 copy-done.11
  644.3 0.1 pad_maximum_fusion.came_ref
  644.4 0.0 copy-done.1
  644.4 2.3 whole_rows.3
  646.7 0.0 slice-done
  646.7 1.3 slice-done.1
  648.0 3.4 copy.21
  (20 shorter events, 0.1 us)
Async XLA Ops:
  63.6 0.6 copy-start.6
  64.3 19.2 %copy-start.9 = (bf16[128,2048]{1,0:T(8,128)(2,1)S(1)}, bf16[128,2048]{1,0:T(8,128)(2,1)}, u32[]{:S(2)}) copy-start(bf16[128,2048]{1,0:T(8,128)(2,1)} %refs_3_.1) | copy-start | bytes 1572868
  64.3 19.2 %copy-start.10 = (bf16[128,2048]{1,0:T(8,128)(2,1)S(1)}, bf16[128,2048]{1,0:T(8,128)(2,1)}, u32[]{:S(2)}) copy-start(bf16[128,2048]{1,0:T(8,128)(2,1)} %get-tuple-element.59) | copy-start | bytes 1572868
  85.2 107.6 %copy-start.8 = (bf16[128,2048]{1,0:T(8,128)(2,1)S(1)}, bf16[128,2048]{1,0:T(8,128)(2,1)}, u32[]{:S(2)}) copy-start(bf16[128,2048]{1,0:T(8,128)(2,1)} %x_ref.1) | copy-start | bytes 1572868
  261.5 39.3 %copy-start.7 = (bf16[128,2048]{1,0:T(8,128)(2,1)S(1)}, bf16[128,2048]{1,0:T(8,128)(2,1)}, u32[]{:S(2)}) copy-start(bf16[128,2048]{1,0:T(8,128)(2,1)} %param.15) | copy-start | bytes 1572868
  445.4 1.9 copy-start
  445.4 1.9 copy-start.2
  518.0 2.4 copy-start.5
  520.3 123.9 %collective-permute-start = (bf16[64,4096]{1,0:T(8,128)(2,1)S(1)}, bf16[64,4096]{1,0:T(8,128)(2,1)S(1)}, u32[]{:S(2)}, u32[]{:S(2)}) collective-permute-start(bf16[64,4096]{1,0:T(8,128)(2,1)S(1)} %get-tuple-element.103), channel_id=1, source_target_pairs={{0,16},{16,0},{1,17},{17,1},{2,18},{18,2},{3,19},{19,3},{4,20},{20... | collective-permute-start | bytes 1572872 | tf_op jit(solution)/shard_map/ppermute | solution.py:1498
  638.0 1.1 copy-start.3
  639.2 1.1 copy-start.4
  640.3 4.0 copy-start.11
  640.3 4.1 copy-start.1
  640.3 6.4 slice-start
  644.3 3.7 slice-start.1
